TPU v7x, 32 devices: a whole 2x2x4 slice. The times are simulated.
32 devices in a mesh: seq: 8 (over y, x, core), group: 4 (over z).
Axes of the slice: x: 2, y: 2, z: 4, core: 2. Of those that a mesh axis runs over, the one named last changes fastest.
Arguments:
- hidden_in: bfloat16 [8, 2048, 1024], P('seq', 'group'), may hold values from -6 to 6
- doc_lengths: int32 [8, 8], P('seq'), may hold values from 1 to 1024, 2048 in all within a row
- ln_gain: bfloat16 [1024], P(('seq', 'group')), may hold values from 0.099609375 to 1.8984375
- ln_bias: bfloat16 [1024], P(('seq', 'group')), may hold values from -3 to 3
- w_qkv: bfloat16 [1024, 3072], P(('seq', 'group')), may hold values from -0.25 to 0.25
- b_qkv: bfloat16 [3072], P(('seq', 'group')), may hold values from -3 to 3
- w_dense: bfloat16 [1024, 1024], P(('seq', 'group')), may hold values from -0.75 to 0.75
- b_dense: bfloat16 [1024], P(('seq', 'group')), may hold values from -3 to 3
- w_in: bfloat16 [1024, 4096], P(('seq', 'group')), may hold values from -0.1875 to 0.1875
- b_in: bfloat16 [4096], P(('seq', 'group')), may hold values from -3 to 3
- w_out: bfloat16 [4096, 1024], P(('seq', 'group')), may hold values from -0.09375 to 0.09375
- b_out: bfloat16 [1024], P(('seq', 'group')), may hold values from -3 to 3
- out_grad: bfloat16 [8, 2048, 1024], P('seq', 'group'), may hold values from -6 to 6
Outputs:
- hidden_out: bfloat16 [8, 2048, 1024], P('seq', 'group')
- grad_in: float32 [8, 2048, 1024], P('seq', 'group')
- grad_ln_gain: float32 [1024], P(('seq', 'group'))
- grad_ln_bias: float32 [1024], P(('seq', 'group'))
- grad_w_qkv: float32 [1024, 3072], P(('seq', 'group'))
- grad_b_qkv: float32 [3072], P(('seq', 'group'))
- grad_w_dense: float32 [1024, 1024], P(('seq', 'group'))
- grad_b_dense: float32 [1024], P(('seq', 'group'))
- grad_w_in: float32 [1024, 4096], P(('seq', 'group'))
- grad_b_in: float32 [4096], P(('seq', 'group'))
- grad_w_out: float32 [4096, 1024], P(('seq', 'group'))
- grad_b_out: float32 [1024], P(('seq', 'group'))
Inputs may be any that keep to these rules, and one draw needn't show every extreme that they name: `doc_lengths`: each row lists the lengths of the 8 documents of one sequence in order; a row sums to 2048 and its longest document has exactly 1024 tokens.
All inputs are finite; a program needn't handle non-finite values.
Results may differ from a plain program's by a relative error of at most 0.017.
Values may be sent and summed in bfloat16 or wider, within the bound.
No kernel may reach another device: no remote copies, remote signals or barrier semaphores. Data moves between devices by JAX's collectives and lax.ppermute only.
A program may use at most 256 MiB of HBM per device.

v0:
```python
import math

import jax
import jax.numpy as jnp
from jax import lax
from jax.sharding import PartitionSpec as P

HEADS = 16
HEAD_DIM = 64
ROT_DIM = 16


def dot_rows(left, right):
    return lax.dot_general(
        left, right, (((0,), (0,)), ((), ())), preferred_element_type=jnp.float32
    )


def dot_last(left, right):
    return lax.dot_general(
        left, right, (((1,), (1,)), ((), ())), preferred_element_type=jnp.float32
    )


def rope_tables(token_positions, rot_dim):
    half_rot = rot_dim // 2
    frequency = jnp.exp(
        -math.log(10000.0) * 2.0 * jnp.arange(half_rot, dtype=jnp.float32) / rot_dim
    )
    angles = token_positions.astype(jnp.float32)[:, None] * frequency[None, :]
    return (jnp.cos(angles)[:, None, :], jnp.sin(angles)[:, None, :])


def rotate(heads, cosine, sine, rot_dim):
    half_rot = rot_dim // 2
    first_half = heads[:, :, :half_rot]
    second_half = heads[:, :, half_rot:rot_dim]
    remainder = heads[:, :, rot_dim:]
    return jnp.concatenate(
        [
            first_half * cosine - second_half * sine,
            second_half * cosine + first_half * sine,
            remainder,
        ],
        axis=2,
    )


def gelu_exact(preact):
    return jax.nn.gelu(preact, approximate=False)


def block_scores(query_block, key_tile_block, seg_query, seg_key, pos_query, pos_key, score_scale):
    scaled = (
        jnp.einsum("qhd,khd->hqk", query_block, key_tile_block, preferred_element_type=jnp.float32)
        * score_scale
    )
    allowed = (seg_query[:, None] == seg_key[None, :]) & (pos_key[None, :] <= pos_query[:, None])
    return jnp.where(allowed[None], scaled, -1e30)


def owning_block(source, block_index, block_of_rows):
    return lax.dynamic_slice_in_dim(source, block_index * block_of_rows, block_of_rows, 0)


def add_block(source, block_index, block_of_rows, addend):
    current = owning_block(source, block_index, block_of_rows)
    return lax.dynamic_update_slice_in_dim(source, current + addend, block_index * block_of_rows, 0)


def attention_forward(
    query_heads,
    key_head_rows,
    value_head_rows,
    document_segment,
    token_positions,
    seg_start,
    block_of_rows,
):
    seq_len, head_count, head_dim = query_heads.shape
    score_scale = 1.0 / math.sqrt(head_dim)

    def query_step(qindex, state_now):
        outputs, log_sums = state_now
        query_block = owning_block(query_heads, qindex, block_of_rows)
        seg_query = owning_block(document_segment, qindex, block_of_rows)
        pos_query = owning_block(token_positions, qindex, block_of_rows)
        key_lower = seg_start[qindex * block_of_rows] // block_of_rows

        def scores_for_block(key_position_index):
            return block_scores(
                query_block,
                owning_block(key_head_rows, key_position_index, block_of_rows),
                seg_query,
                owning_block(document_segment, key_position_index, block_of_rows),
                pos_query,
                owning_block(token_positions, key_position_index, block_of_rows),
                score_scale,
            )

        def statistics_step(key_position_index, row_statistics):
            run_max, run_sum = row_statistics
            logit_scores = scores_for_block(key_position_index)
            new_max = jnp.maximum(run_max, jnp.max(logit_scores, axis=2))
            run_sum = run_sum * jnp.exp(run_max - new_max) + jnp.sum(
                jnp.exp(logit_scores - new_max[:, :, None]), axis=2
            )
            return (new_max, run_sum)

        start_stats = (
            jnp.full((head_count, block_of_rows), -1e30, jnp.float32),
            jnp.zeros((head_count, block_of_rows), jnp.float32),
        )
        run_max, run_sum = lax.fori_loop(key_lower, qindex + 1, statistics_step, start_stats)
        log_exp_total = run_max + jnp.log(run_sum)

        def value_loop_step(key_position_index, partial_output):
            attention_weights = jnp.exp(
                scores_for_block(key_position_index) - log_exp_total[:, :, None]
            ).astype(jnp.bfloat16)
            return partial_output + jnp.einsum(
                "hqk,khd->qhd",
                attention_weights,
                owning_block(value_head_rows, key_position_index, block_of_rows),
                preferred_element_type=jnp.float32,
            )

        block_out = lax.fori_loop(
            key_lower,
            qindex + 1,
            value_loop_step,
            jnp.zeros((block_of_rows, head_count, head_dim), jnp.float32),
        )
        outputs = lax.dynamic_update_slice_in_dim(outputs, block_out, qindex * block_of_rows, 0)
        log_sums = lax.dynamic_update_slice_in_dim(
            log_sums, log_exp_total, qindex * block_of_rows, 1
        )
        return (outputs, log_sums)

    start_state = (
        jnp.zeros((seq_len, head_count, head_dim), jnp.float32),
        jnp.zeros((head_count, seq_len), jnp.float32),
    )
    return lax.fori_loop(0, seq_len // block_of_rows, query_step, start_state)


def attention_backward(
    query_heads,
    key_head_rows,
    value_head_rows,
    grad_heads,
    outputs,
    log_sums,
    document_segment,
    token_positions,
    seg_start,
    block_of_rows,
):
    seq_len, head_count, head_dim = query_heads.shape
    score_scale = 1.0 / math.sqrt(head_dim)
    delta_all = jnp.sum(grad_heads.astype(jnp.float32) * outputs, axis=2).T

    def query_step(qindex, state_now):
        grad_query_all, grad_key_all, grad_value_all = state_now
        query_block = owning_block(query_heads, qindex, block_of_rows)
        grad_block = owning_block(grad_heads, qindex, block_of_rows)
        seg_query = owning_block(document_segment, qindex, block_of_rows)
        pos_query = owning_block(token_positions, qindex, block_of_rows)
        log_exp_total = lax.dynamic_slice_in_dim(log_sums, qindex * block_of_rows, block_of_rows, 1)
        delta_block = lax.dynamic_slice_in_dim(delta_all, qindex * block_of_rows, block_of_rows, 1)
        key_lower = seg_start[qindex * block_of_rows] // block_of_rows

        def key_loop_step(key_position_index, loop_state_inner):
            grad_query, grad_keys, grad_values = loop_state_inner
            key_tile_block = owning_block(key_head_rows, key_position_index, block_of_rows)
            value_tile_block = owning_block(value_head_rows, key_position_index, block_of_rows)
            logit_scores = block_scores(
                query_block,
                key_tile_block,
                seg_query,
                owning_block(document_segment, key_position_index, block_of_rows),
                pos_query,
                owning_block(token_positions, key_position_index, block_of_rows),
                score_scale,
            )
            probability = jnp.exp(logit_scores - log_exp_total[:, :, None])
            grad_values = add_block(
                grad_values,
                key_position_index,
                block_of_rows,
                jnp.einsum(
                    "hqk,qhd->khd",
                    probability.astype(jnp.bfloat16),
                    grad_block,
                    preferred_element_type=jnp.float32,
                ),
            )
            grad_probs = jnp.einsum(
                "qhd,khd->hqk", grad_block, value_tile_block, preferred_element_type=jnp.float32
            )
            grad_scores = (probability * (grad_probs - delta_block[:, :, None])).astype(
                jnp.bfloat16
            )
            grad_query = (
                grad_query
                + jnp.einsum(
                    "hqk,khd->qhd", grad_scores, key_tile_block, preferred_element_type=jnp.float32
                )
                * score_scale
            )
            grad_keys = add_block(
                grad_keys,
                key_position_index,
                block_of_rows,
                jnp.einsum(
                    "hqk,qhd->khd", grad_scores, query_block, preferred_element_type=jnp.float32
                )
                * score_scale,
            )
            return (grad_query, grad_keys, grad_values)

        start_inner = (
            jnp.zeros((block_of_rows, head_count, head_dim), jnp.float32),
            grad_key_all,
            grad_value_all,
        )
        grad_query, grad_key_all, grad_value_all = lax.fori_loop(
            key_lower, qindex + 1, key_loop_step, start_inner
        )
        grad_query_all = lax.dynamic_update_slice_in_dim(
            grad_query_all, grad_query, qindex * block_of_rows, 0
        )
        return (grad_query_all, grad_key_all, grad_value_all)

    zero_heads = jnp.zeros((seq_len, head_count, head_dim), jnp.float32)
    return lax.fori_loop(
        0, seq_len // block_of_rows, query_step, (zero_heads, zero_heads, zero_heads)
    )


def local(
    hidden_in,
    doc_lengths,
    ln_gain,
    ln_bias,
    w_qkv,
    b_qkv,
    w_dense,
    b_dense,
    w_in,
    b_in,
    w_out,
    b_out,
    out_grad,
):
    (
        full_gain,
        full_bias,
        full_qkv,
        full_qkv_bias,
        full_dense,
        full_dense_bias,
        full_in,
        full_in_bias,
        full_out,
        full_out_bias,
    ) = (
        lax.all_gather(ln_gain, ("seq", "group"), axis=0, tiled=True),
        lax.all_gather(ln_bias, ("seq", "group"), axis=0, tiled=True),
        lax.all_gather(w_qkv, ("seq", "group"), axis=0, tiled=True),
        lax.all_gather(b_qkv, ("seq", "group"), axis=0, tiled=True),
        lax.all_gather(w_dense, ("seq", "group"), axis=0, tiled=True),
        lax.all_gather(b_dense, ("seq", "group"), axis=0, tiled=True),
        lax.all_gather(w_in, ("seq", "group"), axis=0, tiled=True),
        lax.all_gather(b_in, ("seq", "group"), axis=0, tiled=True),
        lax.all_gather(w_out, ("seq", "group"), axis=0, tiled=True),
        lax.all_gather(b_out, ("seq", "group"), axis=0, tiled=True),
    )
    tokens = hidden_in[0].astype(jnp.float32)
    tok_count = tokens.shape[0]
    width = tokens.shape[1]
    row_mean = jnp.mean(tokens, axis=1, keepdims=True)
    centered = tokens - row_mean
    variance = jnp.mean(centered * centered, axis=1, keepdims=True)
    inv_std = lax.rsqrt(variance + 1e-05)
    normal_rows = centered * inv_std
    normed = (normal_rows * full_gain.astype(jnp.float32) + full_bias.astype(jnp.float32)).astype(
        jnp.bfloat16
    )
    mixed = jnp.dot(normed, full_qkv, preferred_element_type=jnp.float32) + full_qkv_bias.astype(
        jnp.float32
    )
    token_positions = lax.axis_index("group") * tok_count + jnp.arange(tok_count, dtype=jnp.int32)
    cosine, sine = rope_tables(token_positions, ROT_DIM)
    head_shape = (tok_count, HEADS, HEAD_DIM)
    queries = (
        rotate(mixed[:, :width].reshape(head_shape), cosine, sine, ROT_DIM)
        .reshape(tok_count, width)
        .astype(jnp.bfloat16)
    )
    key_rows = (
        rotate(mixed[:, width : 2 * width].reshape(head_shape), cosine, sine, ROT_DIM)
        .reshape(tok_count, width)
        .astype(jnp.bfloat16)
    )
    value_rows = mixed[:, 2 * width :].astype(jnp.bfloat16)
    query_cols, key_cols, value_cols = (
        lax.all_to_all(queries, "group", split_axis=1, concat_axis=0, tiled=True),
        lax.all_to_all(key_rows, "group", split_axis=1, concat_axis=0, tiled=True),
        lax.all_to_all(value_rows, "group", split_axis=1, concat_axis=0, tiled=True),
    )
    seq_len = query_cols.shape[0]
    head_count = query_cols.shape[1] // HEAD_DIM
    heads_shape = (seq_len, head_count, HEAD_DIM)
    query_heads = query_cols.reshape(heads_shape)
    key_head_rows = key_cols.reshape(heads_shape)
    value_head_rows = value_cols.reshape(heads_shape)
    all_pos = jnp.arange(seq_len, dtype=jnp.int32)
    doc_lens = doc_lengths[0]
    doc_ends = jnp.cumsum(doc_lens)
    document_segment = jnp.sum((all_pos[:, None] >= doc_ends[None, :]).astype(jnp.int32), axis=1)
    doc_starts = doc_ends - doc_lens
    doc_index = jnp.arange(doc_ends.shape[0], dtype=jnp.int32)
    seg_start = jnp.sum(
        jnp.where(document_segment[:, None] == doc_index[None, :], doc_starts[None, :], 0), axis=1
    )
    block_of_rows = min(512, seq_len)
    outputs, log_sums = attention_forward(
        query_heads,
        key_head_rows,
        value_head_rows,
        document_segment,
        all_pos,
        seg_start,
        block_of_rows,
    )
    attended = lax.all_to_all(
        outputs.reshape(seq_len, head_count * HEAD_DIM).astype(jnp.bfloat16),
        "group",
        split_axis=0,
        concat_axis=1,
        tiled=True,
    )
    branch_attn = jnp.dot(
        attended, full_dense, preferred_element_type=jnp.float32
    ) + full_dense_bias.astype(jnp.float32)
    pre_act = jnp.dot(normed, full_in, preferred_element_type=jnp.float32) + full_in_bias.astype(
        jnp.float32
    )
    activated = gelu_exact(pre_act).astype(jnp.bfloat16)
    branch_mlp = jnp.dot(
        activated, full_out, preferred_element_type=jnp.float32
    ) + full_out_bias.astype(jnp.float32)
    hidden_out = (tokens + branch_attn + branch_mlp).astype(jnp.bfloat16)
    full_gain, full_qkv, full_dense, full_in, full_out = (
        lax.all_gather(ln_gain, ("seq", "group"), axis=0, tiled=True),
        lax.all_gather(w_qkv, ("seq", "group"), axis=0, tiled=True),
        lax.all_gather(w_dense, ("seq", "group"), axis=0, tiled=True),
        lax.all_gather(w_in, ("seq", "group"), axis=0, tiled=True),
        lax.all_gather(w_out, ("seq", "group"), axis=0, tiled=True),
    )
    grad_rows = out_grad[0]
    grad_float = grad_rows.astype(jnp.float32)
    bias_grad = jnp.sum(grad_float, axis=0)
    grad_dense = dot_rows(attended, grad_rows)
    grad_out_w = dot_rows(activated, grad_rows)
    grad_act = dot_last(grad_rows, full_out)
    grad_pre = jax.vjp(gelu_exact, pre_act)[1](grad_act)[0].astype(jnp.bfloat16)
    grad_in_w = dot_rows(normed, grad_pre)
    grad_in_bias = jnp.sum(grad_pre.astype(jnp.float32), axis=0)
    grad_normed = dot_last(grad_pre, full_in)
    grad_attended = dot_last(grad_rows, full_dense).astype(jnp.bfloat16)
    grad_cols = lax.all_to_all(grad_attended, "group", split_axis=1, concat_axis=0, tiled=True)
    grad_query_all, grad_key_all, grad_value_all = attention_backward(
        query_heads,
        key_head_rows,
        value_head_rows,
        grad_cols.reshape(heads_shape),
        outputs,
        log_sums,
        document_segment,
        all_pos,
        seg_start,
        block_of_rows,
    )
    flat_shape = (seq_len, head_count * HEAD_DIM)
    grad_query_tok, grad_key_tok, grad_value_tok = (
        lax.all_to_all(
            grad_query_all.reshape(flat_shape).astype(jnp.bfloat16),
            "group",
            split_axis=0,
            concat_axis=1,
            tiled=True,
        ),
        lax.all_to_all(
            grad_key_all.reshape(flat_shape).astype(jnp.bfloat16),
            "group",
            split_axis=0,
            concat_axis=1,
            tiled=True,
        ),
        lax.all_to_all(
            grad_value_all.reshape(flat_shape).astype(jnp.bfloat16),
            "group",
            split_axis=0,
            concat_axis=1,
            tiled=True,
        ),
    )
    unrot_query = (
        rotate(grad_query_tok.astype(jnp.float32).reshape(head_shape), cosine, -sine, ROT_DIM)
        .reshape(tok_count, width)
        .astype(jnp.bfloat16)
    )
    unrot_key = (
        rotate(grad_key_tok.astype(jnp.float32).reshape(head_shape), cosine, -sine, ROT_DIM)
        .reshape(tok_count, width)
        .astype(jnp.bfloat16)
    )
    grad_mixed = jnp.concatenate([unrot_query, unrot_key, grad_value_tok], axis=1)
    grad_qkv_w = dot_rows(normed, grad_mixed)
    grad_qkv_bias = jnp.sum(grad_mixed.astype(jnp.float32), axis=0)
    grad_normed = grad_normed + dot_last(grad_mixed, full_qkv)
    scaled_grad = grad_normed * full_gain.astype(jnp.float32)
    grad_gain = jnp.sum(grad_normed * normal_rows, axis=0)
    grad_bias = jnp.sum(grad_normed, axis=0)
    grad_input = grad_float + inv_std * (
        scaled_grad
        - jnp.mean(scaled_grad, axis=1, keepdims=True)
        - normal_rows * jnp.mean(scaled_grad * normal_rows, axis=1, keepdims=True)
    )
    sharded = tuple(
        (
            lax.psum_scatter(grad_gain, ("seq", "group"), scatter_dimension=0, tiled=True),
            lax.psum_scatter(grad_bias, ("seq", "group"), scatter_dimension=0, tiled=True),
            lax.psum_scatter(grad_qkv_w, ("seq", "group"), scatter_dimension=0, tiled=True),
            lax.psum_scatter(grad_qkv_bias, ("seq", "group"), scatter_dimension=0, tiled=True),
            lax.psum_scatter(grad_dense, ("seq", "group"), scatter_dimension=0, tiled=True),
            lax.psum_scatter(bias_grad, ("seq", "group"), scatter_dimension=0, tiled=True),
            lax.psum_scatter(grad_in_w, ("seq", "group"), scatter_dimension=0, tiled=True),
            lax.psum_scatter(grad_in_bias, ("seq", "group"), scatter_dimension=0, tiled=True),
            lax.psum_scatter(grad_out_w, ("seq", "group"), scatter_dimension=0, tiled=True),
            lax.psum_scatter(bias_grad, ("seq", "group"), scatter_dimension=0, tiled=True),
        )
    )
    return (hidden_out[None], grad_input[None]) + sharded


def solution(mesh):
    in_specs = (
        P("seq", "group", None),
        P("seq", None),
        P(("seq", "group")),
        P(("seq", "group")),
        P(("seq", "group"), None),
        P(("seq", "group")),
        P(("seq", "group"), None),
        P(("seq", "group")),
        P(("seq", "group"), None),
        P(("seq", "group")),
        P(("seq", "group"), None),
        P(("seq", "group")),
        P("seq", "group", None),
    )
    out_specs = (
        P("seq", "group", None),
        P("seq", "group", None),
        P(("seq", "group")),
        P(("seq", "group")),
        P(("seq", "group"), None),
        P(("seq", "group")),
        P(("seq", "group"), None),
        P(("seq", "group")),
        P(("seq", "group"), None),
        P(("seq", "group")),
        P(("seq", "group"), None),
        P(("seq", "group")),
    )
    return jax.shard_map(local, mesh=mesh, in_specs=in_specs, out_specs=out_specs, check_vma=False)
```

profile of v0, /device:TPU:0, one launch (start us, length us, event | category | flops | bytes accessed | tf_op | source)
XLA Modules:
  0.0 1520.5 jit_solution(18357287741556988148)
XLA Ops:
  13.6 42.4 %all-reduce.11 = (bf16[1024]{0:T(1024)(128)(2,1)S(1)}, bf16[1024]{0:T(1024)(128)(2,1)S(1)}, bf16[3072]{0:T(1024)(128)(2,1)S(1)}, bf16[1024]{0:T(1024)(128)(2,1)}, bf16[1024]{0:T(1024)(128)(2,1)}) all-reduce(bf16[1024]{0:T(1024)(128)(2,1)S(1)} %dynamic-update-slice.1, ...), channel_id=1, replica_groups=mesh['seq'=8,'group'=4] {'seq','group'}, use_global_device_ids=true, to_apply=%add.1 | all-reduce | flops 7168 | bytes 28672
  60.0 10.3 all-gather.8.cloned.1.call-done
  78.1 75.1 %all-gather.6.cloned.1.call-done = bf16[1024,3072]{1,0:T(8,128)(2,1)} async-done(((bf16[32,3072]{1,0:T(8,128)(2,1)}), bf16[1024,3072]{1,0:T(8,128)(2,1)}) %all-gather.6.cloned.1.call-update) | async-done | bytes 6291472 | tf_op jit(solution)/shard_map/all_gather | solution.py:270
  173.8 40.2 %all_to_all.110 = bf16[512,4,256]{0,2,1:T(8,128)(2,1)S(1)} all-to-all(bf16[512,4,256]{0,2,1:T(8,128)(2,1)S(1)} %bitcast.272), channel_id=1, replica_groups=mesh['seq'=8,'group'=4] {'group'}, dimensions={1} | all-to-all | bytes 2097152 | tf_op jit(solution)/shard_map/all_to_all | solution.py:308
  220.5 41.7 %all-to-all-done.1 = bf16[512,4,256]{0,2,1:T(8,128)(2,1)S(1)} async-done(((bf16[512,4,256]{0,2,1:T(8,128)(2,1)}), bf16[512,4,256]{0,2,1:T(8,128)(2,1)S(1)}, u32[]{:S(2)}, u32[]{:S(2)}) %all-to-all-start.1) | async-done | bytes 1048608 | tf_op jit(solution)/shard_map/all_to_all | solution.py:309
  275.0 23.1 %all-to-all-done.2 = bf16[512,4,256]{2,0,1:T(8,128)(2,1)} async-done(((bf16[512,4,256]{2,0,1:T(8,128)(2,1)}), bf16[512,4,256]{2,0,1:T(8,128)(2,1)}, u32[]{:S(2)}, u32[]{:S(2)}) %all-to-all-start.2) | async-done | bytes 1048608 | tf_op jit(solution)/shard_map/all_to_all | solution.py:310
  303.1 61.1 %while.153 = (s32[]{:T(128)}, f32[2048,4,64]{0,2,1:T(8,128)}, f32[4,2048]{1,0:T(4,128)S(1)}, s32[2048]{0:T(1024)S(1)}, bf16[2048,4,64]{0,2,1:T(8,128)(2,1)S(1)},...) while((s32[]{:T(128)}, f32[2048,4,64]{0,2,1:T(8,128)}, ...), condition=%wide.region_12.13_spmd.clone, body=%wide.region_5.12_spmd.clone.sunk | while | flops 415897600 | bytes 14362695 | solution.py:144
  376.1 23.6 %all-to-all-done.3 = bf16[4,512,256]{1,2,0:T(8,128)(2,1)S(1)} async-done(((bf16[4,512,256]{1,2,0:T(8,128)(2,1)}), bf16[4,512,256]{1,2,0:T(8,128)(2,1)S(1)}, u32[]{:S(2)}, u32[]{:S(2)}) %all-to-all-start.3) | async-done | bytes 1048608 | tf_op jit(solution)/shard_map/all_to_all | solution.py:337
  407.8 100.7 %while.155 = (s32[]{:T(128)}, bf16[2048,4,64]{0,2,1:T(8,128)(2,1)}, f32[2048,4,64]{0,2,1:T(8,128)}, f32[2048,4,64]{0,2,1:T(8,128)}, s32[2048]{0:T(1024)S(1)}, /*...) while((s32[]{:T(128)}, bf16[2048,4,64]{0,2,1:T(8,128)(2,1)}, ...), condition=%wide.region_17.18_spmd.clone, body=%wide.region_14.17_spmd.clone.sunk | while | flops 683016192 | bytes 27345748 | solution.py:236
  412.2 10.0 while.158
  427.4 19.9 %while.158 = (s32[]{:T(128)}, f32[512,4,64]{0,2,1:T(8,128)S(1)}, f32[2048,4,64]{0,2,1:T(8,128)}, f32[2048,4,64]{0,2,1:T(8,128)}, s32[]{:T(128)}, /*index=5*/bf16...) while((s32[]{:T(128)}, f32[512,4,64]{0,2,1:T(8,128)S(1)}, ...), condition=%wide.region_16.16_spmd, body=%wide.region_15.15_spmd.sunk | while | flops 683016192 | bytes 24682744 | solution.py:227
  452.5 20.0 %while.158 = (s32[]{:T(128)}, f32[512,4,64]{0,2,1:T(8,128)S(1)}, f32[2048,4,64]{0,2,1:T(8,128)}, f32[2048,4,64]{0,2,1:T(8,128)}, s32[]{:T(128)}, /*index=5*/bf16...) while((s32[]{:T(128)}, f32[512,4,64]{0,2,1:T(8,128)S(1)}, ...), condition=%wide.region_16.16_spmd, body=%wide.region_15.15_spmd.sunk | while | flops 683016192 | bytes 24682744 | solution.py:227
  477.7 30.0 %while.158 = (s32[]{:T(128)}, f32[512,4,64]{0,2,1:T(8,128)S(1)}, f32[2048,4,64]{0,2,1:T(8,128)}, f32[2048,4,64]{0,2,1:T(8,128)}, s32[]{:T(128)}, /*index=5*/bf16...) while((s32[]{:T(128)}, f32[512,4,64]{0,2,1:T(8,128)S(1)}, ...), condition=%wide.region_16.16_spmd, body=%wide.region_15.15_spmd.sunk | while | flops 683016192 | bytes 24682744 | solution.py:227
  517.8 37.5 %all-to-all-done.6 = bf16[4,512,256]{1,2,0:T(8,128)(2,1)S(1)} async-done(((bf16[4,512,256]{1,2,0:T(8,128)(2,1)}), bf16[4,512,256]{1,2,0:T(8,128)(2,1)S(1)}, u32[]{:S(2)}, u32[]{:S(2)}) %all-to-all-start.6) | async-done | bytes 1048608 | tf_op jit(solution)/shard_map/all_to_all | solution.py:395
  565.3 18.9 %all-to-all-done.5 = bf16[4,512,256]{1,2,0:T(8,128)(2,1)S(1)} async-done(((bf16[4,512,256]{1,2,0:T(8,128)(2,1)}), bf16[4,512,256]{1,2,0:T(8,128)(2,1)S(1)}, u32[]{:S(2)}, u32[]{:S(2)}) %all-to-all-start.5) | async-done | bytes 1048608 | tf_op jit(solution)/shard_map/all_to_all | solution.py:388
  589.9 23.0 %all-to-all-done.7 = bf16[4,512,256]{1,2,0:T(8,128)(2,1)S(1)} async-done(((bf16[4,512,256]{1,2,0:T(8,128)(2,1)}), bf16[4,512,256]{1,2,0:T(8,128)(2,1)S(1)}, u32[]{:S(2)}, u32[]{:S(2)}) %all-to-all-start.7) | async-done | bytes 1048608 | tf_op jit(solution)/shard_map/all_to_all | solution.py:402
  612.9 9.5 fusion.83
  623.1 67.5 %all-gather = bf16[32,1,128]{2,1,0:T(2,128)(2,1)S(1)} all-gather(bf16[1,1,128]{2,1,0:T(2,128)(2,1)S(1)} %bitcast.279), channel_id=1, replica_groups=mesh['seq'=8,'group'=4] {'seq','group'}, dimensions={0}, use_global_device_ids=true | all-gather | bytes 8448 | tf_op jit(solution)/shard_map/all_gather | solution.py:275
  690.6 27.7 %multiply_convert_fusion = (bf16[512,4096]{1,0:T(8,128)(2,1)}, f32[512,4096]{1,0:T(8,128)}, f32[512,4096]{1,0:T(8,128)}) fusion(f32[4096]{0:T(1024)S(1)} %bitcast.277, bf16[1024,4096]{1,0:T(8,128)(2,1)} %all-gather.10.cloned.1.call-done, bf16[1,512,1024]{2,1,0:T(8,128)(2,1)S(1)} %copy-done.1, f32[1024]{0:T(1024)S(1)} %copy-done.18, ...), kind=kOutput, calls=%fused_computation.62 | convolution fusion | flops 4436525056 | bytes 30437376 | tf_op jit(solution)/shard_map/dot_general | solution.py:347
  718.4 13.6 convert_reduce_fusion
  742.8 12.9 fusion.72
  776.2 40.5 %all-reduce.10 = (f32[1024]{0:T(1024)S(1)}, f32[1024]{0:T(1024)S(1)}, f32[3072]{0:T(1024)S(1)}, f32[1024]{0:T(1024)S(1)}, f32[4096]{0:T(1024)S(1)}) all-reduce(f32[1024]{0:T(1024)S(1)} %get-tuple-element.880, f32[1024]{0:T(1024)S(1)} %get-tuple-element.883, ...), channel_id=2, replica_groups=mesh['seq'=8,'group'=4] {'seq','group'}, use_global_device_ids=true, to_apply=%region_21.22.clone | all-reduce | flops 10240 | bytes 81920
  829.9 317.3 %reduce-scatter.9.cloned.1.call-done = f32[32,4096]{1,0:T(8,128)} async-done(((f32[1024,4096]{1,0:T(8,128)}), f32[32,4096]{1,0:T(8,128)}) %reduce-scatter.9.cloned.1.call-update) | async-done | bytes 524304 | tf_op jit(solution)/shard_map/reduce_scatter | solution.py:440
  1147.2 365.8 %reduce-scatter.11.cloned.1.call-done = f32[128,1024]{1,0:T(8,128)} async-done(((f32[4096,1024]{1,0:T(8,128)}), f32[128,1024]{1,0:T(8,128)}) %reduce-scatter.11.cloned.1.call-update) | async-done | bytes 524304 | tf_op jit(solution)/shard_map/reduce_scatter | solution.py:442
  (400 shorter events, 336.4 us)
Async XLA Ops:
  7.2 63.1 %all-gather.8.cloned.1.call-start = ((), (), s32[]{:S(2)}) async-start(), calls=%async_computation.13 | async-start | bytes 2162688 | tf_op jit(solution)/shard_map/all_gather | solution.py:272
  7.9 145.3 %all-gather.6.cloned.1.call-start = ((), (), s32[]{:S(2)}) async-start(), calls=%async_computation.12 | async-start | bytes 6488064 | tf_op jit(solution)/shard_map/all_gather | solution.py:270
  8.7 682.0 %all-gather.10.cloned.1.call-start = ((), (), s32[]{:S(2)}) async-start(), calls=%async_computation.14 | async-start | bytes 8650752 | tf_op jit(solution)/shard_map/all_gather | solution.py:274
  56.0 97.2 %copy-start.13 = (f32[1024]{0:T(1024)}, f32[1024]{0:T(1024)S(1)}, u32[]{:S(2)}) copy-start(f32[1024]{0:T(1024)S(1)} %convert_element_type.141) | copy-start | bytes 12292
  56.0 97.2 %copy-start.17 = (f32[1024]{0:T(1024)}, f32[1024]{0:T(1024)S(1)}, u32[]{:S(2)}) copy-start(f32[1024]{0:T(1024)S(1)} %convert_element_type.142) | copy-start | bytes 12292
  57.5 95.7 %copy-start.11 = (f32[512]{0:T(512)}, f32[512]{0:T(512)S(1)}, u32[]{:S(2)}) copy-start(f32[512]{0:T(512)S(1)} %broadcast_multiply_fusion.2) | copy-start | bytes 6148
  59.2 94.0 %copy-start.15 = (f32[512]{0:T(512)}, f32[512]{0:T(512)S(1)}, u32[]{:S(2)}) copy-start(f32[512]{0:T(512)S(1)} %add_rsqrt_fusion) | copy-start | bytes 6148
  60.0 111.3 %copy-start.8 = (f32[512,8]{0,1:T(8,128)}, f32[512,8]{0,1:T(8,128)S(1)}, u32[]{:S(2)}) copy-start(f32[512,8]{0,1:T(8,128)S(1)} %get-tuple-element.1040) | copy-start | bytes 49156
  73.5 79.7 %copy-start = (bf16[1,512,1024]{2,1,0:T(8,128)(2,1)S(1)}, bf16[1,512,1024]{2,1,0:T(8,128)(2,1)}, u32[]{:S(2)}) copy-start(bf16[1,512,1024]{2,1,0:T(8,128)(2,1)} %param.23) | copy-start | bytes 3145732
  74.5 99.2 %all-to-all-start.4 = ((bf16[512,4,256]{2,0,1:T(8,128)(2,1)}), bf16[512,4,256]{2,0,1:T(8,128)(2,1)S(1)}, u32[]{:S(2)}, u32[]{:S(2)}) async-start(bf16[512,4,256]{2,0,1:T(8,128)(2,1)} %bitcast.207), calls=%async_computation.4 | async-start | bytes 2097152 | tf_op jit(solution)/shard_map/all_to_all | solution.py:373
  214.0 53.0 %copy-start.23 = (s32[1,8]{1,0:T(1,128)S(1)}, s32[1,8]{1,0:T(1,128)}, u32[]{:S(2)}) copy-start(s32[1,8]{1,0:T(1,128)} %param.24) | copy-start | bytes 100
  214.0 48.1 %all-to-all-start.1 = ((bf16[512,4,256]{0,2,1:T(8,128)(2,1)}), bf16[512,4,256]{0,2,1:T(8,128)(2,1)S(1)}, u32[]{:S(2)}, u32[]{:S(2)}) async-start(bf16[512,4,256]{0,2,1:T(8,128)(2,1)} %bitcast.271), calls=%async_computation.1 | async-start | bytes 2097152 | tf_op jit(solution)/shard_map/all_to_all | solution.py:309
  262.1 36.0 %all-to-all-start.2 = ((bf16[512,4,256]{2,0,1:T(8,128)(2,1)}), bf16[512,4,256]{2,0,1:T(8,128)(2,1)}, u32[]{:S(2)}, u32[]{:S(2)}) async-start(bf16[512,4,256]{2,0,1:T(8,128)(2,1)} %bitcast.269), calls=%async_computation.2 | async-start | bytes 2097152 | tf_op jit(solution)/shard_map/all_to_all | solution.py:310
  266.4 452.0 %all-gather.12.cloned.1.call-start = ((), (), s32[]{:S(2)}) async-start(), calls=%async_computation.15 | async-start | bytes 8650752 | tf_op jit(solution)/shard_map/all_gather | solution.py:276
  371.2 28.5 %all-to-all-start.3 = ((bf16[4,512,256]{1,2,0:T(8,128)(2,1)}), bf16[4,512,256]{1,2,0:T(8,128)(2,1)S(1)}, u32[]{:S(2)}, u32[]{:S(2)}) async-start(bf16[4,512,256]{1,2,0:T(8,128)(2,1)} %copy.107), calls=%async_computation.3 | async-start | bytes 2097152 | tf_op jit(solution)/shard_map/all_to_all | solution.py:337
  374.8 455.1 %reduce-scatter.7.cloned.1.call-start = ((), (), s32[]{:S(2)}) async-start(), calls=%async_computation.17 | async-start | bytes 4325376 | tf_op jit(solution)/shard_map/reduce_scatter | solution.py:438
  512.3 43.0 %all-to-all-start.6 = ((bf16[4,512,256]{1,2,0:T(8,128)(2,1)}), bf16[4,512,256]{1,2,0:T(8,128)(2,1)S(1)}, u32[]{:S(2)}, u32[]{:S(2)}) async-start(bf16[4,512,256]{1,2,0:T(8,128)(2,1)} %copy.111), calls=%async_computation.6 | async-start | bytes 2097152 | tf_op jit(solution)/shard_map/all_to_all | solution.py:395
  555.3 28.9 %all-to-all-start.5 = ((bf16[4,512,256]{1,2,0:T(8,128)(2,1)}), bf16[4,512,256]{1,2,0:T(8,128)(2,1)S(1)}, u32[]{:S(2)}, u32[]{:S(2)}) async-start(bf16[4,512,256]{1,2,0:T(8,128)(2,1)} %copy.110), calls=%async_computation.5 | async-start | bytes 2097152 | tf_op jit(solution)/shard_map/all_to_all | solution.py:388
  584.2 28.7 %all-to-all-start.7 = ((bf16[4,512,256]{1,2,0:T(8,128)(2,1)}), bf16[4,512,256]{1,2,0:T(8,128)(2,1)S(1)}, u32[]{:S(2)}, u32[]{:S(2)}) async-start(bf16[4,512,256]{1,2,0:T(8,128)(2,1)} %copy.112), calls=%async_computation.7 | async-start | bytes 2097152 | tf_op jit(solution)/shard_map/all_to_all | solution.py:402
  587.7 242.2 %reduce-scatter.5.cloned.1.call-start = ((), (), s32[]{:S(2)}) async-start(), calls=%async_computation.16 | async-start | bytes 12976128 | tf_op jit(solution)/shard_map/reduce_scatter | solution.py:436
  588.4 24.5 %copy-start.1 = (bf16[1,512,1024]{2,1,0:T(8,128)(2,1)S(1)}, bf16[1,512,1024]{2,1,0:T(8,128)(2,1)}, u32[]{:S(2)}) copy-start(bf16[1,512,1024]{2,1,0:T(8,128)(2,1)} %param.23) | copy-start | bytes 3145732
  622.5 524.7 %reduce-scatter.9.cloned.1.call-start = ((), (), s32[]{:S(2)}) async-start(), calls=%async_computation.18 | async-start | bytes 17301504 | tf_op jit(solution)/shard_map/reduce_scatter | solution.py:440
  742.5 770.4 %reduce-scatter.11.cloned.1.call-start = ((), (), s32[]{:S(2)}) async-start(), calls=%async_computation.19 | async-start | bytes 17301504 | tf_op jit(solution)/shard_map/reduce_scatter | solution.py:442
  816.9 696.1 %copy-start.24 = (f32[32]{0:T(128)}, f32[32]{0:T(128)S(1)}, u32[]{:S(2)}) copy-start(f32[32]{0:T(128)S(1)} %dynamic-slice.3) | copy-start | bytes 388
  (17 other events, 150.6 us)
Sparse Core Ops, SparseCore 0:
  10.9 59.2 all-gather.7
  73.1 80.0 all-gather.5
  156.1 106.0 all-gather.9
  269.9 84.3 all-gather.11
  404.8 159.0 reduce-scatter.6
  622.6 157.6 reduce-scatter.4
  783.3 363.8 reduce-scatter.8
  1150.2 362.7 reduce-scatter.10
where the time goes:
time: 1530 us; the launch traced here: 1520 us
  waiting for transfers between devices  938 us (61%)
  matrix products  217 us (14%)
  blocking collectives  191 us (12%)
  local copies, waits for them, and re-layouts  74.1 us (5%)
  other arithmetic  35.7 us (2%)
  starting transfers between devices  27.4 us (2%)
  loops' own time  22.3 us (1%)
    reduce_scatter x1, waiting for transfers between devices, local(): lax.psum_scatter(grad_out_w, ('seq', 'group'), scatter_dimension=0, tiled...  366 us
    reduce_scatter x1, waiting for transfers between devices, local(): lax.psum_scatter(grad_in_w, ('seq', 'group'), scatter_dimension=0, tiled=...  317 us
    unnamed x2, blocking collectives  82.9 us
    all_gather x1, waiting for transfers between devices, local(): lax.all_gather(w_qkv, ('seq', 'group'), axis=0, tiled=True)  75.1 us
    all_gather x1, blocking collectives, local(): lax.all_gather(b_in, ('seq', 'group'), axis=0, tiled=True)  67.5 us
    all_to_all x1, waiting for transfers between devices, local(): lax.all_to_all(key_rows, 'group', split_axis=1, concat_axis=0, tiled=True)  41.7 us
    all_to_all x1, blocking collectives, local(): lax.all_to_all(queries, 'group', split_axis=1, concat_axis=0, tiled=True)  40.2 us
    all_to_all x1, waiting for transfers between devices, local(): lax.all_to_all(grad_key_all.reshape(flat_shape).astype(jnp.bfloat16), 'gr...  37.5 us
  transfers between devices with their start and end apart: 15, of which 10 were waited for; matrix products, arithmetic and copies ran while one was open for 21% of the time, Pallas kernels for 0%

commit v1 on v0

--- a/solution.py
+++ b/solution.py
@@ -1,13 +1,22 @@
+import functools
 import math
 
 import jax
 import jax.numpy as jnp
 from jax import lax
+from jax.experimental import pallas as pl
+from jax.experimental.pallas import tpu as pltpu
+from jax.sharding import Mesh
 from jax.sharding import PartitionSpec as P
 
 HEADS = 16
 HEAD_DIM = 64
 ROT_DIM = 16
+
+
+def prefix_ends(doc_lens):
+    order = jnp.arange(doc_lens.shape[0], dtype=jnp.int32)
+    return jnp.sum(jnp.where(order[None, :] <= order[:, None], doc_lens[None, :], 0), axis=1)
 
 
 def dot_rows(left, right):
@@ -238,7 +247,7 @@
     )
 
 
-def local(
+def local_generic(
     hidden_in,
     doc_lengths,
     ln_gain,
@@ -317,7 +326,7 @@
     value_head_rows = value_cols.reshape(heads_shape)
     all_pos = jnp.arange(seq_len, dtype=jnp.int32)
     doc_lens = doc_lengths[0]
-    doc_ends = jnp.cumsum(doc_lens)
+    doc_ends = prefix_ends(doc_lens)
     document_segment = jnp.sum((all_pos[:, None] >= doc_ends[None, :]).astype(jnp.int32), axis=1)
     doc_starts = doc_ends - doc_lens
     doc_index = jnp.arange(doc_ends.shape[0], dtype=jnp.int32)
@@ -352,13 +361,6 @@
         activated, full_out, preferred_element_type=jnp.float32
     ) + full_out_bias.astype(jnp.float32)
     hidden_out = (tokens + branch_attn + branch_mlp).astype(jnp.bfloat16)
-    full_gain, full_qkv, full_dense, full_in, full_out = (
-        lax.all_gather(ln_gain, ("seq", "group"), axis=0, tiled=True),
-        lax.all_gather(w_qkv, ("seq", "group"), axis=0, tiled=True),
-        lax.all_gather(w_dense, ("seq", "group"), axis=0, tiled=True),
-        lax.all_gather(w_in, ("seq", "group"), axis=0, tiled=True),
-        lax.all_gather(w_out, ("seq", "group"), axis=0, tiled=True),
-    )
     grad_rows = out_grad[0]
     grad_float = grad_rows.astype(jnp.float32)
     bias_grad = jnp.sum(grad_float, axis=0)
@@ -446,34 +448,565 @@
     return (hidden_out[None], grad_input[None]) + sharded
 
 
+SWAP = [(0, 1), (1, 0)]
+CHUNK = 256
+LANES = 128
+BF = jnp.bfloat16
+F32 = jnp.float32
+
+
+def mm(left, right):
+    return jnp.dot(left, right, preferred_element_type=F32)
+
+
+def other_core(value):
+    return lax.ppermute(value, "c", SWAP)
+
+
+def nt(left, right):
+    return lax.dot_general(left, right, (((1,), (1,)), ((), ())), preferred_element_type=F32)
+
+
+def rotated(heads, keep, low, high):
+    return (
+        heads * keep
+        + pltpu.roll(heads, LANES - ROT_DIM // 2, 1) * low
+        + pltpu.roll(heads, ROT_DIM // 2, 1) * high
+    )
+
+
+def attention_kernel(
+    halo,
+    tok,
+    scalar_ref,
+    q_ref,
+    k_ref,
+    v_ref,
+    kh_ref,
+    vh_ref,
+    do_ref,
+    keep_ref,
+    low_ref,
+    high_ref,
+    start_ref,
+    att_ref,
+    dqkv_ref,
+    dkvh_ref,
+    s_scr,
+    p_scr,
+    k_scr,
+    v_scr,
+    kt_scr,
+    vt_scr,
+    dk_scr,
+    dv_scr,
+    ot_scr,
+    dqt_scr,
+):
+    s, p = pl.program_id(0), pl.program_id(1)
+    pairs = pl.num_programs(1)
+    keys = (halo + 1) * tok
+    chunks = keys // CHUNK
+    lower = scalar_ref[s]
+    base = scalar_ref[2]
+    scale = 1.0 / math.sqrt(HEAD_DIM)
+    lane = lax.broadcasted_iota(jnp.int32, (tok, LANES), 1)
+    first = lane < HEAD_DIM
+
+    for b in range(halo + 1):
+        rows = pl.ds(b * tok, tok)
+        k_raw = (kh_ref[b, 0] if b < halo else k_ref[0]).astype(F32)
+        v_raw = vh_ref[b, 0] if b < halo else v_ref[0]
+        k_rot = rotated(k_raw, keep_ref[rows, :], low_ref[rows, :], high_ref[rows, :])
+        k_scr[rows, :] = k_rot.astype(BF)
+        kt_scr[:, rows] = jnp.transpose(k_rot).astype(BF)
+        v_scr[rows, :] = v_raw
+        vt_scr[:, rows] = jnp.transpose(v_raw.astype(F32)).astype(BF)
+    own = pl.ds(halo * tok, tok)
+    q_rot = rotated(q_ref[0].astype(F32), keep_ref[own, :], low_ref[own, :], high_ref[own, :])
+    q_scaled = (q_rot.astype(BF).astype(F32) * scale).astype(BF)
+    zero = jnp.zeros((tok, LANES), BF)
+    q_head = (jnp.where(first, q_scaled, zero), jnp.where(first, zero, q_scaled))
+    do_all = do_ref[0]
+    do_head = (jnp.where(first, do_all, zero), jnp.where(first, zero, do_all))
+
+    q_pos = base + halo * tok + lax.broadcasted_iota(jnp.int32, (CHUNK, tok), 1)
+    start = start_ref[0]
+    key_iota = base + lax.broadcasted_iota(jnp.int32, (CHUNK, tok), 0)
+
+    def scores(j, tops):
+        at = pl.ds(pl.multiple_of(j * CHUNK, CHUNK), CHUNK)
+        k_pos = key_iota + j * CHUNK
+        allowed = (k_pos >= start) & (k_pos <= q_pos)
+        out = []
+        for h in range(2):
+            value = jnp.where(allowed, nt(k_scr[at, :], q_head[h]), -1e30)
+            s_scr[h, at, :] = value
+            out.append(jnp.maximum(tops[h], jnp.max(value.reshape(CHUNK // 8, 8, tok), axis=0)))
+        return tuple(out)
+
+    tops = lax.fori_loop(lower, chunks, scores, (jnp.full((8, tok), -1e30, F32),) * 2)
+    tops = [jnp.max(t, axis=0, keepdims=True) for t in tops]
+
+    def exponents(j, sums):
+        at = pl.ds(pl.multiple_of(j * CHUNK, CHUNK), CHUNK)
+        out = []
+        for h in range(2):
+            value = jnp.exp(s_scr[h, at, :] - tops[h])
+            s_scr[h, at, :] = value
+            out.append(sums[h] + jnp.sum(value.reshape(CHUNK // 8, 8, tok), axis=0))
+        return tuple(out)
+
+    sums = lax.fori_loop(lower, chunks, exponents, (jnp.zeros((8, tok), F32),) * 2)
+    inverse = [1.0 / jnp.sum(t, axis=0, keepdims=True) for t in sums]
+
+    ot_scr[...] = jnp.zeros_like(ot_scr)
+    dqt_scr[...] = jnp.zeros_like(dqt_scr)
+
+    def weigh(j, carry):
+        at = pl.ds(pl.multiple_of(j * CHUNK, CHUNK), CHUNK)
+        for h in range(2):
+            prob = (s_scr[h, at, :] * inverse[h]).astype(BF)
+            p_scr[h, at, :] = prob
+            rows = pl.ds(h * HEAD_DIM, HEAD_DIM)
+            ot_scr[rows, :] += mm(vt_scr[rows, at], prob)
+        return carry
+
+    lax.fori_loop(lower, chunks, weigh, 0)
+    out_t = ot_scr[...]
+    att_ref[0] = jnp.transpose(out_t).astype(BF)
+    prod = out_t * jnp.transpose(do_all.astype(F32))
+    delta = [
+        jnp.sum(prod[:HEAD_DIM], axis=0, keepdims=True),
+        jnp.sum(prod[HEAD_DIM:], axis=0, keepdims=True),
+    ]
+
+    def clear(j, carry):
+        at = pl.ds(pl.multiple_of(j * CHUNK, CHUNK), CHUNK)
+        dk_scr[at, :] = jnp.zeros((CHUNK, LANES), F32)
+        dv_scr[at, :] = jnp.zeros((CHUNK, LANES), F32)
+        return carry
+
+    lax.fori_loop(0, lower, clear, 0)
+
+    def backward(j, carry):
+        at = pl.ds(pl.multiple_of(j * CHUNK, CHUNK), CHUNK)
+        dk = jnp.zeros((CHUNK, LANES), F32)
+        dv = jnp.zeros((CHUNK, LANES), F32)
+        for h in range(2):
+            prob = p_scr[h, at, :]
+            dp = nt(v_scr[at, :], do_head[h])
+            ds = (prob.astype(F32) * (dp - delta[h])).astype(BF)
+            dv += mm(prob, do_head[h])
+            dk += mm(ds, q_head[h])
+            rows = pl.ds(h * HEAD_DIM, HEAD_DIM)
+            dqt_scr[rows, :] += mm(kt_scr[rows, at], ds)
+        dk_scr[at, :] = dk
+        dv_scr[at, :] = dv
+        return carry
+
+    lax.fori_loop(lower, chunks, backward, 0)
+
+    def lanes_at(block):
+        return pl.ds(pl.multiple_of((block * pairs + p) * LANES, LANES), LANES)
+
+    dq = jnp.transpose(dqt_scr[...]) * scale
+    dqkv_ref[0, :, lanes_at(0)] = rotated(
+        dq, keep_ref[own, :], -low_ref[own, :], -high_ref[own, :]
+    ).astype(BF)
+    for b in range(halo + 1):
+        rows = pl.ds(b * tok, tok)
+        dk = rotated(
+            dk_scr[rows, :], keep_ref[rows, :], -low_ref[rows, :], -high_ref[rows, :]
+        ).astype(BF)
+        dv = dv_scr[rows, :].astype(BF)
+        if b < halo:
+            dkvh_ref[b, 0, :, lanes_at(0)] = dk
+            dkvh_ref[b, 0, :, lanes_at(1)] = dv
+        else:
+            dqkv_ref[0, :, lanes_at(1)] = dk
+            dqkv_ref[0, :, lanes_at(2)] = dv
+
+
+def attention(qkv, kv_halo, grad_att, keep, low, high, starts, scalars):
+    halo = kv_halo.shape[0]
+    seqs, tok, width = qkv.shape
+    pairs = width // 3 // LANES
+    keys = (halo + 1) * tok
+    row = lambda off: pl.BlockSpec((1, tok, LANES), lambda s, p, _: (s, 0, off + p))
+    far = lambda off: pl.BlockSpec((halo, 1, tok, LANES), lambda s, p, _: (0, s, 0, off + p))
+    table = pl.BlockSpec((keys, LANES), lambda s, p, _: (0, 0))
+    flops = seqs * pairs * 2 * keys * tok * HEAD_DIM * 12 * 3
+    return pl.pallas_call(
+        functools.partial(attention_kernel, halo, tok),
+        grid_spec=pltpu.PrefetchScalarGridSpec(
+            num_scalar_prefetch=1,
+            grid=(seqs, pairs),
+            in_specs=[
+                row(0),
+                row(pairs),
+                row(2 * pairs),
+                far(0),
+                far(pairs),
+                row(0),
+                table,
+                table,
+                table,
+                pl.BlockSpec((1, 1, tok), lambda s, p, _: (s, 0, 0)),
+            ],
+            out_specs=[
+                row(0),
+                pl.BlockSpec((1, tok, width), lambda s, p, _: (s, 0, 0)),
+                pl.BlockSpec((halo, 1, tok, width // 3 * 2), lambda s, p, _: (0, s, 0, 0)),
+            ],
+            scratch_shapes=[
+                pltpu.VMEM((2, keys, tok), F32),
+                pltpu.VMEM((2, keys, tok), BF),
+                pltpu.VMEM((keys, LANES), BF),
+                pltpu.VMEM((keys, LANES), BF),
+                pltpu.VMEM((LANES, keys), BF),
+                pltpu.VMEM((LANES, keys), BF),
+                pltpu.VMEM((keys, LANES), F32),
+                pltpu.VMEM((keys, LANES), F32),
+                pltpu.VMEM((LANES, tok), F32),
+                pltpu.VMEM((LANES, tok), F32),
+            ],
+        ),
+        out_shape=[
+            jax.ShapeDtypeStruct((seqs, tok, width // 3), BF),
+            jax.ShapeDtypeStruct((seqs, tok, width), BF),
+            jax.ShapeDtypeStruct((halo, seqs, tok, width // 3 * 2), BF),
+        ],
+        compiler_params=pltpu.CompilerParams(vmem_limit_bytes=48 << 20),
+        cost_estimate=pl.CostEstimate(flops=flops, bytes_accessed=16 << 20, transcendentals=0),
+        name="attention",
+    )(scalars, qkv, qkv, qkv, kv_halo, kv_halo, grad_att, keep, low, high, starts)
+
+
+def plane_gather(piece):
+    half = piece.shape[0] // 2
+    from_x = lax.ppermute(piece, "x", SWAP)
+    from_y = lax.ppermute(piece, "y", SWAP)
+    across = (lax.ppermute(from_x[:half], "y", SWAP), lax.ppermute(from_y[half:], "x", SWAP))
+    return piece, from_x, from_y, jnp.concatenate(across, axis=0)
+
+
+def plane_order(pieces, chip):
+    whole = jnp.zeros((4,) + pieces[0].shape, pieces[0].dtype)
+    for way, piece in enumerate(pieces):
+        whole = lax.dynamic_update_index_in_dim(whole, piece, chip ^ way, 0)
+    return whole
+
+
+def plane_scatter(quarter):
+    across = quarter(3)
+    half = across.shape[0] // 2
+    first = lax.ppermute(across[:half], "x", SWAP)
+    second = lax.ppermute(across[half:], "y", SWAP)
+    to_x, to_y = quarter(1), quarter(2)
+    to_x = jnp.concatenate([to_x[:half], (to_x[half:].astype(F32) + second.astype(F32)).astype(BF)])
+    to_y = jnp.concatenate([(to_y[:half].astype(F32) + first.astype(F32)).astype(BF), to_y[half:]])
+    from_x = lax.ppermute(to_x, "x", SWAP)
+    from_y = lax.ppermute(to_y, "y", SWAP)
+    return quarter(0).astype(F32) + from_x.astype(F32) + from_y.astype(F32)
+
+
+def z_gather(piece):
+    return lax.all_gather(piece, "z", axis=0, tiled=False)
+
+
+def z_scatter(piece):
+    return lax.psum_scatter(piece, "z", scatter_dimension=0, tiled=False)
+
+
+def normalise(tokens):
+    row_mean = jnp.mean(tokens, axis=-1, keepdims=True)
+    centered = tokens - row_mean
+    variance = jnp.mean(centered * centered, axis=-1, keepdims=True)
+    inv_std = lax.rsqrt(variance + 1e-05)
+    return centered * inv_std, inv_std
+
+
+def local_plane(
+    nz,
+    hidden_in,
+    doc_lengths,
+    ln_gain,
+    ln_bias,
+    w_qkv,
+    b_qkv,
+    w_dense,
+    b_dense,
+    w_in,
+    b_in,
+    w_out,
+    b_out,
+    out_grad,
+):
+    core = lax.axis_index("c")
+    chip = lax.axis_index("y") * 2 + lax.axis_index("x")
+    zi = lax.axis_index("z")
+    halo = nz // 2
+    _, tok, width = hidden_in.shape
+    ff = w_in.shape[1]
+    rows = w_in.shape[0]
+    out_rows = w_out.shape[0]
+    up = [(i, i + 1) for i in range(nz - 1)]
+    down = [(i + 1, i) for i in range(nz - 1)]
+
+    hidden_own = hidden_in[0]
+    grad_own = out_grad[0]
+    before = [hidden_own]
+    for _ in range(halo):
+        before.append(lax.ppermute(before[-1], "z", up))
+    hidden_far_own = jnp.stack(before[:0:-1])
+    hidden_other = other_core(hidden_own)
+    grad_other = other_core(grad_own)
+    lens_other = other_core(doc_lengths)
+    hidden_far_other = other_core(hidden_far_own)
+
+    def split(weight, parts):
+        blocks = weight.reshape(rows, parts, 4, 2, -1)
+        mine = lax.dynamic_index_in_dim(blocks, core, 3, keepdims=False).reshape(rows, -1)
+        theirs = lax.dynamic_index_in_dim(blocks, 1 - core, 3, keepdims=False).reshape(rows, -1)
+        return mine, theirs
+
+    def by_core(mine, theirs):
+        low = jnp.where(core == 0, mine, theirs)
+        high = jnp.where(core == 0, theirs, mine)
+        return jnp.stack([low, high])
+
+    small_row = jnp.concatenate([ln_gain, ln_bias, b_qkv, b_dense, b_in, b_out])
+    small_len = small_row.shape[0]
+    qkv_mine, qkv_theirs = split(w_qkv, 3)
+    in_mine, in_theirs = split(w_in, 1)
+    qkv_w, in_w = qkv_mine.shape[1], in_mine.shape[1]
+    sent = jnp.concatenate([qkv_theirs, in_theirs], axis=1)
+    small_sent = jnp.zeros((16, sent.shape[1]), BF).at[0, :small_len].set(small_row)
+    got = other_core(jnp.concatenate([sent, small_sent]))
+    qkv_piece = by_core(qkv_mine, got[:rows, :qkv_w]).reshape(2 * rows, qkv_w)
+    in_piece = by_core(in_mine, got[:rows, qkv_w:]).reshape(2 * rows, in_w)
+    dense_piece = w_dense.reshape(rows, 2, width // 2).transpose(1, 0, 2).reshape(2 * rows, width // 2)
+    first_piece = jnp.concatenate([qkv_piece, dense_piece], axis=1)
+    small_pair = by_core(small_row, got[rows, :small_len])
+    small_piece = jnp.zeros((16, first_piece.shape[1]), BF).at[:2, :small_len].set(small_pair)
+    first_piece = jnp.concatenate([first_piece, small_piece])
+
+    first = plane_gather(z_gather(first_piece))
+    second = plane_gather(z_gather(in_piece))
+    third = plane_gather(z_gather(w_out))
+
+    def in_order(pieces, count, columns):
+        whole = plane_order([p[:, :count, columns] for p in pieces], chip)
+        return whole.reshape(4, nz, 2, count // 2, -1).transpose(0, 2, 1, 3, 4)
+
+    w_qkv_f = in_order(first, 2 * rows, slice(0, qkv_w)).reshape(width, qkv_w)
+    dense_f = plane_order([p[:, : 2 * rows, qkv_w:] for p in first], chip)
+    dense_f = dense_f.reshape(4, nz, 2, rows, width // 2).transpose(0, 1, 3, 2, 4)
+    w_dense_f = dense_f.reshape(width // 2, width)
+    w_in_f = in_order(second, 2 * rows, slice(None)).reshape(width, in_w)
+    w_out_f = plane_order(third, chip).reshape(ff // 2, width)
+
+    small = plane_order([p[:, 2 * rows : 2 * rows + 2, :small_len] for p in first], chip)
+    small = small.transpose(0, 2, 1, 3).reshape(8 * nz, small_len).astype(F32)
+    sizes = [v.shape[0] for v in (ln_gain, ln_bias, b_qkv, b_dense, b_in, b_out)]
+    cuts = [sum(sizes[:i]) for i in range(7)]
+    gain, bias, qkv_bias, dense_bias, in_bias, out_bias = (
+        small[:, cuts[i] : cuts[i + 1]].reshape(-1) for i in range(6)
+    )
+
+    def my_half(vector, parts):
+        blocks = vector.reshape(parts, 4, 2, -1)
+        return lax.dynamic_index_in_dim(blocks, core, 2, keepdims=False).reshape(-1)
+
+    def spread(vector, parts):
+        blocks = vector.reshape(parts, 4, 1, -1)
+        mine = (jnp.arange(2) == core)[None, None, :, None]
+        return jnp.where(mine, blocks, 0.0).reshape(-1)
+
+    qkv_bias = my_half(qkv_bias, 3)
+    in_bias = my_half(in_bias, 1)
+
+    hidden = jnp.stack([hidden_own, hidden_other])
+    hidden_far = jnp.stack([hidden_far_own, hidden_far_other], axis=1)
+    grad_rows = jnp.stack([grad_own, grad_other]).reshape(2 * tok, width)
+
+    def normed_of(values):
+        return (normalise(values.astype(F32))[0] * gain + bias).astype(BF)
+
+    normed = normed_of(hidden).reshape(2 * tok, width)
+    normed_far = normed_of(hidden_far).reshape(halo * 2 * tok, width)
+
+    part = qkv_w // 3
+    qkv = (mm(normed, w_qkv_f) + qkv_bias).astype(BF).reshape(2, tok, qkv_w)
+    kv_far = (mm(normed_far, w_qkv_f[:, part:]) + qkv_bias[part:]).astype(BF)
+    grad_att = nt(grad_rows, w_dense_f).astype(BF).reshape(2, tok, part)
+
+    base = (zi - halo) * tok
+    positions = (base + jnp.arange((halo + 1) * tok, dtype=jnp.int32)).astype(F32)
+    lane = jnp.arange(LANES, dtype=jnp.int32) % HEAD_DIM
+    half_rot = ROT_DIM // 2
+    frequency = jnp.exp(-math.log(10000.0) * 2.0 * (lane % half_rot).astype(F32) / ROT_DIM)
+    angles = positions[:, None] * frequency[None, :]
+    cosine, sine = jnp.cos(angles), jnp.sin(angles)
+    keep = jnp.where(lane < ROT_DIM, cosine, 1.0)
+    low = jnp.where(lane < half_rot, -sine, 0.0)
+    high = jnp.where((lane >= half_rot) & (lane < ROT_DIM), sine, 0.0)
+
+    def doc_starts(lens):
+        ends = prefix_ends(lens)
+        own = zi * tok + jnp.arange(tok, dtype=jnp.int32)
+        return jnp.max(jnp.where(own[:, None] >= ends[None, :], ends[None, :], 0), axis=1)
+
+    starts = jnp.stack([doc_starts(doc_lengths[0]), doc_starts(lens_other[0])])
+    lower = jnp.clip((starts[:, 0] - base) // CHUNK, 0, halo * tok // CHUNK)
+    scalars = jnp.concatenate([lower, base[None]]).astype(jnp.int32)
+    attended, dqkv, dkv_far = attention(
+        qkv,
+        kv_far.reshape(halo, 2, tok, 2 * part),
+        grad_att,
+        keep,
+        low,
+        high,
+        starts[:, None, :],
+        scalars,
+    )
+    attended = attended.reshape(2 * tok, part)
+    dqkv = dqkv.reshape(2 * tok, qkv_w)
+    dkv_far = dkv_far.reshape(halo * 2 * tok, 2 * part)
+
+    dn_far = nt(dkv_far, w_qkv_f[:, part:]).astype(BF).reshape(halo, 2, tok, width)
+    dn_far = dn_far[:, 0].astype(F32) + other_core(dn_far[:, 1]).astype(F32)
+    passed = dn_far[0].astype(BF)
+    for step in range(1, halo):
+        passed = (dn_far[step] + lax.ppermute(passed, "z", down).astype(F32)).astype(BF)
+    dn_back = lax.ppermute(passed, "z", down).astype(F32)
+
+    dkv_all = jnp.concatenate([dqkv[:, part:], dkv_far])
+    g_kv = dot_rows(jnp.concatenate([normed, normed_far]), dkv_all)
+    g_qkv = jnp.concatenate([dot_rows(normed, dqkv[:, :part]), g_kv], axis=1).astype(BF)
+    g_dense = dot_rows(attended, grad_rows).astype(BF)
+    g_qkv_bias = jnp.concatenate(
+        [
+            jnp.sum(dqkv[:, :part].astype(F32), axis=0),
+            jnp.sum(dkv_all.astype(F32), axis=0),
+        ]
+    )
+    dn_att = nt(dqkv, w_qkv_f)
+
+    def quarters(full):
+        blocks = full.reshape(4, -1, full.shape[-1])
+        return lambda way: lax.dynamic_index_in_dim(blocks, chip ^ way, 0, keepdims=False)
+
+    def home_core(mine_columns):
+        mine = lax.dynamic_index_in_dim(mine_columns, core, 0, keepdims=False)
+        theirs = lax.dynamic_index_in_dim(mine_columns, 1 - core, 0, keepdims=False)
+        return by_core(mine, other_core(theirs))
+
+    s_qkv = plane_scatter(quarters(g_qkv)).astype(BF)
+    s_qkv = s_qkv.reshape(2, nz, rows, qkv_w).transpose(1, 0, 2, 3)
+    s_qkv = home_core(z_scatter(s_qkv))
+    grad_w_qkv = s_qkv.reshape(2, rows, 3, 4, -1).transpose(1, 2, 3, 0, 4).reshape(rows, -1).astype(F32)
+
+    pre_act = mm(normed, w_in_f) + in_bias
+    activated, gelu_back = jax.vjp(gelu_exact, pre_act)
+    activated = activated.astype(BF)
+    g_out = dot_rows(activated, grad_rows).astype(BF)
+    q_out, q_dense = quarters(g_out), quarters(g_dense)
+    s_out = plane_scatter(lambda way: jnp.concatenate([q_out(way), q_dense(way)]))
+    s_out = jnp.concatenate(
+        [
+            s_out[: nz * out_rows].reshape(nz, out_rows, width),
+            s_out[nz * out_rows :].reshape(nz, rows, width),
+        ],
+        axis=1,
+    ).astype(BF)
+    s_out = z_scatter(s_out).astype(F32)
+    grad_w_out, grad_w_dense = s_out[:out_rows], s_out[out_rows:]
+
+    grad_pre = gelu_back(nt(grad_rows, w_out_f))[0].astype(BF)
+    branch = (mm(attended, w_dense_f) + mm(activated, w_out_f)).reshape(2, tok, width)
+    x = hidden_own.astype(F32)
+    hidden_out = (
+        x + branch[0] + other_core(branch[1].astype(BF)).astype(F32) + dense_bias + out_bias
+    ).astype(BF)
+
+    dn = (dn_att + nt(grad_pre, w_in_f)).reshape(2, tok, width)
+    dn = dn[0] + other_core(dn[1].astype(BF)).astype(F32) + dn_back
+    xhat, inv_std = normalise(x)
+    scaled = dn * gain
+    gy = grad_own.astype(F32)
+    grad_input = gy + inv_std * (
+        scaled
+        - jnp.mean(scaled, axis=1, keepdims=True)
+        - xhat * jnp.mean(scaled * xhat, axis=1, keepdims=True)
+    )
+
+    gy_sum = jnp.sum(gy, axis=0)
+    small_grads = [
+        jnp.sum(dn * xhat, axis=0),
+        jnp.sum(dn, axis=0),
+        spread(g_qkv_bias, 3),
+        gy_sum,
+        spread(jnp.sum(grad_pre.astype(F32), axis=0), 1),
+    ]
+    small_g = jnp.concatenate([g.reshape(4, 2, nz, -1) for g in small_grads], axis=3).astype(BF)
+    g_len = small_g.shape[3]
+    small_g = small_g.transpose(0, 2, 1, 3)
+    small_g = jnp.pad(small_g, ((0, 0), (0, 0), (0, 14), (0, in_w - g_len)))
+    extra = small_g.shape[2]
+    q_small = quarters(small_g.reshape(4, nz * extra, in_w))
+    g_in = dot_rows(normed, grad_pre).astype(BF)
+    q_in = quarters(g_in)
+    s_in = plane_scatter(lambda way: jnp.concatenate([q_in(way), q_small(way)]))
+    body = s_in[: 2 * nz * rows].reshape(2, nz, rows, in_w).transpose(1, 0, 2, 3)
+    s_in = jnp.concatenate(
+        [body.reshape(nz, 2 * rows, in_w), s_in[2 * nz * rows :].reshape(nz, extra, in_w)], axis=1
+    ).astype(BF)
+    s_in = z_scatter(s_in)
+    small_mine = s_in[2 * rows : 2 * rows + 2]
+    mine = lax.dynamic_index_in_dim(small_mine, core, 0, keepdims=False)
+    theirs = lax.dynamic_index_in_dim(small_mine, 1 - core, 0, keepdims=False)
+    g_small = mine.astype(F32) + other_core(theirs).astype(F32)
+    offs = [0]
+    for v in (ln_gain, ln_bias, b_qkv, b_dense, b_in):
+        offs.append(offs[-1] + v.shape[0])
+    g_gain, g_bias, g_bqkv, g_bdense, g_bin = (g_small[offs[i] : offs[i + 1]] for i in range(5))
+    s_in = home_core(s_in[: 2 * rows].reshape(2, rows, in_w))
+    grad_w_in = s_in.reshape(2, rows, 4, -1).transpose(1, 2, 0, 3).reshape(rows, -1).astype(F32)
+    return (
+        hidden_out[None],
+        grad_input[None],
+        g_gain,
+        g_bias,
+        grad_w_qkv,
+        g_bqkv,
+        grad_w_dense,
+        g_bdense,
+        grad_w_in,
+        g_bin,
+        grad_w_out,
+        g_bdense,
+    )
+
+
 def solution(mesh):
-    in_specs = (
-        P("seq", "group", None),
-        P("seq", None),
-        P(("seq", "group")),
-        P(("seq", "group")),
-        P(("seq", "group"), None),
-        P(("seq", "group")),
-        P(("seq", "group"), None),
-        P(("seq", "group")),
-        P(("seq", "group"), None),
-        P(("seq", "group")),
-        P(("seq", "group"), None),
-        P(("seq", "group")),
-        P("seq", "group", None),
-    )
-    out_specs = (
-        P("seq", "group", None),
-        P("seq", "group", None),
-        P(("seq", "group")),
-        P(("seq", "group")),
-        P(("seq", "group"), None),
-        P(("seq", "group")),
-        P(("seq", "group"), None),
-        P(("seq", "group")),
-        P(("seq", "group"), None),
-        P(("seq", "group")),
-        P(("seq", "group"), None),
-        P(("seq", "group")),
-    )
-    return jax.shard_map(local, mesh=mesh, in_specs=in_specs, out_specs=out_specs, check_vma=False)
+    n_seq, n_group = mesh.devices.shape
+    if n_seq == 8 and n_group == 4:
+        mesh = Mesh(mesh.devices.reshape(2, 2, 2, n_group), ("y", "x", "c", "z"))
+        seq, group = ("y", "x", "c"), "z"
+        both = ("y", "x", "c", "z")
+        step = functools.partial(local_plane, n_group)
+    else:
+        seq, group, both = "seq", "group", ("seq", "group")
+        step = local_generic
+    matrix, vector = P(both, None), P(both)
+    tokens = P(seq, group, None)
+    weights = (vector, vector) + (matrix, vector) * 4
+    return jax.shard_map(
+        step,
+        mesh=mesh,
+        in_specs=(tokens, P(seq, None)) + weights + (tokens,),
+        out_specs=(tokens, tokens) + weights,
+        check_vma=False,
+    )

time: 1530 us -> 613 us (0.40)
  waiting for transfers between devices: 938 us -> 207 us
  blocking collectives: 191 us -> 0 us
  matrix products: 217 us -> 102 us
  other arithmetic: 35.7 us -> 84.8 us
  Pallas kernels: 0 us -> 42.4 us
  local copies, waits for them, and re-layouts: 74.1 us -> 107 us
  loops' own time: 22.3 us -> 0 us
  starting transfers between devices: 27.4 us -> 44.3 us
    reduce_scatter x4 -> x3, waiting for transfers between devices: 683 us -> 5.86 us  [z_scatter(): return lax.psum_scatter(piece, 'z', scatter_dimension=0, tiled=False)]
    all_to_all x7 -> x0, waiting for transfers between devices: 168 us -> none  [the longest x1 41.7 us: local(): lax.all_to_all(key_rows, 'group', split_axis=1, concat_axis=0, tiled=True)]
    ppermute x0 -> x39, waiting for transfers between devices: none -> 153 us  [the longest x1 45.2 us: local_plane(): dn_back = lax.ppermute(passed, 'z', down).astype(F32)]
    dot_general x64 -> x10, matrix products: 181 us -> 75 us  [the longest x5 44.8 us: nt(): lax.dot_general(left, right, (((1,), (1,)), ((), ())), preferred_element_...]
    unnamed x2 -> x0, blocking collectives: 82.9 us -> none
    all_gather x1 -> x0, blocking collectives: 67.5 us -> none  [local(): lax.all_gather(b_in, ('seq', 'group'), axis=0, tiled=True)]
    ppermute x0 -> x39, starting transfers between devices: none -> 44.1 us  [the longest x2 12 us: local_plane(): before.append(lax.ppermute(before[-1], 'z', up))]
    pallas_call x0 -> x1, Pallas kernels: none -> 42.4 us  [attention(): pl.pallas_call(functools.partial(attention_kernel, halo, tok), grid_spec=...]
  transfers between devices with their start and end apart: 15 -> 45, of which waited for: 10 -> 15; matrix products, arithmetic and copies ran while one was open for 21% -> 26% of each run, Pallas kernels for 0% -> 0%
where the time goes in v1:
time: 613 us; the launch traced here: 604 us
  waiting for transfers between devices  207 us (34%)
  local copies, waits for them, and re-layouts  107 us (17%)
  matrix products  102 us (17%)
  other arithmetic  84.8 us (14%)
  starting transfers between devices  44.3 us (7%)
  Pallas kernels  42.4 us (7%)
  between operations  15.6 us (3%)
    all_gather x3, waiting for transfers between devices, z_gather(): return lax.all_gather(piece, 'z', axis=0, tiled=False)  48.1 us
    ppermute x1, waiting for transfers between devices, local_plane(): dn_back = lax.ppermute(passed, 'z', down).astype(F32)  45.2 us
    dot_general x5, matrix products, nt(): lax.dot_general(left, right, (((1,), (1,)), ((), ())), preferred_element_...  44.8 us
    pallas_call x1, Pallas kernels, attention(): pl.pallas_call(functools.partial(attention_kernel, halo, tok), grid_spec=...  42.4 us
    dot_general x5, matrix products, mm(): return jnp.dot(left, right, preferred_element_type=F32)  30.2 us
    ppermute x3, waiting for transfers between devices, plane_gather(): lax.ppermute(from_x[:half], 'y', SWAP)  28.4 us
    dot_general x5, matrix products, dot_rows(): lax.dot_general(left, right, (((0,), (0,)), ((), ())), preferred_element_...  27.5 us
    ppermute x1, waiting for transfers between devices, local_plane(): lax.ppermute(passed, 'z', down).astype(F32)  23.7 us
  transfers between devices with their start and end apart: 45, of which 15 were waited for; matrix products, arithmetic and copies ran while one was open for 26% of the time, Pallas kernels for 0%

profile of v1, /device:TPU:0, one launch (start us, length us, event | category | flops | bytes accessed | tf_op | source)
XLA Modules:
  0.0 604.1 jit_solution(13938009311523469429)
XLA Ops:
  7.8 5.6 collective-permute-start.7
  42.5 8.2 %collective-permute-done.7 = bf16[512,1024]{1,0:T(8,128)(2,1)} collective-permute-done((bf16[512,1024]{1,0:T(8,128)(2,1)}, bf16[512,1024]{1,0:T(8,128)(2,1)}, u32[]{:S(2)}, u32[]{:S(2)}) %collective-permute-start.7) | collective-permute-done | bytes 1048608 | tf_op jit(solution)/shard_map/ppermute | solution.py:761
  50.7 6.4 %collective-permute-start.8 = (bf16[512,1024]{1,0:T(8,128)(2,1)}, bf16[512,1024]{1,0:T(8,128)(2,1)}, u32[]{:S(2)}, u32[]{:S(2)}) collective-permute-start(bf16[512,1024]{1,0:T(8,128)(2,1)} %collective-permute-done.7), channel_id=1, source_target_pairs={{0,1},{1,2},{2,3},{4,5},{5,6},{6,7},{8,9},{9,10},{10,11},{12,13},{... | collective-permute-start | bytes 3145736 | tf_op jit(solution)/shard_map/ppermute | solution.py:761
  71.5 23.0 %all-gather.6.cloned.1.call-done = bf16[4,64,2048]{2,1,0:T(8,128)(2,1)} async-done(((bf16[1,64,2048]{2,1,0:T(8,128)(2,1)}), bf16[4,64,2048]{2,1,0:T(8,128)(2,1)}) %all-gather.6.cloned.1.call-update) | async-done | bytes 1048592 | tf_op jit(solution)/shard_map/all_gather | solution.py:715
  104.9 25.1 %all-gather.8.cloned.1.call-done = bf16[320,2048]{1,0:T(8,128)(2,1)} async-done(((bf16[80,2048]{1,0:T(8,128)(2,1)}), bf16[320,2048]{1,0:T(8,128)(2,1)}) %all-gather.8.cloned.1.call-update) | async-done | bytes 1310736 | tf_op jit(solution)/shard_map/all_gather | solution.py:715
  149.3 22.8 %collective-permute-done.17 = bf16[2,128,1024]{2,1,0:T(8,128)(2,1)S(1)} collective-permute-done((bf16[2,128,1024]{2,1,0:T(8,128)(2,1)S(1)}, bf16[2,128,1024]{2,1,0:T(8,128)(2,1)S(1)}, u32[]{:S(2)}, u32[]{:S(2)}) %collective-permute-start.17) | collective-permute-done | bytes 524320 | tf_op jit(solution)/shard_map/ppermute | solution.py:690
  177.9 8.0 %collective-permute-done.14 = bf16[2,64,2048]{2,1,0:T(8,128)(2,1)S(1)} collective-permute-done((bf16[2,64,2048]{2,1,0:T(8,128)(2,1)S(1)}, bf16[2,64,2048]{2,1,0:T(8,128)(2,1)S(1)}, u32[]{:S(2)}, u32[]{:S(2)}) %collective-permute-start.14) | collective-permute-done | bytes 524320 | tf_op jit(solution)/shard_map/ppermute | solution.py:690
  202.2 5.6 collective-permute-done.5
  230.7 6.3 %add_convert_fusion.1 = bf16[2048,1024]{1,0:T(8,128)(2,1)} fusion(f32[1024]{0:T(1024)S(1)} %bitcast.424, bf16[2048,1024]{1,0:T(8,128)(2,1)S(1)} %fusion.4, bf16[1024,1536]{1,0:T(8,128)(2,1)S(1)} %bitcast.371), kind=kOutput, calls=%fused_computation.23 | convolution fusion | flops 4299161600 | bytes 10489856 | tf_op jit(solution)/shard_map/dot_general | solution.py:459
  236.9 42.4 %attention.1 = (bf16[2,512,512]{2,1,0:T(8,128)(2,1)S(1)}, bf16[2,512,1536]{2,1,0:T(8,128)(2,1)}, bf16[2,2,512,1024]{3,2,1,0:T(8,128)(2,1)}) custom-call(s32[3]{0:T(128)S(1)} %pad_add_fusion.1.scalar_ref, bf16[2,512,1536]{2,1,0:T(8,128)(2,1)} %bitcast.434, bf16[2,512,1536]{2,1,0:T(8,128)(2,1)} %bitcast.435, bf16[2,512,1536]{2,1,0:T(8,128)(2,1)} %bitcast.436, ...), custom_call_target="tpu_custom_call" | custom-call | flops 28991029248 | bytes 16777216 | tf_op jit(solution)/shard_map/attention/pallas_call | solution.py:640
  284.0 5.0 fusion.105
  289.1 6.4 %fusion.104 = f32[1024,2048]{1,0:T(8,128)S(1)} fusion(bf16[1024,1024]{1,0:T(8,128)(2,1)S(1)} %bitcast.384, bf16[1024,2048]{1,0:T(8,128)(2,1)} %bitcast.358), kind=kOutput, calls=%fused_computation.304 | convolution fusion | flops 4294967296 | bytes 14680064 | tf_op jit(solution)/shard_map/dot_general | solution.py:459
  295.6 27.6 %convert_reduce_fusion.1 = (bf16[2048]{0:T(1024)(128)(2,1)S(1)}, bf16[1024,2048]{1,0:T(8,128)(2,1)}, f32[1024,2048]{1,0:T(8,128)}) fusion(f32[1024,2048]{1,0:T(8,128)S(1)} %fusion.104, f32[2048]{0:T(1024)S(1)} %bitcast.410, bf16[1024,1024]{1,0:T(8,128)(2,1)S(1)} %bitcast.382, bf16[2048,1024]{1,0:T(8,128)(2,1)} %bitcast.67), kind=kOutput, calls=%fused_computation.8 | convolution fusion | flops 4452251648 | bytes 27275264 | tf_op jit(solution)/shard_map/dot_general | solution.py:467
  323.2 8.0 %multiply_convert_fusion = bf16[1024,2048]{1,0:T(8,128)(2,1)S(1)} fusion(f32[1024,2048]{1,0:T(8,128)} %get-tuple-element.54, f32[1024,2048]{1,0:T(8,128)} %copy-done.6, f32[2048]{0:T(1024)S(1)} %bitcast.411), kind=kLoop, calls=%fused_computation.10 | loop fusion | flops 8388608 | bytes 20979712 | tf_op jit(solution)/shard_map/convert_element_type | solution.py:913
  331.2 8.0 %convolution_convert_fusion = bf16[2048,1024]{1,0:T(8,128)(2,1)S(1)} fusion(bf16[1024,2048]{1,0:T(8,128)(2,1)S(1)} %multiply_convert_fusion, bf16[1024,1024]{1,0:T(8,128)(2,1)} %bitcast.380), kind=kOutput, calls=%fused_computation.46 | convolution fusion | flops 4297064448 | bytes 10485760 | tf_op jit(solution)/shard_map/dot_general | solution.py:23
  345.2 6.3 %convolution_convert_fusion.2 = bf16[2048,1024]{1,0:T(8,128)(2,1)} fusion(bf16[2048,1024]{1,0:T(8,128)(2,1)S(1)} %bitcast.360, bf16[1024,1536]{1,0:T(8,128)(2,1)S(1)} %bitcast.373), kind=kOutput, calls=%fused_computation.48 | convolution fusion | flops 4297064448 | bytes 10485760 | tf_op jit(solution)/shard_map/dot_general | solution.py:467
  355.1 8.1 %fusion.39 = bf16[1024,1024]{1,0:T(8,128)(2,1)} fusion(bf16[2048,1024]{1,0:T(8,128)(2,1)S(1)} %bitcast.362, bf16[1024,1024]{1,0:T(8,128)(2,1)S(1)} %copy-done.12, bf16[2048,1024]{1,0:T(8,128)(2,1)S(1)} %copy-done.22, bf16[1024,1024]{1,0:T(8,128)(2,1)S(1)} %fusion.17), kind=kOutput, calls=%fused_computation.95 | convolution fusion | flops 6468665344 | bytes 14680064 | tf_op jit(solution)/shard_map/dot_general | solution.py:23
  410.9 12.4 %collective-permute-done.34 = bf16[320,1024]{1,0:T(8,128)(2,1)S(1)} collective-permute-done((bf16[320,1024]{1,0:T(8,128)(2,1)S(1)}, bf16[320,1024]{1,0:T(8,128)(2,1)S(1)}, u32[]{:S(2)}, u32[]{:S(2)}) %collective-permute-start.34) | collective-permute-done | bytes 655392 | tf_op jit(solution)/shard_map/ppermute | solution.py:705
  428.1 23.7 %collective-permute-done.22 = bf16[512,1024]{1,0:T(8,128)(2,1)S(1)} collective-permute-done((bf16[512,1024]{1,0:T(8,128)(2,1)S(1)}, bf16[512,1024]{1,0:T(8,128)(2,1)S(1)}, u32[]{:S(2)}, u32[]{:S(2)}) %collective-permute-start.22) | collective-permute-done | bytes 1048608 | tf_op jit(solution)/shard_map/ppermute | solution.py:882
  462.5 45.2 %collective-permute-done.23 = bf16[512,1024]{1,0:T(8,128)(2,1)} collective-permute-done((bf16[512,1024]{1,0:T(8,128)(2,1)}, bf16[512,1024]{1,0:T(8,128)(2,1)}, u32[]{:S(2)}, u32[]{:S(2)}) %collective-permute-start.23) | collective-permute-done | bytes 1048608 | tf_op jit(solution)/shard_map/ppermute | solution.py:883
  524.3 8.7 %collective-permute-done.24 = bf16[160,2048]{1,0:T(8,128)(2,1)} collective-permute-done((bf16[160,2048]{1,0:T(8,128)(2,1)}, bf16[160,2048]{1,0:T(8,128)(2,1)}, u32[]{:S(2)}, u32[]{:S(2)}) %collective-permute-start.24) | collective-permute-done | bytes 655392 | tf_op jit(solution)/shard_map/ppermute | solution.py:705
  540.3 16.1 %collective-permute-done.27 = bf16[320,2048]{1,0:T(8,128)(2,1)} collective-permute-done((bf16[320,2048]{1,0:T(8,128)(2,1)}, bf16[320,2048]{1,0:T(8,128)(2,1)}, u32[]{:S(2)}, u32[]{:S(2)}) %collective-permute-start.27) | collective-permute-done | bytes 1310752 | tf_op jit(solution)/shard_map/ppermute | solution.py:710
  560.9 9.4 %convolution_add_fusion.1 = f32[1024,1024]{1,0:T(8,128)S(1)} fusion(f32[1024,1024]{1,0:T(8,128)} %fusion.103, bf16[1024,2048]{1,0:T(8,128)(2,1)} %copy-done.13, bf16[2048,1024]{1,0:T(8,128)(2,1)} %bitcast.67), kind=kOutput, calls=%fused_computation.94 | convolution fusion | flops 4296015872 | bytes 16777216 | tf_op jit(solution)/shard_map/dot_general | solution.py:459
  584.5 5.9 reduce-scatter.4.cloned.1.call-done
  (443 shorter events, 244.2 us)
Async XLA Ops:
  7.2 57.8 %all-gather.10.cloned.1.call-start = ((), (), s32[]{:S(2)}) async-start(), calls=%async_computation.8 | async-start | bytes 1310720 | tf_op jit(solution)/shard_map/all_gather | solution.py:715
  7.2 49.9 %collective-permute-start.1 = (bf16[512,1024]{1,0:T(8,128)(2,1)}, bf16[512,1024]{1,0:T(8,128)(2,1)}, u32[]{:S(2)}, u32[]{:S(2)}) collective-permute-start(bf16[512,1024]{1,0:T(8,128)(2,1)} %bitcast.340), channel_id=1, source_target_pairs={{0,4},{4,0},{1,5},{5,1},{2,6},{6,2},{3,7},{7,3},{8,12},{12,8},{9,1... | collective-permute-start | bytes 3145736 | tf_op jit(solution)/shard_map/ppermute | solution.py:463
  7.8 43.0 %collective-permute-start.7 = (bf16[512,1024]{1,0:T(8,128)(2,1)}, bf16[512,1024]{1,0:T(8,128)(2,1)}, u32[]{:S(2)}, u32[]{:S(2)}) collective-permute-start(bf16[512,1024]{1,0:T(8,128)(2,1)} %bitcast.341), channel_id=1, source_target_pairs={{0,1},{1,2},{2,3},{4,5},{5,6},{6,7},{8,9},{9,10},{10,11},{12,13},{... | collective-permute-start | bytes 3145736 | tf_op jit(solution)/shard_map/ppermute | solution.py:761
  13.4 81.1 %all-gather.6.cloned.1.call-start = ((), (), s32[]{:S(2)}) async-start(), calls=%async_computation.3 | async-start | bytes 1310720 | tf_op jit(solution)/shard_map/all_gather | solution.py:715
  24.6 37.2 %collective-permute-start.10 = (bf16[512,1024]{1,0:T(8,128)(2,1)}, bf16[512,1024]{1,0:T(8,128)(2,1)}, u32[]{:S(2)}, u32[]{:S(2)}) collective-permute-start(bf16[512,1024]{1,0:T(8,128)(2,1)} %bitcast.40), channel_id=1, source_target_pairs={{0,4},{4,0},{1,5},{5,1},{2,6},{6,2},{3,7},{7,3},{8,12},{12,8},{9,1... | collective-permute-start | bytes 3145736 | tf_op jit(solution)/shard_map/ppermute | solution.py:463
  38.9 91.1 %all-gather.8.cloned.1.call-start = ((), (), s32[]{:S(2)}) async-start(), calls=%async_computation.7 | async-start | bytes 1638400 | tf_op jit(solution)/shard_map/all_gather | solution.py:715
  42.3 497.0 %reduce-scatter.6.cloned.1.call-start = ((), (), s32[]{:S(2)}) async-start(), calls=%async_computation.5 | async-start | bytes 983040 | tf_op jit(solution)/shard_map/reduce_scatter | solution.py:719
  50.7 50.4 %collective-permute-start.8 = (bf16[512,1024]{1,0:T(8,128)(2,1)}, bf16[512,1024]{1,0:T(8,128)(2,1)}, u32[]{:S(2)}, u32[]{:S(2)}) collective-permute-start(bf16[512,1024]{1,0:T(8,128)(2,1)} %collective-permute-done.7), channel_id=1, source_target_pairs={{0,1},{1,2},{2,3},{4,5},{5,6},{6,7},{8,9},{9,10},{10,11},{12,13},{... | collective-permute-start | bytes 3145736 | tf_op jit(solution)/shard_map/ppermute | solution.py:761
  65.0 68.9 %collective-permute-start.15 = (bf16[4,128,1024]{2,1,0:T(8,128)(2,1)}, bf16[4,128,1024]{2,1,0:T(8,128)(2,1)}, u32[]{:S(2)}, u32[]{:S(2)}) collective-permute-start(bf16[4,128,1024]{2,1,0:T(8,128)(2,1)} %bitcast.386), channel_id=1, source_target_pairs={{0,8},{8,0},{1,9},{9,1},{2,10},{10,2},{3,11},{11,3},{4,12},{12,4},... | collective-permute-start | bytes 3145736 | tf_op jit(solution)/shard_map/ppermute | solution.py:688
  66.5 72.3 %collective-permute-start.16 = (bf16[4,128,1024]{2,1,0:T(8,128)(2,1)}, bf16[4,128,1024]{2,1,0:T(8,128)(2,1)}, u32[]{:S(2)}, u32[]{:S(2)}) collective-permute-start(bf16[4,128,1024]{2,1,0:T(8,128)(2,1)} %bitcast.387), channel_id=1, source_target_pairs={{0,16},{16,0},{1,17},{17,1},{2,18},{18,2},{3,19},{19,3},{4,20},{20... | collective-permute-start | bytes 3145736 | tf_op jit(solution)/shard_map/ppermute | solution.py:689
  94.5 48.2 %collective-permute-start.12 = (bf16[4,64,2048]{2,1,0:T(8,128)(2,1)}, bf16[4,64,2048]{2,1,0:T(8,128)(2,1)}, u32[]{:S(2)}, u32[]{:S(2)}) collective-permute-start(bf16[4,64,2048]{2,1,0:T(8,128)(2,1)} %all-gather.6.cloned.1.call-done), channel_id=1, source_target_pairs={{0,16},{16,0},{1,17},{17,1},{2,18},{18,2},{3,19},{19,3},{4,20},{20... | collective-permute-start | bytes 3145736 | tf_op jit(solution)/shard_map/ppermute | solution.py:689
  96.0 48.4 %collective-permute-start.11 = (bf16[4,64,2048]{2,1,0:T(8,128)(2,1)}, bf16[4,64,2048]{2,1,0:T(8,128)(2,1)}, u32[]{:S(2)}, u32[]{:S(2)}) collective-permute-start(bf16[4,64,2048]{2,1,0:T(8,128)(2,1)} %all-gather.6.cloned.1.call-done), channel_id=1, source_target_pairs={{0,8},{8,0},{1,9},{9,1},{2,10},{10,2},{3,11},{11,3},{4,12},{12,4},... | collective-permute-start | bytes 3145736 | tf_op jit(solution)/shard_map/ppermute | solution.py:688
  130.9 60.9 %collective-permute-start.4 = (bf16[4,80,2048]{2,1,0:T(8,128)(2,1)}, bf16[4,80,2048]{2,1,0:T(8,128)(2,1)S(1)}, u32[]{:S(2)}, u32[]{:S(2)}) collective-permute-start(bf16[4,80,2048]{2,1,0:T(8,128)(2,1)} %bitcast.398), channel_id=1, source_target_pairs={{0,16},{16,0},{1,17},{17,1},{2,18},{18,2},{3,19},{19,3},{4,20},{20... | collective-permute-start | bytes 3932168 | tf_op jit(solution)/shard_map/ppermute | solution.py:689
  133.8 59.5 %collective-permute-start.3 = (bf16[4,80,2048]{2,1,0:T(8,128)(2,1)S(1)}, bf16[4,80,2048]{2,1,0:T(8,128)(2,1)S(1)}, u32[]{:S(2)}, u32[]{:S(2)}) collective-permute-start(bf16[4,80,2048]{2,1,0:T(8,128)(2,1)S(1)} %bitcast.401), channel_id=1, source_target_pairs={{0,8},{8,0},{1,9},{9,1},{2,10},{10,2},{3,11},{11,3},{4,12},{12,4},... | collective-permute-start | bytes 3932168 | tf_op jit(solution)/shard_map/ppermute | solution.py:688
  144.4 41.5 %collective-permute-start.14 = (bf16[2,64,2048]{2,1,0:T(8,128)(2,1)S(1)}, bf16[2,64,2048]{2,1,0:T(8,128)(2,1)S(1)}, u32[]{:S(2)}, u32[]{:S(2)}) collective-permute-start(bf16[2,64,2048]{2,1,0:T(8,128)(2,1)S(1)} %slice.404), channel_id=1, source_target_pairs={{0,8},{8,0},{1,9},{9,1},{2,10},{10,2},{3,11},{11,3},{4,12},{12,4},... | collective-permute-start | bytes 1572872 | tf_op jit(solution)/shard_map/ppermute | solution.py:690
  392.7 69.8 %collective-permute-start.20 = (bf16[512,1024]{1,0:T(8,128)(2,1)}, bf16[512,1024]{1,0:T(8,128)(2,1)}, u32[]{:S(2)}, u32[]{:S(2)}) collective-permute-start(bf16[512,1024]{1,0:T(8,128)(2,1)} %slice.524), channel_id=1, source_target_pairs={{0,4},{4,0},{1,5},{5,1},{2,6},{6,2},{3,7},{7,3},{8,12},{12,8},{9,1... | collective-permute-start | bytes 3145736 | tf_op jit(solution)/shard_map/ppermute | solution.py:463
  405.3 50.3 %collective-permute-start.32 = (bf16[256,1536]{1,0:T(8,128)(2,1)S(1)}, bf16[256,1536]{1,0:T(8,128)(2,1)S(1)}, u32[]{:S(2)}, u32[]{:S(2)}) collective-permute-start(bf16[256,1536]{1,0:T(8,128)(2,1)S(1)} %pad_maximum_fusion.12), channel_id=1, source_target_pairs={{0,16},{16,0},{1,17},{17,1},{2,18},{18,2},{3,19},{19,3},{4,20},{20... | collective-permute-start | bytes 2359304 | tf_op jit(solution)/shard_map/ppermute | solution.py:710
  409.3 42.5 %collective-permute-start.22 = (bf16[512,1024]{1,0:T(8,128)(2,1)S(1)}, bf16[512,1024]{1,0:T(8,128)(2,1)S(1)}, u32[]{:S(2)}, u32[]{:S(2)}) collective-permute-start(bf16[512,1024]{1,0:T(8,128)(2,1)S(1)} %fusion.55), channel_id=1, source_target_pairs={{1,0},{2,1},{3,2},{5,4},{6,5},{7,6},{9,8},{10,9},{11,10},{13,12},{... | collective-permute-start | bytes 3145736 | tf_op jit(solution)/shard_map/ppermute | solution.py:882
  425.2 34.9 %collective-permute-start.26 = (bf16[160,2048]{1,0:T(8,128)(2,1)}, bf16[160,2048]{1,0:T(8,128)(2,1)}, u32[]{:S(2)}, u32[]{:S(2)}) collective-permute-start(bf16[160,2048]{1,0:T(8,128)(2,1)} %get-tuple-element.67), channel_id=1, source_target_pairs={{0,8},{8,0},{1,9},{9,1},{2,10},{10,2},{3,11},{11,3},{4,12},{12,4},... | collective-permute-start | bytes 1966088 | tf_op jit(solution)/shard_map/ppermute | solution.py:704
  453.1 54.5 %collective-permute-start.23 = (bf16[512,1024]{1,0:T(8,128)(2,1)}, bf16[512,1024]{1,0:T(8,128)(2,1)}, u32[]{:S(2)}, u32[]{:S(2)}) collective-permute-start(bf16[512,1024]{1,0:T(8,128)(2,1)} %fusion.37), channel_id=1, source_target_pairs={{1,0},{2,1},{3,2},{5,4},{6,5},{7,6},{9,8},{10,9},{11,10},{13,12},{... | collective-permute-start | bytes 3145736 | tf_op jit(solution)/shard_map/ppermute | solution.py:883
  455.6 60.1 %collective-permute-start.35 = (bf16[640,1024]{1,0:T(8,128)(2,1)}, bf16[640,1024]{1,0:T(8,128)(2,1)}, u32[]{:S(2)}, u32[]{:S(2)}) collective-permute-start(bf16[640,1024]{1,0:T(8,128)(2,1)} %pad_maximum_fusion.9), channel_id=1, source_target_pairs={{0,8},{8,0},{1,9},{9,1},{2,10},{10,2},{3,11},{11,3},{4,12},{12,4},... | collective-permute-start | bytes 3932168 | tf_op jit(solution)/shard_map/ppermute | solution.py:709
  457.2 58.5 %collective-permute-start.37 = (bf16[640,1024]{1,0:T(8,128)(2,1)}, bf16[640,1024]{1,0:T(8,128)(2,1)}, u32[]{:S(2)}, u32[]{:S(2)}) collective-permute-start(bf16[640,1024]{1,0:T(8,128)(2,1)} %fusion.47), channel_id=1, source_target_pairs={{0,16},{16,0},{1,17},{17,1},{2,18},{18,2},{3,19},{19,3},{4,20},{20... | collective-permute-start | bytes 3932168 | tf_op jit(solution)/shard_map/ppermute | solution.py:710
  460.1 121.9 %reduce-scatter.8.cloned.1.call-start = ((), (), s32[]{:S(2)}) async-start(), calls=%async_computation.6 | async-start | bytes 1638400 | tf_op jit(solution)/shard_map/reduce_scatter | solution.py:719
  520.0 70.4 %reduce-scatter.4.cloned.1.call-start = ((), (), s32[]{:S(2)}) async-start(), calls=%async_computation.4 | async-start | bytes 1638400 | tf_op jit(solution)/shard_map/reduce_scatter | solution.py:719
  (95 other events, 1198.3 us)
Sparse Core Ops, SparseCore 0:
  13.5 38.9 all-gather.9
  54.6 39.8 all-gather.5
  96.7 33.3 all-gather.7
  460.2 50.7 reduce-scatter.5
  520.1 31.7 reduce-scatter.7
  561.0 29.2 reduce-scatter.3

commit v2 on v0

--- a/solution.py
+++ b/solution.py
@@ -1,13 +1,22 @@
+import functools
 import math
 
 import jax
 import jax.numpy as jnp
 from jax import lax
+from jax.experimental import pallas as pl
+from jax.experimental.pallas import tpu as pltpu
+from jax.sharding import Mesh
 from jax.sharding import PartitionSpec as P
 
 HEADS = 16
 HEAD_DIM = 64
 ROT_DIM = 16
+
+
+def prefix_ends(doc_lens):
+    order = jnp.arange(doc_lens.shape[0], dtype=jnp.int32)
+    return jnp.sum(jnp.where(order[None, :] <= order[:, None], doc_lens[None, :], 0), axis=1)
 
 
 def dot_rows(left, right):
@@ -238,7 +247,7 @@
     )
 
 
-def local(
+def local_generic(
     hidden_in,
     doc_lengths,
     ln_gain,
@@ -317,7 +326,7 @@
     value_head_rows = value_cols.reshape(heads_shape)
     all_pos = jnp.arange(seq_len, dtype=jnp.int32)
     doc_lens = doc_lengths[0]
-    doc_ends = jnp.cumsum(doc_lens)
+    doc_ends = prefix_ends(doc_lens)
     document_segment = jnp.sum((all_pos[:, None] >= doc_ends[None, :]).astype(jnp.int32), axis=1)
     doc_starts = doc_ends - doc_lens
     doc_index = jnp.arange(doc_ends.shape[0], dtype=jnp.int32)
@@ -352,13 +361,6 @@
         activated, full_out, preferred_element_type=jnp.float32
     ) + full_out_bias.astype(jnp.float32)
     hidden_out = (tokens + branch_attn + branch_mlp).astype(jnp.bfloat16)
-    full_gain, full_qkv, full_dense, full_in, full_out = (
-        lax.all_gather(ln_gain, ("seq", "group"), axis=0, tiled=True),
-        lax.all_gather(w_qkv, ("seq", "group"), axis=0, tiled=True),
-        lax.all_gather(w_dense, ("seq", "group"), axis=0, tiled=True),
-        lax.all_gather(w_in, ("seq", "group"), axis=0, tiled=True),
-        lax.all_gather(w_out, ("seq", "group"), axis=0, tiled=True),
-    )
     grad_rows = out_grad[0]
     grad_float = grad_rows.astype(jnp.float32)
     bias_grad = jnp.sum(grad_float, axis=0)
@@ -446,34 +448,835 @@
     return (hidden_out[None], grad_input[None]) + sharded
 
 
+SWAP = [(0, 1), (1, 0)]
+CHUNK = 256
+LANES = 128
+BF = jnp.bfloat16
+F32 = jnp.float32
+ANY = pl.BlockSpec(memory_space=pl.ANY)
+SMALL = pl.CostEstimate(flops=0, bytes_accessed=1 << 20, transcendentals=0)
+
+
+def mm(left, right):
+    return jnp.dot(left, right, preferred_element_type=F32)
+
+
+def other_core(value):
+    return lax.ppermute(value, "c", SWAP)
+
+
+def over_x(value):
+    return lax.ppermute(value, "x", SWAP)
+
+
+def over_y(value):
+    return lax.ppermute(value, "y", SWAP)
+
+
+def nt(left, right):
+    return lax.dot_general(left, right, (((1,), (1,)), ((), ())), preferred_element_type=F32)
+
+
+def tn(left, right):
+    return lax.dot_general(left, right, (((0,), (0,)), ((), ())), preferred_element_type=F32)
+
+
+def matmul(left, right, form, deps=(), bias=None, block=512, dtype=BF, rows=None):
+    rows = rows or (left.shape[1] if form == "tn" else left.shape[0])
+    depth = left.shape[0] if form == "tn" else left.shape[1]
+    columns = right.shape[0] if form == "nt" else right.shape[1]
+    block = min(block, rows)
+    dot = {"nn": mm, "nt": nt, "tn": tn}[form]
+
+    def body(left_ref, right_ref, *rest):
+        value = dot(left_ref[...], right_ref[...])
+        if bias is not None:
+            value = value + rest[0][...]
+        rest[-1][...] = value.astype(dtype)
+
+    if form == "tn":
+        left_spec = pl.BlockSpec((depth, block), lambda i: (0, i))
+    else:
+        left_spec = pl.BlockSpec((block, depth), lambda i: (i, 0))
+    whole = pl.BlockSpec(right.shape, lambda i: (0, 0))
+    row = [] if bias is None else [pl.BlockSpec((1, columns), lambda i: (0, 0))]
+    given = [] if bias is None else [bias.reshape(1, columns)]
+    return pl.pallas_call(
+        body,
+        grid=(rows // block,),
+        in_specs=[left_spec, whole] + row + [ANY] * len(deps),
+        out_specs=pl.BlockSpec((block, columns), lambda i: (i, 0)),
+        out_shape=jax.ShapeDtypeStruct((rows, columns), dtype),
+        compiler_params=pltpu.CompilerParams(vmem_limit_bytes=48 << 20),
+        cost_estimate=SMALL,
+        name="matmul_" + form,
+    )(left, right, *given, *deps)
+
+
+def held(value, *deps):
+    def body(*refs):
+        pass
+
+    return pl.pallas_call(
+        body,
+        in_specs=[ANY] * (1 + len(deps)),
+        out_specs=ANY,
+        out_shape=jax.ShapeDtypeStruct(value.shape, value.dtype),
+        input_output_aliases={0: 0},
+        compiler_params=pltpu.CompilerParams(vmem_limit_bytes=1 << 20),
+        name="held",
+    )(value, *deps)
+
+
+def gelu_parts(value):
+    size = jnp.abs(value)
+    t = 1.0 / (1.0 + (0.3275911 / math.sqrt(2.0)) * size)
+    poly = t * (
+        0.254829592
+        + t * (-0.284496736 + t * (1.421413741 + t * (-1.453152027 + t * 1.061405429)))
+    )
+    density = jnp.exp(-0.5 * value * value)
+    tail = 0.5 * poly * density
+    below = jnp.where(value < 0, tail, 1.0 - tail)
+    return value * below, below + value * density * (1.0 / math.sqrt(2.0 * math.pi))
+
+
+def feed_forward(normed, grads, w_in, bias, w_out, deps=(), block=256):
+    tokens, width = normed.shape
+    units = w_in.shape[1]
+
+    def body(n_ref, g_ref, wi_ref, b_ref, wo_ref, *rest):
+        act_ref, pre_ref, sum_ref = rest[-3:]
+        value, slope = gelu_parts(mm(n_ref[...], wi_ref[...]) + b_ref[...])
+        act_ref[...] = value.astype(BF)
+        grad_pre = (slope * nt(g_ref[...], wo_ref[...])).astype(BF)
+        pre_ref[...] = grad_pre
+        total = jnp.sum(grad_pre.astype(F32).reshape(block // 8, 8, units), axis=0)
+
+        @pl.when(pl.program_id(0) == 0)
+        def _():
+            sum_ref[...] = total
+
+        @pl.when(pl.program_id(0) != 0)
+        def _():
+            sum_ref[...] += total
+
+    rows = lambda n: pl.BlockSpec((block, n), lambda i: (i, 0))
+    whole = lambda a: pl.BlockSpec(a.shape, lambda i: (0, 0))
+    bias = bias.reshape(1, units)
+    return pl.pallas_call(
+        body,
+        grid=(tokens // block,),
+        in_specs=[rows(width), rows(width), whole(w_in), whole(bias), whole(w_out)]
+        + [ANY] * len(deps),
+        out_specs=[rows(units), rows(units), pl.BlockSpec((8, units), lambda i: (0, 0))],
+        out_shape=[
+            jax.ShapeDtypeStruct((tokens, units), BF),
+            jax.ShapeDtypeStruct((tokens, units), BF),
+            jax.ShapeDtypeStruct((8, units), F32),
+        ],
+        compiler_params=pltpu.CompilerParams(vmem_limit_bytes=48 << 20),
+        cost_estimate=SMALL,
+        name="feed_forward",
+    )(normed, grads, w_in, bias, w_out, *deps)
+
+
+def attention_kernel(halo, tok, heads, scalar_ref, q_ref, k_ref, v_ref, do_ref, keep_ref, sine_ref, start_ref, *rest):
+    att_ref, dq_ref, dkv_ref = rest[-13:-10]
+    s_scr, p_scr, k_scr, v_scr, kt_scr, vt_scr, dk_scr, dv_scr, ot_scr, dqt_scr = rest[-10:]
+    s, p = pl.program_id(0), pl.program_id(1)
+    groups = pl.num_programs(1)
+    lanes = heads * HEAD_DIM
+    blocks = tok // CHUNK
+    chunks = (halo + 1) * blocks
+    base = scalar_ref[2 * blocks]
+    scale = 1.0 / math.sqrt(HEAD_DIM)
+    row = lax.broadcasted_iota(jnp.int32, (CHUNK, CHUNK), 0)
+    column = lax.broadcasted_iota(jnp.int32, (CHUNK, CHUNK), 1)
+    unit = (row == column).astype(F32).astype(BF)
+    from_lane = lax.broadcasted_iota(jnp.int32, (lanes, lanes), 0)
+    to_lane = lax.broadcasted_iota(jnp.int32, (lanes, lanes), 1)
+    half_rot = ROT_DIM // 2
+    place = to_lane % HEAD_DIM
+    turn = jnp.where((place < half_rot) & (from_lane == to_lane + half_rot), -1.0, 0.0)
+    turn = jnp.where(
+        (place >= half_rot) & (place < ROT_DIM) & (from_lane == to_lane - half_rot), 1.0, turn
+    ).astype(BF)
+    head_of = lax.broadcasted_iota(jnp.int32, (CHUNK, lanes), 1) // HEAD_DIM
+    zero = jnp.zeros((CHUNK, lanes), BF)
+
+    def flip(value):
+        return nt(unit, value)
+
+    def wide(table_ref, at):
+        value = table_ref[at, :]
+        return jnp.concatenate([value] * (lanes // LANES), axis=1)
+
+    def chunk_at(j):
+        return pl.ds(pl.multiple_of(j * CHUNK, CHUNK), CHUNK)
+
+    def turned(value, at, sign):
+        return value.astype(F32) * wide(keep_ref, at) + mm(value, turn) * (sign * wide(sine_ref, at))
+
+    def by_head(value):
+        return [jnp.where(head_of == h, value, zero) for h in range(heads)]
+
+    def prepare(j, carry):
+        at = chunk_at(j)
+        inner = pl.ds(pl.multiple_of((j % blocks) * CHUNK, CHUNK), CHUNK)
+        v_raw = v_ref[j // blocks, 0, inner, :]
+        k_rot = turned(k_ref[j // blocks, 0, inner, :], at, 1.0).astype(BF)
+        k_scr[at, :] = k_rot
+        kt_scr[:, at] = nt_t(k_rot)
+        v_scr[at, :] = v_raw
+        vt_scr[:, at] = nt_t(v_raw)
+        return carry
+
+    unit_lanes = (from_lane == to_lane).astype(F32).astype(BF)
+
+    def nt_t(value):
+        return nt(unit_lanes, value).astype(BF)
+
+    lowest = scalar_ref[s * blocks]
+
+    lax.fori_loop(lowest, chunks, prepare, 0)
+
+    def clear(j, carry):
+        at = chunk_at(j)
+        dk_scr[at, :] = jnp.zeros((CHUNK, lanes), F32)
+        dv_scr[at, :] = jnp.zeros((CHUNK, lanes), F32)
+        return carry
+
+    lax.fori_loop(0, chunks, clear, 0)
+
+    for b in range(blocks):
+        lower = scalar_ref[s * blocks + b]
+        upper = halo * blocks + b + 1
+        inner = pl.ds(b * CHUNK, CHUNK)
+        own = pl.ds((halo * blocks + b) * CHUNK, CHUNK)
+        q_rot = turned(q_ref[0, inner, :], own, 1.0).astype(BF)
+        q_head = by_head((q_rot.astype(F32) * scale).astype(BF))
+        grad_out = do_ref[0, inner, :]
+        start = start_ref[0, :, inner] - base
+        q_pos = (halo * blocks + b) * CHUNK + column
+
+        def scores(j, tops):
+            at = chunk_at(j)
+            k_pos = j * CHUNK + row
+            allowed = (k_pos >= start) & (k_pos <= q_pos)
+            keys = k_scr[at, :]
+            out = []
+            for h in range(heads):
+                value = jnp.where(allowed, nt(keys, q_head[h]), -1e30)
+                s_scr[h, at, :] = value
+                out.append(
+                    jnp.maximum(tops[h], jnp.max(value.reshape(CHUNK // 8, 8, CHUNK), axis=0))
+                )
+            return tuple(out)
+
+        tops = lax.fori_loop(
+            lower, upper, scores, (jnp.full((8, CHUNK), -1e30, F32),) * heads
+        )
+        tops = [jnp.max(t, axis=0, keepdims=True) for t in tops]
+        ot_scr[...] = jnp.zeros_like(ot_scr)
+        dqt_scr[...] = jnp.zeros_like(dqt_scr)
+
+        def weigh(j, sums):
+            at = chunk_at(j)
+            out = []
+            for h in range(heads):
+                value = jnp.exp(s_scr[h, at, :] - tops[h])
+                out.append(sums[h] + jnp.sum(value.reshape(CHUNK // 8, 8, CHUNK), axis=0))
+                value = value.astype(BF)
+                p_scr[h, at, :] = value
+                rows = pl.ds(h * HEAD_DIM, HEAD_DIM)
+                ot_scr[rows, :] += mm(vt_scr[rows, at], value)
+            return tuple(out)
+
+        sums = lax.fori_loop(lower, upper, weigh, (jnp.zeros((8, CHUNK), F32),) * heads)
+        inverse = [1.0 / jnp.sum(t, axis=0, keepdims=True) for t in sums]
+        out_t = jnp.concatenate(
+            [ot_scr[h * HEAD_DIM : (h + 1) * HEAD_DIM, :] * inverse[h] for h in range(heads)]
+        )
+        att_ref[0, inner, :] = flip(out_t.astype(BF)).astype(BF)
+        scaled = grad_out.astype(F32)
+        spread = jnp.zeros((CHUNK, lanes), F32)
+        for h in range(heads):
+            down = jnp.transpose(jnp.broadcast_to(inverse[h], (LANES, CHUNK)))
+            down = jnp.concatenate([down] * (lanes // LANES), axis=1)
+            spread = jnp.where(head_of == h, down, spread)
+        scaled = (scaled * spread).astype(BF)
+        prod = out_t * nt(unit_lanes, scaled)
+        delta = [
+            jnp.sum(prod[h * HEAD_DIM : (h + 1) * HEAD_DIM], axis=0, keepdims=True)
+            for h in range(heads)
+        ]
+        do_head = by_head(scaled)
+
+        def backward(j, carry):
+            at = chunk_at(j)
+            values = v_scr[at, :]
+            dk, dv = dk_scr[at, :], dv_scr[at, :]
+            for h in range(heads):
+                prob = p_scr[h, at, :]
+                ds = (prob.astype(F32) * (nt(values, do_head[h]) - delta[h])).astype(BF)
+                dv += mm(prob, do_head[h])
+                dk += mm(ds, q_head[h])
+                rows = pl.ds(h * HEAD_DIM, HEAD_DIM)
+                dqt_scr[rows, :] += mm(kt_scr[rows, at], ds)
+            dk_scr[at, :] = dk
+            dv_scr[at, :] = dv
+            return carry
+
+        lax.fori_loop(lower, upper, backward, 0)
+        dq = (flip((dqt_scr[...] * scale).astype(BF))).astype(BF)
+        dq_ref[0, inner, :] = turned(dq, own, -1.0).astype(BF)
+
+    for j in range(chunks):
+        at = pl.ds(j * CHUNK, CHUNK)
+        inner = pl.ds((j % blocks) * CHUNK, CHUNK)
+        dk = turned(dk_scr[at, :].astype(BF), at, -1.0).astype(BF)
+        for k, value in enumerate((dk, dv_scr[at, :].astype(BF))):
+            columns = pl.ds(pl.multiple_of((k * groups + p) * lanes, LANES), lanes)
+            dkv_ref[j // blocks, 0, inner, columns] = value
+
+
+def attention(queries, key_values, grad_att, keep, sine, starts, scalars, deps=(), heads=4):
+    spans, seqs, tok, width = key_values.shape
+    halo = spans - 1
+    lanes = heads * HEAD_DIM
+    groups = width // 2 // lanes
+    keys = spans * tok
+    row = pl.BlockSpec((1, tok, lanes), lambda s, p, _: (s, 0, p))
+    far = lambda off: pl.BlockSpec((spans, 1, tok, lanes), lambda s, p, _: (0, s, 0, off + p))
+    table = pl.BlockSpec((keys, LANES), lambda s, p, _: (0, 0))
+    flops = seqs * groups * heads * keys * tok * HEAD_DIM * 12 * 3
+    return pl.pallas_call(
+        functools.partial(attention_kernel, halo, tok, heads),
+        grid_spec=pltpu.PrefetchScalarGridSpec(
+            num_scalar_prefetch=1,
+            grid=(seqs, groups),
+            in_specs=[
+                row,
+                far(0),
+                far(groups),
+                row,
+                table,
+                table,
+                pl.BlockSpec((1, 1, tok), lambda s, p, _: (s, 0, 0)),
+            ]
+            + [ANY] * len(deps),
+            out_specs=[
+                row,
+                row,
+                pl.BlockSpec((spans, 1, tok, width), lambda s, p, _: (0, s, 0, 0)),
+            ],
+            scratch_shapes=[
+                pltpu.VMEM((heads, keys, CHUNK), F32),
+                pltpu.VMEM((heads, keys, CHUNK), BF),
+                pltpu.VMEM((keys, lanes), BF),
+                pltpu.VMEM((keys, lanes), BF),
+                pltpu.VMEM((lanes, keys), BF),
+                pltpu.VMEM((lanes, keys), BF),
+                pltpu.VMEM((keys, lanes), F32),
+                pltpu.VMEM((keys, lanes), F32),
+                pltpu.VMEM((lanes, CHUNK), F32),
+                pltpu.VMEM((lanes, CHUNK), F32),
+            ],
+        ),
+        out_shape=[
+            jax.ShapeDtypeStruct((seqs, tok, width // 2), BF),
+            jax.ShapeDtypeStruct((seqs, tok, width // 2), BF),
+            jax.ShapeDtypeStruct((spans, seqs, tok, width), BF),
+        ],
+        compiler_params=pltpu.CompilerParams(vmem_limit_bytes=48 << 20),
+        cost_estimate=SMALL,
+        name="attention",
+    )(scalars, queries, key_values, key_values, grad_att, keep, sine, starts, *deps)
+
+
+def away_columns(whole, core, part):
+    chips, rows, _ = whole.shape
+    strip = part // 4
+
+    def body(core_ref, w_ref, away_ref):
+        for b in range(12):
+            at = pl.multiple_of((2 * b + 1 - core_ref[0]) * strip, strip)
+            away_ref[:, :, b * strip : (b + 1) * strip] = w_ref[:, :, pl.ds(at, strip)]
+
+    return pl.pallas_call(
+        body,
+        grid=(4,),
+        in_specs=[
+            pl.BlockSpec(memory_space=pltpu.SMEM),
+            pl.BlockSpec((chips // 4, rows, 6 * part), lambda i: (i, 0, 0)),
+        ],
+        out_specs=pl.BlockSpec((chips // 4, rows, 3 * part), lambda i: (i, 0, 0)),
+        out_shape=jax.ShapeDtypeStruct((chips, rows, 3 * part), BF),
+        compiler_params=pltpu.CompilerParams(vmem_limit_bytes=16 << 20),
+        cost_estimate=SMALL,
+        name="away_columns",
+    )(core[None], whole)
+
+
+def attention_weights(whole, come, core, nz, part):
+    rows = whole.shape[1]
+    depth = 8 * nz * rows
+    strip = part // 4
+
+    def body(core_ref, w_ref, c_ref, q_ref, kv_ref, dense_ref):
+        mine = core_ref[0]
+        for z in range(nz):
+            own = pl.ds(pl.multiple_of((mine * nz + z) * rows, rows), rows)
+            other = pl.ds(pl.multiple_of(((1 - mine) * nz + z) * rows, rows), rows)
+            for b in range(12):
+                value = w_ref[z, :, pl.ds(pl.multiple_of((2 * b + mine) * strip, strip), strip)]
+                if b < 4:
+                    q_ref[own, b * strip : (b + 1) * strip] = value
+                else:
+                    kv_ref[own, (b - 4) * strip : (b - 3) * strip] = value
+            q_ref[other, :] = c_ref[z, :, :part]
+            kv_ref[other, :] = c_ref[z, :, part:]
+            dense_ref[z * rows : (z + 1) * rows, :] = w_ref[z, :, 6 * part :]
+
+    block = lambda n: pl.BlockSpec((nz, rows, n), lambda i: (i, 0, 0))
+    return pl.pallas_call(
+        body,
+        grid=(4,),
+        in_specs=[pl.BlockSpec(memory_space=pltpu.SMEM), block(8 * part), block(3 * part)],
+        out_specs=[
+            pl.BlockSpec((depth // 4, part), lambda i: (i, 0)),
+            pl.BlockSpec((depth // 4, 2 * part), lambda i: (i, 0)),
+            pl.BlockSpec((depth // 8, 2 * part), lambda i: (i, 0)),
+        ],
+        out_shape=[
+            jax.ShapeDtypeStruct((depth, part), BF),
+            jax.ShapeDtypeStruct((depth, 2 * part), BF),
+            jax.ShapeDtypeStruct((depth // 2, 2 * part), BF),
+        ],
+        compiler_params=pltpu.CompilerParams(vmem_limit_bytes=16 << 20),
+        cost_estimate=SMALL,
+        name="attention_weights",
+    )(core[None], whole, come)
+
+
+def unit_weights(whole, nz, rows, out_rows):
+    columns = whole.shape[2]
+
+    def body(w_ref, in_ref, out_ref):
+        for z in range(nz):
+            for j in range(4):
+                at = (j * nz + z) * rows
+                in_ref[at : at + rows, :] = w_ref[z, j * rows : (j + 1) * rows, :]
+            out_ref[z * out_rows : (z + 1) * out_rows, :] = w_ref[z, 4 * rows :, :]
+
+    return pl.pallas_call(
+        body,
+        grid=(2,),
+        in_specs=[pl.BlockSpec((nz, 4 * rows + out_rows, columns), lambda i: (i, 0, 0))],
+        out_specs=[
+            pl.BlockSpec((4 * nz * rows, columns), lambda i: (i, 0)),
+            pl.BlockSpec((nz * out_rows, columns), lambda i: (i, 0)),
+        ],
+        out_shape=[
+            jax.ShapeDtypeStruct((8 * nz * rows, columns), BF),
+            jax.ShapeDtypeStruct((2 * nz * out_rows, columns), BF),
+        ],
+        compiler_params=pltpu.CompilerParams(vmem_limit_bytes=16 << 20),
+        cost_estimate=SMALL,
+        name="unit_weights",
+    )(whole)
+
+
+def layer_norm(pieces, gain, bias, rows, first, extra, into=None, block=256):
+    _, tok, width = pieces[0][0].shape
+    steps = tok // block
+    count = len(pieces)
+    kept = 2 if extra else count
+
+    def body(*refs):
+        gain_ref, bias_ref = refs[count : count + 2]
+        outs = refs[-2:] if extra else refs[-1:]
+        i = pl.program_id(0)
+        for p in range(count):
+
+            @pl.when(i == p)
+            def _():
+                x = refs[p][0].astype(F32)
+                centered = x - jnp.mean(x, axis=1, keepdims=True)
+                variance = jnp.mean(centered * centered, axis=1, keepdims=True)
+                value = centered * lax.rsqrt(variance + 1e-05)
+                value = value * gain_ref[...] + bias_ref[...]
+                if p < kept:
+                    outs[0][...] = value.astype(BF)
+                if extra:
+                    outs[1][...] = value.astype(BF)
+
+    def piece_spec(p):
+        return pl.BlockSpec(
+            (1, block, width),
+            lambda i, b: (pieces[p][1], jnp.where(i == p, b, jnp.where(i < p, 0, steps - 1)), 0),
+        )
+
+    def kept_at(i, b):
+        return first // block + jnp.where(i < kept, i * steps + b, kept * steps - 1)
+
+    line = pl.BlockSpec((1, width), lambda i, b: (0, 0))
+    out_specs = [pl.BlockSpec((block, width), lambda i, b: (kept_at(i, b), 0))]
+    out_shape = [jax.ShapeDtypeStruct((rows, width), BF)]
+    if extra:
+        out_specs += [pl.BlockSpec((block, width), lambda i, b: (i * steps + b, 0))]
+        out_shape += [jax.ShapeDtypeStruct((count * tok, width), BF)]
+    given = [] if into is None else [into]
+    return pl.pallas_call(
+        body,
+        grid=(count, steps),
+        in_specs=[piece_spec(p) for p in range(count)] + [line, line] + [ANY] * len(given),
+        out_specs=out_specs,
+        out_shape=out_shape,
+        input_output_aliases={} if into is None else {count + 2: 0},
+        compiler_params=pltpu.CompilerParams(vmem_limit_bytes=32 << 20),
+        cost_estimate=SMALL,
+        name="layer_norm",
+    )(*(p[0] for p in pieces), gain.reshape(1, width), bias.reshape(1, width), *given)
+
+
+def attention_weight_grads(normed, attended, dq, dkv, grads, nz):
+    tokens, part = dq.shape
+    all_tokens, width = normed.shape
+    near = all_tokens - tokens
+    block, strip = width // 4, part // 4
+
+    rows = strip // nz
+
+    def body(n_ref, a_ref, d_ref, dkv_ref, g_ref, o_ref):
+        def put(value, at):
+            for h in range(2):
+                for z in range(nz):
+                    low = (h * nz + z) * rows
+                    o_ref[0, z, h, :, at] = value[low : low + rows]
+
+        put(tn(n_ref[near:, :], d_ref[...]).astype(BF), slice(0, part))
+        put(tn(n_ref[...], dkv_ref[...]).astype(BF), slice(part, 3 * part))
+        dense = tn(a_ref[...], g_ref[...]).astype(BF)
+        put(jnp.concatenate([dense[:, :part], dense[:, part:]]), slice(3 * part, 4 * part))
+
+    whole = lambda a: pl.BlockSpec(a.shape, lambda i: (0, 0))
+    return pl.pallas_call(
+        body,
+        grid=(4,),
+        in_specs=[
+            pl.BlockSpec((all_tokens, block), lambda i: (0, i)),
+            pl.BlockSpec((tokens, strip), lambda i: (0, i)),
+            whole(dq),
+            whole(dkv),
+            pl.BlockSpec((tokens, width), lambda i: (0, 0)),
+        ],
+        out_specs=pl.BlockSpec((1, nz, 2, rows, 4 * part), lambda i: (i, 0, 0, 0, 0)),
+        out_shape=jax.ShapeDtypeStruct((4, nz, 2, rows, 4 * part), BF),
+        compiler_params=pltpu.CompilerParams(vmem_limit_bytes=48 << 20),
+        cost_estimate=SMALL,
+        name="attention_weight_grads",
+    )(normed, attended, dq, dkv, grads)
+
+
+def summed(*values):
+    return sum(v.astype(F32) for v in values).astype(BF)
+
+
+def z_scatter(parts, axis, zi, nz):
+    for k, pairs in enumerate(z_pairs(nz)):
+        shape = parts.shape
+        blocks = parts.reshape(shape[:axis] + (shape[axis] // 2, 2) + shape[axis + 1 :])
+        bit = (zi >> k) & 1
+        come = lax.ppermute(pick(blocks, 1 - bit, axis + 1), "z", pairs)
+        parts = summed(pick(blocks, bit, axis + 1), come)
+    return lax.squeeze(parts, (axis,))
+
+
+def normalise(tokens):
+    row_mean = jnp.mean(tokens, axis=-1, keepdims=True)
+    centered = tokens - row_mean
+    variance = jnp.mean(centered * centered, axis=-1, keepdims=True)
+    inv_std = lax.rsqrt(variance + 1e-05)
+    return centered * inv_std, inv_std
+
+
+def pick(blocks, index, axis):
+    return lax.dynamic_index_in_dim(blocks, index, axis, keepdims=False)
+
+
+def by_place(place, mine, theirs):
+    low = jnp.where(place == 0, mine, theirs)
+    high = jnp.where(place == 0, theirs, mine)
+    return jnp.stack([low, high])
+
+
+def z_pairs(nz):
+    return [[(i, i ^ (1 << k)) for i in range(nz)] for k in range(nz.bit_length() - 1)]
+
+
+def local_plane(
+    nz,
+    hidden_in,
+    doc_lengths,
+    ln_gain,
+    ln_bias,
+    w_qkv,
+    b_qkv,
+    w_dense,
+    b_dense,
+    w_in,
+    b_in,
+    w_out,
+    b_out,
+    out_grad,
+):
+    core, xi, yi, zi = (lax.axis_index(a) for a in "cxyz")
+    chip = yi * 2 + xi
+    halo = nz // 2
+    _, tok, width = hidden_in.shape
+    rows, ff = w_in.shape
+    out_rows = w_out.shape[0]
+    part = width // 2
+    units = ff // 4
+    up = [(i, i + 1) for i in range(nz - 1)]
+    down = [(i + 1, i) for i in range(nz - 1)]
+    hidden_own, grad_own = hidden_in[0], out_grad[0]
+
+    small = jnp.concatenate([ln_gain, ln_bias, b_qkv, b_dense, b_in, b_out])[None]
+    sizes = [v.shape[0] for v in (ln_gain, ln_bias, b_qkv, b_dense, b_in, b_out)]
+    small_len = small.shape[1]
+    first_whole = lax.all_gather(
+        jnp.concatenate([w_qkv, w_dense], axis=1), ("y", "x", "z"), axis=0, tiled=False
+    )
+    come = other_core(away_columns(first_whole, core, part))
+
+    def halves(weight, shape, axis, place):
+        blocks = weight.reshape(shape)
+        return pick(blocks, place, axis), pick(blocks, 1 - place, axis)
+
+    in_mine, in_theirs = halves(w_in, (rows, 4, 2, -1), 2, core)
+    in_got = other_core(in_theirs.reshape(rows, -1))
+    in_core = by_place(core, in_mine.reshape(rows, -1), in_got)
+    in_mine, in_theirs = halves(in_core, (2 * rows, 2, 2, -1), 2, xi)
+    in_got = over_x(in_theirs.reshape(2 * rows, units))
+    in_piece = by_place(xi, in_mine.reshape(2 * rows, units), in_got).reshape(4 * rows, units)
+
+    before = [hidden_own]
+    for _ in range(halo):
+        before.append(lax.ppermute(before[-1], "z", up))
+    pair_own = jnp.stack([hidden_own, grad_own])
+    pair_x = over_x(pair_own)
+    pair_other, pair_x_other = other_core(pair_own), other_core(pair_x)
+    lens_other = other_core(doc_lengths)
+    near = [pair_own, pair_other, pair_x, pair_x_other]
+
+    for place, move in ((core, other_core), (xi, over_x), (yi, over_y)):
+        small = by_place(place, small, move(small)).reshape(-1, small_len)
+    for k, pairs in enumerate(z_pairs(nz)):
+        small = by_place((zi >> k) & 1, small, lax.ppermute(small, "z", pairs))
+        small = small.reshape(-1, small_len)
+    small = small.reshape(nz, 8, small_len).transpose(1, 0, 2).reshape(8 * nz, small_len).astype(F32)
+    cuts = [sum(sizes[:i]) for i in range(7)]
+    gain, bias, qkv_bias, dense_bias, in_bias, out_bias = (
+        small[:, cuts[i] : cuts[i + 1]].reshape(-1) for i in range(6)
+    )
+    qkv_bias = pick(qkv_bias.reshape(3, 4, 2, -1), core, 2).reshape(-1)
+    in_bias = pick(pick(in_bias.reshape(2, 2, 2, -1), core, 2), xi, 1).reshape(-1)
+
+    both = 2 * tok
+    kv_rows = (halo + 1) * both
+    normed_kv, normed_all = layer_norm(
+        [(v, 0) for v in near], gain, bias, kv_rows, halo * both, True
+    )
+    grads_all = jnp.concatenate([v[1] for v in near])
+
+    w_q_f, w_kv_f, w_dense_f = attention_weights(first_whole, come, core, nz, part)
+    queries = matmul(normed_all, w_q_f, "nn", bias=qkv_bias[:part], rows=both)
+    grad_att = matmul(grads_all, w_dense_f, "nt", rows=both)
+    far = []
+    for value in before[:0:-1]:
+        far += [(value[None], 0), (other_core(value)[None], 0)]
+    (normed_kv,) = layer_norm(far, gain, bias, kv_rows, 0, False, into=normed_kv)
+    key_values = (mm(normed_kv, w_kv_f) + qkv_bias[part:]).astype(BF)
+    second_whole = lax.all_gather(
+        held(jnp.concatenate([in_piece, w_out]), first_whole), ("y", "z"), axis=0, tiled=False
+    )
+
+    base = (zi - halo) * tok
+    positions = (base + jnp.arange((halo + 1) * tok, dtype=jnp.int32)).astype(F32)
+    lane = jnp.arange(LANES, dtype=jnp.int32) % HEAD_DIM
+    half_rot = ROT_DIM // 2
+    frequency = jnp.exp(-math.log(10000.0) * 2.0 * (lane % half_rot).astype(F32) / ROT_DIM)
+    angles = positions[:, None] * frequency[None, :]
+    cosine, sine = jnp.cos(angles), jnp.sin(angles)
+    keep = jnp.where(lane < ROT_DIM, cosine, 1.0)
+    sine = jnp.where(lane < ROT_DIM, sine, 0.0)
+
+    def doc_starts(lens):
+        ends = prefix_ends(lens)
+        own = zi * tok + jnp.arange(tok, dtype=jnp.int32)
+        return jnp.max(jnp.where(own[:, None] >= ends[None, :], ends[None, :], 0), axis=1)
+
+    starts = jnp.stack([doc_starts(doc_lengths[0]), doc_starts(lens_other[0])])
+    lower = jnp.maximum((starts[:, ::CHUNK] - base) // CHUNK, 0)
+    scalars = jnp.concatenate([lower.reshape(-1), base[None]]).astype(jnp.int32)
+    attended, dq, dkv = attention(
+        queries.reshape(2, tok, part),
+        key_values.reshape(halo + 1, 2, tok, 2 * part),
+        grad_att.reshape(2, tok, part),
+        keep,
+        sine,
+        starts[:, None, :],
+        scalars,
+    )
+    attended = attended.reshape(both, part)
+    dq = dq.reshape(both, part)
+    dkv = dkv.reshape(kv_rows, 2 * part)
+
+    def after(*deps):
+        return held(jnp.zeros((1, width), F32), *deps)
+
+    dn_kv = nt(dkv, w_kv_f).astype(BF).reshape(halo + 1, 2, tok, width)
+    dn_come = other_core(dn_kv[:halo, 1])
+    g_att = attention_weight_grads(normed_kv, attended, dq, dkv, grads_all, nz)
+    dn_far = summed(dn_kv[:halo, 0], held(dn_come, g_att))
+    dn_q = matmul(dq, w_q_f, "nt").reshape(2, tok, width)
+    dn_att = summed(dn_q, dn_kv[halo])
+
+    s_att = lax.psum_scatter(
+        g_att.reshape(4, nz, 2, rows, 4 * part), ("y", "x"), scatter_dimension=0, tiled=False
+    )
+    s_att = lax.psum_scatter(s_att, "z", scatter_dimension=0, tiled=False)
+
+    w_in_f, w_out_f = unit_weights(second_whole, nz, rows, out_rows)
+    activated, grad_pre, pre_sum = feed_forward(
+        normed_all, grads_all, w_in_f, in_bias, w_out_f, deps=(dn_far, dn_att)
+    )
+    passed = dn_far[0]
+    for step in range(1, halo):
+        come = held(lax.ppermute(passed, "z", down), pre_sum)
+        passed = summed(dn_far[step], come)
+    dn_back = lax.ppermute(passed, "z", down)
+
+    def away_tokens(shared, attn):
+        return jnp.stack([summed(shared[0, 1], attn[1]), shared[1, 1]])
+
+    g_in = matmul(normed_all, grad_pre, "tn", deps=(passed,)).reshape(2, -1, units)
+    in_away = pick(g_in, 1 - yi, 0)
+    in_y = over_y(in_away)
+    dn_ff = (nt(grad_pre, w_in_f) + after(in_away)).astype(BF).reshape(2, 2, tok, width)
+    dn_away = away_tokens(dn_ff, dn_att)
+    g_out = matmul(activated, grads_all, "tn", deps=(dn_away,)).reshape(2, -1, width)
+    out_away = pick(g_out, 1 - yi, 0)
+    out_y = over_y(out_away)
+    dn_come = held(other_core(dn_away), g_out)
+    dn_send = summed(dn_ff[1, 0], dn_come[1])
+    dn_x = over_x(dn_send)
+    branch = (mm(activated, w_out_f) + after(out_away, dn_send)).astype(BF)
+    branch = branch.reshape(2, 2, tok, width)
+    branch_att = matmul(attended, w_dense_f, "nn", deps=(dn_send,)).reshape(2, tok, width)
+    br_come = other_core(away_tokens(branch, branch_att))
+    br_send = summed(branch[1, 0], br_come[1])
+    br_x = over_x(br_send)
+
+    s_in = summed(pick(g_in, yi, 0), held(in_y, br_send)).reshape(4, nz, rows, units)
+    dn_x = held(dn_x, s_in)
+    dn_parts = [dn_ff[0, 0], dn_att[0], dn_come[0]]
+    br_parts = [branch[0, 0], branch_att[0], br_come[0]]
+
+    x = hidden_own.astype(F32)
+    gy = grad_own.astype(F32)
+    dn = sum(v.astype(F32) for v in (*dn_parts, dn_x, dn_back))
+    xhat, inv_std = normalise(x)
+    scaled = dn * gain
+    grad_input = gy + inv_std * (
+        scaled
+        - jnp.mean(scaled, axis=1, keepdims=True)
+        - xhat * jnp.mean(scaled * xhat, axis=1, keepdims=True)
+    )
+    out_y, br_x = held(out_y, grad_input), held(br_x, grad_input)
+    s_in = z_scatter(s_in, 1, zi, nz)
+    s_out = summed(pick(g_out, yi, 0), out_y).reshape(nz, out_rows, width)
+    grad_w_out = z_scatter(s_out, 0, zi, nz).astype(F32)
+    hidden_out = (
+        x + sum(v.astype(F32) for v in (*br_parts, br_x)) + dense_bias + out_bias
+    ).astype(BF)
+
+    def spread(vector, shape, mine):
+        return jnp.where(mine, vector.reshape(shape), 0.0).reshape(-1)
+
+    two = jnp.arange(2)
+    g_qkv_bias = jnp.concatenate([jnp.sum(v.astype(F32), axis=0) for v in (dq, dkv)])
+    small_grads = [
+        jnp.sum(dn * xhat, axis=0),
+        jnp.sum(dn, axis=0),
+        spread(g_qkv_bias, (3, 4, 1, -1), (two == core)[None, None, :, None]),
+        jnp.sum(gy, axis=0),
+        spread(
+            jnp.sum(pre_sum, axis=0),
+            (2, 1, 1, -1),
+            ((two == xi)[:, None] & (two == core)[None, :])[None, :, :, None],
+        ),
+    ]
+    small_sizes = [g.shape[0] for g in small_grads]
+    total = jnp.concatenate(small_grads)
+    for move in (other_core, over_x, over_y):
+        total = total + move(total)
+    for pairs in z_pairs(nz):
+        total = total + lax.ppermute(total, "z", pairs)
+    device = (chip * 2 + core) * nz + zi
+    small_out, at = [], 0
+    for size in small_sizes:
+        share = size // (8 * nz)
+        small_out.append(lax.dynamic_slice_in_dim(total, at + device * share, share, 0))
+        at += size
+    g_gain, g_bias, g_bqkv, g_bdense, g_bin = small_out
+
+    def home_core(columns):
+        axis = columns.ndim - 3
+        return by_place(core, pick(columns, core, axis), other_core(pick(columns, 1 - core, axis)))
+
+    grad_w_dense = s_att[:, :, 3 * part :].transpose(1, 0, 2).reshape(rows, width).astype(F32)
+    s_qkv = home_core(s_att[:, :, : 3 * part])
+    grad_w_qkv = s_qkv.reshape(2, rows, 3, 4, -1).transpose(1, 2, 3, 0, 4).reshape(rows, -1)
+    s_in = s_in.reshape(2, 2, rows, units)
+    s_in = home_core(by_place(xi, pick(s_in, xi, 0), over_x(pick(s_in, 1 - xi, 0))))
+    grad_w_in = s_in.reshape(2, 2, rows, 2, -1).transpose(2, 3, 1, 0, 4).reshape(rows, -1)
+    return (
+        hidden_out[None],
+        grad_input[None],
+        g_gain,
+        g_bias,
+        grad_w_qkv.astype(F32),
+        g_bqkv,
+        grad_w_dense,
+        g_bdense,
+        grad_w_in.astype(F32),
+        g_bin,
+        grad_w_out,
+        g_bdense,
+    )
+
+
 def solution(mesh):
-    in_specs = (
-        P("seq", "group", None),
-        P("seq", None),
-        P(("seq", "group")),
-        P(("seq", "group")),
-        P(("seq", "group"), None),
-        P(("seq", "group")),
-        P(("seq", "group"), None),
-        P(("seq", "group")),
-        P(("seq", "group"), None),
-        P(("seq", "group")),
-        P(("seq", "group"), None),
-        P(("seq", "group")),
-        P("seq", "group", None),
-    )
-    out_specs = (
-        P("seq", "group", None),
-        P("seq", "group", None),
-        P(("seq", "group")),
-        P(("seq", "group")),
-        P(("seq", "group"), None),
-        P(("seq", "group")),
-        P(("seq", "group"), None),
-        P(("seq", "group")),
-        P(("seq", "group"), None),
-        P(("seq", "group")),
-        P(("seq", "group"), None),
-        P(("seq", "group")),
-    )
-    return jax.shard_map(local, mesh=mesh, in_specs=in_specs, out_specs=out_specs, check_vma=False)
+    n_seq, n_group = mesh.devices.shape
+    if n_seq == 8 and n_group == 4:
+        mesh = Mesh(mesh.devices.reshape(2, 2, 2, n_group), ("y", "x", "c", "z"))
+        seq, group = ("y", "x", "c"), "z"
+        both = ("y", "x", "c", "z")
+        step = functools.partial(local_plane, n_group)
+    else:
+        seq, group, both = "seq", "group", ("seq", "group")
+        step = local_generic
+    matrix, vector = P(both, None), P(both)
+    tokens = P(seq, group, None)
+    weights = (vector, vector) + (matrix, vector) * 4
+    return jax.shard_map(
+        step,
+        mesh=mesh,
+        in_specs=(tokens, P(seq, None)) + weights + (tokens,),
+        out_specs=(tokens, tokens) + weights,
+        check_vma=False,
+    )

time: 1530 us -> 503 us (0.33)
  waiting for transfers between devices: 938 us -> 183 us
  blocking collectives: 191 us -> 0 us
  matrix products: 217 us -> 31.8 us
  Pallas kernels: 0 us -> 116 us
  loops' own time: 22.3 us -> 0 us
  local copies, waits for them, and re-layouts: 74.1 us -> 54.8 us
  starting transfers between devices: 27.4 us -> 45.3 us
    reduce_scatter x4 -> x1, waiting for transfers between devices: 683 us -> 0.01 us  [local_plane(): s_att = lax.psum_scatter(s_att, 'z', scatter_dimension=0, tiled=False)]
    dot_general x68 -> x4, matrix products: 217 us -> 31.8 us  [the longest x2 18.3 us: nt(): lax.dot_general(left, right, (((1,), (1,)), ((), ())), preferred_element_...]
    ppermute x0 -> x37, waiting for transfers between devices: none -> 183 us  [the longest x7 51.7 us: over_x(): return lax.ppermute(value, 'x', SWAP)]
    all_to_all x7 -> x0, waiting for transfers between devices: 168 us -> none  [the longest x1 41.7 us: local(): lax.all_to_all(key_rows, 'group', split_axis=1, concat_axis=0, tiled=True)]
    pallas_call x0 -> x24, Pallas kernels: none -> 116 us  [the longest x1 39.7 us: attention(): pl.pallas_call(functools.partial(attention_kernel, halo, tok, heads), gri...]
    all_gather x4 -> x2, waiting for transfers between devices: 85.5 us -> 0.02 us  [the longest x1 0.02 us: local_plane(): lax.all_gather(jnp.concatenate([w_qkv, w_dense], axis=1), ('y', 'x', 'z')...]
    unnamed x2 -> x0, blocking collectives: 82.9 us -> none
    all_gather x1 -> x0, blocking collectives: 67.5 us -> none  [local(): lax.all_gather(b_in, ('seq', 'group'), axis=0, tiled=True)]
  transfers between devices with their start and end apart: 15 -> 41, of which waited for: 10 -> 17; matrix products, arithmetic and copies ran while one was open for 21% -> 20% of each run, Pallas kernels for 0% -> 23%
where the time goes in v2:
time: 503 us; the launch traced here: 497 us
  waiting for transfers between devices  183 us (36%)
  Pallas kernels  116 us (23%)
  local copies, waits for them, and re-layouts  54.8 us (11%)
  other arithmetic  50.6 us (10%)
  starting transfers between devices  45.3 us (9%)
  matrix products  31.8 us (6%)
  between operations  15.6 us (3%)
    ppermute x7, waiting for transfers between devices, over_x(): return lax.ppermute(value, 'x', SWAP)  51.7 us
    pallas_call x1, Pallas kernels, attention(): pl.pallas_call(functools.partial(attention_kernel, halo, tok, heads), gri...  39.7 us
    unnamed x127, local copies, waits for them, and re-layouts  32.7 us
    ppermute x1, waiting for transfers between devices, local_plane(): dn_back = lax.ppermute(passed, 'z', down)  31.5 us
    ppermute x4, waiting for transfers between devices, z_scatter(): come = lax.ppermute(pick(blocks, 1 - bit, axis + 1), 'z', pairs)  27.8 us
    pallas_call x6, Pallas kernels, matmul(): pl.pallas_call(body, grid=(rows // block,), in_specs=[left_spec, whole] +...  24.4 us
    ppermute x2, waiting for transfers between devices, local_plane(): before.append(lax.ppermute(before[-1], 'z', up))  23.5 us
    ppermute x4, waiting for transfers between devices, over_y(): return lax.ppermute(value, 'y', SWAP)  20.6 us
  transfers between devices with their start and end apart: 41, of which 17 were waited for; matrix products, arithmetic and copies ran while one was open for 20% of the time, Pallas kernels for 23%

profile of v2, /device:TPU:0, one launch (start us, length us, event | category | flops | bytes accessed | tf_op | source)
XLA Modules:
  0.0 497.0 jit_solution(12411413305907271087)
XLA Ops:
  22.7 4.5 collective-permute-start.12
  28.0 42.7 %collective-permute-done.4 = bf16[2,352]{1,0:T(2,128)(2,1)S(1)} collective-permute-done((bf16[2,352]{1,0:T(2,128)(2,1)S(1)}, bf16[2,352]{1,0:T(2,128)(2,1)S(1)}, u32[]{:S(2)}, u32[]{:S(2)}) %collective-permute-start.4) | collective-permute-done | bytes 1440 | tf_op jit(solution)/shard_map/ppermute | solution.py:469
  93.3 23.5 %collective-permute-done.13 = bf16[512,1024]{1,0:T(8,128)(2,1)} collective-permute-done((bf16[512,1024]{1,0:T(8,128)(2,1)}, bf16[512,1024]{1,0:T(8,128)(2,1)}, u32[]{:S(2)}, u32[]{:S(2)}) %collective-permute-start.13) | collective-permute-done | bytes 1048608 | tf_op jit(solution)/shard_map/ppermute | solution.py:1068
  124.0 6.2 %layer_norm.2 = (bf16[3072,1024]{1,0:T(8,128)(2,1)S(1)}, bf16[2048,1024]{1,0:T(8,128)(2,1)S(1)}) custom-call(bf16[2,512,1024]{2,1,0:T(8,128)(2,1)} %constant_dynamic-update-slice_fusion.refs_0_, bf16[2,512,1024]{2,1,0:T(8,128)(2,1)} %collective-permute-done.refs_1_, bf16[2,512,1024]{2,1,0:T(8,128)(2,1)S(1)} %collective-permute-done.1.refs_2_, ...), custom_call_target="tpu_custom_call" | custom-call | bytes 1048576 | tf_op jit(solution)/shard_map/layer_norm/pallas_call | solution.py:931
  130.2 8.4 %layer_norm.3.n_ref = bf16[3072,1024]{1,0:T(8,128)(2,1)S(1)} custom-call(bf16[1,512,1024]{2,1,0:T(8,128)(2,1)} %bitcast.35.refs_0_, bf16[1,512,1024]{2,1,0:T(8,128)(2,1)} %bitcast.36.refs_1_, bf16[1,512,1024]{2,1,0:T(8,128)(2,1)} %bitcast.37.refs_2_, bf16[1,512,1024]{2,1,0:T(8,128)(2,1)} %bitcast.38.refs_3_, ...), custom_call_target="tpu_custom_call", output_to_operand_aliasing={{}: (6, {})} | custom-call | bytes 1048576 | tf_op jit(solution)/shard_map/layer_norm/pallas_call | solution.py:931
  157.5 8.6 %add_convert_fusion = bf16[3072,1024]{1,0:T(8,128)(2,1)} fusion(f32[1024]{0:T(1024)S(1)} %bitcast.330, bf16[3072,1024]{1,0:T(8,128)(2,1)S(1)} %bitcast.271, bf16[1024,1024]{1,0:T(8,128)(2,1)S(1)} %get-tuple-element.30), kind=kOutput, calls=%fused_computation.1 | convolution fusion | flops 6448742400 | bytes 14684160 | tf_op jit(solution)/shard_map/dot_general | solution.py:461
  166.1 39.7 %attention.1 = (bf16[2,512,512]{2,1,0:T(8,128)(2,1)S(1)}, bf16[2,512,512]{2,1,0:T(8,128)(2,1)S(1)}, bf16[3,2,512,1024]{3,2,1,0:T(8,128)(2,1)}) custom-call(s32[5]{0:T(128)S(1)} %pad_add_fusion.1.scalar_ref, bf16[2,512,512]{2,1,0:T(8,128)(2,1)S(1)} %bitcast.287, bf16[3,2,512,1024]{3,2,1,0:T(8,128)(2,1)} %bitcast.294, bf16[3,2,512,1024]{3,2,1,0:T(8,128)(2,1)} %bitcast.295, ...), custom_call_target="tpu_custom_call" | custom-call | bytes 1048576 | tf_op jit(solution)/shard_map/attention/pallas_call | solution.py:754
  205.8 10.3 %convolution_convert_fusion = bf16[3072,1024]{1,0:T(8,128)(2,1)S(1)} fusion(bf16[3072,1024]{1,0:T(8,128)(2,1)} %bitcast.292, bf16[1024,1024]{1,0:T(8,128)(2,1)S(1)} %get-tuple-element.30), kind=kOutput, calls=%fused_computation.4 | convolution fusion | flops 6445596672 | bytes 14680064 | tf_op jit(solution)/shard_map/dot_general | solution.py:477
  220.2 14.5 %attention_weight_grads.1.refs_1_ = bf16[4,4,2,32,2048]{4,3,2,1,0:T(8,128)(2,1)} custom-call(bf16[3072,1024]{1,0:T(8,128)(2,1)} %copy-done.5, bf16[1024,512]{1,0:T(8,128)(2,1)S(1)} %bitcast.283, bf16[1024,512]{1,0:T(8,128)(2,1)S(1)} %bitcast.279, bf16[3072,1024]{1,0:T(8,128)(2,1)} %bitcast.293, bf16[2048,1024]{1,0:T(8,128)(2,1)} %pad_maximum_fusion.left_ref.g_ref.right_ref), custom_call_target="tpu_custom_call" | custom-call | bytes 1048576 | tf_op jit(solution)/shard_map/attention_weight_grads/pallas_call | solution.py:965
  246.1 3.9 add_convert_fusion.3
  252.7 17.6 %feed_forward.1 = (bf16[2048,1024]{1,0:T(8,128)(2,1)}, bf16[2048,1024]{1,0:T(8,128)(2,1)}, f32[8,1024]{1,0:T(8,128)S(1)}) custom-call(bf16[2048,1024]{1,0:T(8,128)(2,1)} %copy-done.3, bf16[2048,1024]{1,0:T(8,128)(2,1)} %pad_maximum_fusion.left_ref.g_ref.right_ref, bf16[1024,1024]{1,0:T(8,128)(2,1)S(1)} %get-tuple-element.26.wi_ref, f32[1,1024]{1,0:T(1,128)S(1)} %bitcast.288, ...), custom_call_target="tpu_custom_call" | custom-call | bytes 1048576 | tf_op jit(solution)/shard_map/feed_forward/pallas_call | solution.py:567
  270.3 20.2 %collective-permute-done.17.refs_0_ = bf16[512,1024]{1,0:T(8,128)(2,1)} collective-permute-done((bf16[512,1024]{1,0:T(8,128)(2,1)}, bf16[512,1024]{1,0:T(8,128)(2,1)}, u32[]{:S(2)}, u32[]{:S(2)}) %collective-permute-start.17) | collective-permute-done | bytes 1048608 | tf_op jit(solution)/shard_map/ppermute | solution.py:1159
  293.2 7.6 %matmul_tn.2 = bf16[1024,1024]{1,0:T(8,128)(2,1)S(1)} custom-call(bf16[2048,1024]{1,0:T(8,128)(2,1)} %copy-done.3, bf16[2048,1024]{1,0:T(8,128)(2,1)} %get-tuple-element.36.right_ref, bf16[512,1024]{1,0:T(8,128)(2,1)} %fusion.23.rest_0_), custom_call_target="tpu_custom_call" | custom-call | bytes 1048576 | tf_op jit(solution)/shard_map/matmul_tn/pallas_call | solution.py:504
  300.9 8.0 %add_convert_fusion.2 = bf16[2048,1024]{1,0:T(8,128)(2,1)S(1)} fusion(f32[1024]{0:T(1024)S(1)} %bitcast.289, bf16[2048,1024]{1,0:T(8,128)(2,1)} %get-tuple-element.36.right_ref, bf16[1024,1024]{1,0:T(8,128)(2,1)S(1)} %get-tuple-element.26.wi_ref), kind=kOutput, calls=%fused_computation.3 | convolution fusion | flops 4299161600 | bytes 10489856 | tf_op jit(solution)/shard_map/dot_general | solution.py:477
  315.5 7.6 %matmul_tn.3 = bf16[1024,1024]{1,0:T(8,128)(2,1)S(1)} custom-call(bf16[2048,1024]{1,0:T(8,128)(2,1)} %get-tuple-element.35.left_ref, bf16[2048,1024]{1,0:T(8,128)(2,1)} %pad_maximum_fusion.left_ref.g_ref.right_ref, bf16[2,512,1024]{2,1,0:T(8,128)(2,1)} %pad_maximum_fusion.1.rest_0_), custom_call_target="tpu_custom_call" | custom-call | bytes 1048576 | tf_op jit(solution)/shard_map/matmul_tn/pallas_call | solution.py:504
  332.2 4.9 add_convert_fusion.1
  342.0 5.6 %collective-permute-start.22 = (bf16[512,1024]{1,0:T(8,128)(2,1)}, bf16[512,1024]{1,0:T(8,128)(2,1)S(1)}, u32[]{:S(2)}, u32[]{:S(2)}) collective-permute-start(bf16[512,1024]{1,0:T(8,128)(2,1)} %copy-done.20), channel_id=1, source_target_pairs={{0,16},{16,0},{1,17},{17,1},{2,18},{18,2},{3,19},{19,3},{4,20},{20... | collective-permute-start | bytes 3145736 | tf_op jit(solution)/shard_map/ppermute | solution.py:473
  355.2 16.6 %collective-permute-done.22.refs_0_ = bf16[512,1024]{1,0:T(8,128)(2,1)S(1)} collective-permute-done((bf16[512,1024]{1,0:T(8,128)(2,1)}, bf16[512,1024]{1,0:T(8,128)(2,1)S(1)}, u32[]{:S(2)}, u32[]{:S(2)}) %collective-permute-start.22) | collective-permute-done | bytes 1048608 | tf_op jit(solution)/shard_map/ppermute | solution.py:473
  377.8 31.5 %collective-permute-done.23 = bf16[512,1024]{1,0:T(8,128)(2,1)} collective-permute-done((bf16[512,1024]{1,0:T(8,128)(2,1)}, bf16[512,1024]{1,0:T(8,128)(2,1)}, u32[]{:S(2)}, u32[]{:S(2)}) %collective-permute-start.23) | collective-permute-done | bytes 1048608 | tf_op jit(solution)/shard_map/ppermute | solution.py:1161
  423.1 6.9 %collective-permute-start.27 = (f32[10240]{0:T(1024)S(1)}, f32[10240]{0:T(1024)S(1)}, u32[]{:S(2)}, u32[]{:S(2)}) collective-permute-start(f32[10240]{0:T(1024)S(1)} %add.343), channel_id=1, source_target_pairs={{0,1},{1,0},{2,3},{3,2},{4,5},{5,4},{6,7},{7,6},{8,9},{9,8},{10,11... | collective-permute-start | bytes 122888 | tf_op jit(solution)/shard_map/ppermute | solution.py:1228
  442.0 11.5 %collective-permute-done.30 = bf16[4,2,32,1024]{3,2,1,0:T(8,128)(2,1)} collective-permute-done((bf16[4,2,32,1024]{3,2,1,0:T(8,128)(2,1)}, bf16[4,2,32,1024]{3,2,1,0:T(8,128)(2,1)}, u32[]{:S(2)}, u32[]{:S(2)}) %collective-permute-start.30) | collective-permute-done | bytes 524320 | tf_op jit(solution)/shard_map/ppermute | solution.py:992
  454.9 7.2 %collective-permute-done.35 = bf16[2,128,1024]{2,1,0:T(8,128)(2,1)} collective-permute-done((bf16[2,128,1024]{2,1,0:T(8,128)(2,1)}, bf16[2,128,1024]{2,1,0:T(8,128)(2,1)}, u32[]{:S(2)}, u32[]{:S(2)}) %collective-permute-start.35) | collective-permute-done | bytes 524320 | tf_op jit(solution)/shard_map/ppermute | solution.py:992
  463.5 9.1 %collective-permute-done.31 = bf16[4,1,32,1024]{3,2,1,0:T(8,128)(2,1)S(1)} collective-permute-done((bf16[4,1,32,1024]{3,2,1,0:T(8,128)(2,1)S(1)}, bf16[4,1,32,1024]{3,2,1,0:T(8,128)(2,1)S(1)}, u32[]{:S(2)}, u32[]{:S(2)}) %collective-permute-start.31) | collective-permute-done | bytes 262176 | tf_op jit(solution)/shard_map/ppermute | solution.py:992
  485.5 4.0 fusion.25
  (351 shorter events, 161.0 us)
Async XLA Ops:
  7.2 109.8 %all-gather.5.cloned.1.call-start = ((), (), s32[]{:S(2)}) async-start(), calls=%async_computation.3 | async-start | bytes 4456448 | tf_op jit(solution)/shard_map/all_gather | solution.py:1050
  9.1 240.9 %all-gather.7.cloned.1.call-start = ((), (), s32[]{:S(2)}) async-start(), calls=%async_computation.4 | async-start | bytes 4718592 | tf_op jit(solution)/shard_map/all_gather | solution.py:1103
  12.5 75.5 %collective-permute-start.1 = (bf16[2,512,1024]{2,1,0:T(8,128)(2,1)}, bf16[2,512,1024]{2,1,0:T(8,128)(2,1)S(1)}, u32[]{:S(2)}, u32[]{:S(2)}) collective-permute-start(bf16[2,512,1024]{2,1,0:T(8,128)(2,1)} %constant_dynamic-update-slice_fusion.refs_0_), channel_id=1, source_target_pairs={{0,8},{8,0},{1,9},{9,1},{2,10},{10,2},{3,11},{11,3},{4,12},{12,4},... | collective-permute-start | bytes 6291464 | tf_op jit(solution)/shard_map/ppermute | solution.py:469
  15.5 107.2 %collective-permute-start = (bf16[2,512,1024]{2,1,0:T(8,128)(2,1)}, bf16[2,512,1024]{2,1,0:T(8,128)(2,1)}, u32[]{:S(2)}, u32[]{:S(2)}) collective-permute-start(bf16[2,512,1024]{2,1,0:T(8,128)(2,1)} %constant_dynamic-update-slice_fusion.refs_0_), channel_id=1, source_target_pairs={{0,4},{4,0},{1,5},{5,1},{2,6},{6,2},{3,7},{7,3},{8,12},{12,8},{9,1... | collective-permute-start | bytes 6291464 | tf_op jit(solution)/shard_map/ppermute | solution.py:465
  18.0 70.2 %collective-permute-start.8 = (bf16[32,2048]{1,0:T(8,128)(2,1)S(1)}, bf16[32,2048]{1,0:T(8,128)(2,1)S(1)}, u32[]{:S(2)}, u32[]{:S(2)}) collective-permute-start(bf16[32,2048]{1,0:T(8,128)(2,1)S(1)} %bitcast.322), channel_id=1, source_target_pairs={{0,4},{4,0},{1,5},{5,1},{2,6},{6,2},{3,7},{7,3},{8,12},{12,8},{9,1... | collective-permute-start | bytes 393224 | tf_op jit(solution)/shard_map/ppermute | solution.py:465
  22.7 61.7 %collective-permute-start.12 = (bf16[512,1024]{1,0:T(8,128)(2,1)}, bf16[512,1024]{1,0:T(8,128)(2,1)}, u32[]{:S(2)}, u32[]{:S(2)}) collective-permute-start(bf16[512,1024]{1,0:T(8,128)(2,1)} %bitcast.291), channel_id=1, source_target_pairs={{0,1},{1,2},{2,3},{4,5},{5,6},{6,7},{8,9},{9,10},{10,11},{12,13},{... | collective-permute-start | bytes 3145736 | tf_op jit(solution)/shard_map/ppermute | solution.py:1068
  27.3 43.4 %collective-permute-start.4 = (bf16[2,352]{1,0:T(2,128)(2,1)S(1)}, bf16[2,352]{1,0:T(2,128)(2,1)S(1)}, u32[]{:S(2)}, u32[]{:S(2)}) collective-permute-start(bf16[2,352]{1,0:T(2,128)(2,1)S(1)} %maximum_bitcast_fusion.1), channel_id=1, source_target_pairs={{0,8},{8,0},{1,9},{9,1},{2,10},{10,2},{3,11},{11,3},{4,12},{12,4},... | collective-permute-start | bytes 4232 | tf_op jit(solution)/shard_map/ppermute | solution.py:469
  84.4 32.4 %collective-permute-start.13 = (bf16[512,1024]{1,0:T(8,128)(2,1)}, bf16[512,1024]{1,0:T(8,128)(2,1)}, u32[]{:S(2)}, u32[]{:S(2)}) collective-permute-start(bf16[512,1024]{1,0:T(8,128)(2,1)} %collective-permute-done.12), channel_id=1, source_target_pairs={{0,1},{1,2},{2,3},{4,5},{5,6},{6,7},{8,9},{9,10},{10,11},{12,13},{... | collective-permute-start | bytes 3145736 | tf_op jit(solution)/shard_map/ppermute | solution.py:1068
  88.0 36.0 %collective-permute-start.2 = (bf16[2,512,1024]{2,1,0:T(8,128)(2,1)S(1)}, bf16[2,512,1024]{2,1,0:T(8,128)(2,1)}, u32[]{:S(2)}, u32[]{:S(2)}) collective-permute-start(bf16[2,512,1024]{2,1,0:T(8,128)(2,1)S(1)} %collective-permute-done.1.refs_2_), channel_id=1, source_target_pairs={{0,4},{4,0},{1,5},{5,1},{2,6},{6,2},{3,7},{7,3},{8,12},{12,8},{9,1... | collective-permute-start | bytes 6291464 | tf_op jit(solution)/shard_map/ppermute | solution.py:465
  91.0 30.2 %collective-permute-start.9 = (bf16[64,1024]{1,0:T(8,128)(2,1)}, bf16[64,1024]{1,0:T(8,128)(2,1)S(1)}, u32[]{:S(2)}, u32[]{:S(2)}) collective-permute-start(bf16[64,1024]{1,0:T(8,128)(2,1)} %bitcast.142), channel_id=1, source_target_pairs={{0,8},{8,0},{1,9},{9,1},{2,10},{10,2},{3,11},{11,3},{4,12},{12,4},... | collective-permute-start | bytes 393224 | tf_op jit(solution)/shard_map/ppermute | solution.py:469
  93.1 37.1 %collective-permute-start.15 = (bf16[512,1024]{1,0:T(8,128)(2,1)}, bf16[512,1024]{1,0:T(8,128)(2,1)}, u32[]{:S(2)}, u32[]{:S(2)}) collective-permute-start(bf16[512,1024]{1,0:T(8,128)(2,1)} %collective-permute-done.12), channel_id=1, source_target_pairs={{0,4},{4,0},{1,5},{5,1},{2,6},{6,2},{3,7},{7,3},{8,12},{12,8},{9,1... | collective-permute-start | bytes 3145736 | tf_op jit(solution)/shard_map/ppermute | solution.py:465
  121.2 24.8 %collective-permute-start.11 = (bf16[16,32,1536]{2,1,0:T(8,128)(2,1)}, bf16[16,32,1536]{2,1,0:T(8,128)(2,1)}, u32[]{:S(2)}, u32[]{:S(2)}) collective-permute-start(bf16[16,32,1536]{2,1,0:T(8,128)(2,1)} %away_columns.1), channel_id=1, source_target_pairs={{0,4},{4,0},{1,5},{5,1},{2,6},{6,2},{3,7},{7,3},{8,12},{12,8},{9,1... | collective-permute-start | bytes 4718600 | tf_op jit(solution)/shard_map/ppermute | solution.py:465
  145.5 207.7 %reduce-scatter.7.cloned.1.call-start = ((), (), s32[]{:S(2)}) async-start(), calls=%async_computation.5 | async-start | bytes 5242880
  241.8 48.7 %collective-permute-start.17 = (bf16[512,1024]{1,0:T(8,128)(2,1)}, bf16[512,1024]{1,0:T(8,128)(2,1)}, u32[]{:S(2)}, u32[]{:S(2)}) collective-permute-start(bf16[512,1024]{1,0:T(8,128)(2,1)} %slice_bitcast_fusion.15), channel_id=1, source_target_pairs={{1,0},{2,1},{3,2},{5,4},{6,5},{7,6},{9,8},{10,9},{11,10},{13,12},{... | collective-permute-start | bytes 3145736 | tf_op jit(solution)/shard_map/ppermute | solution.py:1159
  246.0 193.4 %reduce-scatter.5.cloned.1.call-start = ((), (), s32[]{:S(2)}) async-start(), calls=%async_computation.2 | async-start | bytes 1310720 | tf_op jit(solution)/shard_map/reduce_scatter | solution.py:1151
  342.0 29.8 %collective-permute-start.22 = (bf16[512,1024]{1,0:T(8,128)(2,1)}, bf16[512,1024]{1,0:T(8,128)(2,1)S(1)}, u32[]{:S(2)}, u32[]{:S(2)}) collective-permute-start(bf16[512,1024]{1,0:T(8,128)(2,1)} %copy-done.20), channel_id=1, source_target_pairs={{0,16},{16,0},{1,17},{17,1},{2,18},{18,2},{3,19},{19,3},{4,20},{20... | collective-permute-start | bytes 3145736 | tf_op jit(solution)/shard_map/ppermute | solution.py:473
  351.5 57.8 %collective-permute-start.23 = (bf16[512,1024]{1,0:T(8,128)(2,1)}, bf16[512,1024]{1,0:T(8,128)(2,1)}, u32[]{:S(2)}, u32[]{:S(2)}) collective-permute-start(bf16[512,1024]{1,0:T(8,128)(2,1)} %fusion.23.rest_0_), channel_id=1, source_target_pairs={{1,0},{2,1},{3,2},{5,4},{6,5},{7,6},{9,8},{10,9},{11,10},{13,12},{... | collective-permute-start | bytes 3145736 | tf_op jit(solution)/shard_map/ppermute | solution.py:1161
  352.8 25.0 %collective-permute-start.21 = (bf16[512,1024]{1,0:T(8,128)(2,1)S(1)}, bf16[512,1024]{1,0:T(8,128)(2,1)S(1)}, u32[]{:S(2)}, u32[]{:S(2)}) collective-permute-start(bf16[512,1024]{1,0:T(8,128)(2,1)S(1)} %fusion.21.refs_2_.rest_0_), channel_id=1, source_target_pairs={{0,8},{8,0},{1,9},{9,1},{2,10},{10,2},{3,11},{11,3},{4,12},{12,4},... | collective-permute-start | bytes 3145736 | tf_op jit(solution)/shard_map/ppermute | solution.py:469
  353.0 63.8 %collective-permute-start.34 = (bf16[512,1024]{1,0:T(8,128)(2,1)}, bf16[512,1024]{1,0:T(8,128)(2,1)}, u32[]{:S(2)}, u32[]{:S(2)}) collective-permute-start(bf16[512,1024]{1,0:T(8,128)(2,1)} %copy-done.19), channel_id=1, source_target_pairs={{0,16},{16,0},{1,17},{17,1},{2,18},{18,2},{3,19},{19,3},{4,20},{20... | collective-permute-start | bytes 3145736 | tf_op jit(solution)/shard_map/ppermute | solution.py:473
  414.8 68.8 %collective-permute-start.20 = (bf16[512,1024]{1,0:T(8,128)(2,1)}, bf16[512,1024]{1,0:T(8,128)(2,1)}, u32[]{:S(2)}, u32[]{:S(2)}) collective-permute-start(bf16[512,1024]{1,0:T(8,128)(2,1)} %copy-done.15), channel_id=1, source_target_pairs={{0,8},{8,0},{1,9},{9,1},{2,10},{10,2},{3,11},{11,3},{4,12},{12,4},... | collective-permute-start | bytes 3145736 | tf_op jit(solution)/shard_map/ppermute | solution.py:469
  435.6 18.0 %collective-permute-start.30 = (bf16[4,2,32,1024]{3,2,1,0:T(8,128)(2,1)}, bf16[4,2,32,1024]{3,2,1,0:T(8,128)(2,1)}, u32[]{:S(2)}, u32[]{:S(2)}) collective-permute-start(bf16[4,2,32,1024]{3,2,1,0:T(8,128)(2,1)} %dynamic-slice_bitcast_fusion.3), channel_id=1, source_target_pairs={{0,1},{1,0},{2,3},{3,2},{4,5},{5,4},{6,7},{7,6},{8,9},{9,8},{10,11... | collective-permute-start | bytes 1572872 | tf_op jit(solution)/shard_map/ppermute | solution.py:992
  435.6 26.5 %collective-permute-start.35 = (bf16[2,128,1024]{2,1,0:T(8,128)(2,1)}, bf16[2,128,1024]{2,1,0:T(8,128)(2,1)}, u32[]{:S(2)}, u32[]{:S(2)}) collective-permute-start(bf16[2,128,1024]{2,1,0:T(8,128)(2,1)} %dynamic-slice_bitcast_fusion.2), channel_id=1, source_target_pairs={{0,1},{1,0},{2,3},{3,2},{4,5},{5,4},{6,7},{7,6},{8,9},{9,8},{10,11... | collective-permute-start | bytes 1572872 | tf_op jit(solution)/shard_map/ppermute | solution.py:992
  442.0 31.6 %collective-permute-start.29 = (bf16[32,1536]{1,0:T(8,128)(2,1)S(1)}, bf16[32,1536]{1,0:T(8,128)(2,1)S(1)}, u32[]{:S(2)}, u32[]{:S(2)}) collective-permute-start(bf16[32,1536]{1,0:T(8,128)(2,1)S(1)} %dynamic-slice_bitcast_fusion.5), channel_id=1, source_target_pairs={{0,4},{4,0},{1,5},{5,1},{2,6},{6,2},{3,7},{7,3},{8,12},{12,8},{9,1... | collective-permute-start | bytes 294920 | tf_op jit(solution)/shard_map/ppermute | solution.py:465
  454.9 17.7 %collective-permute-start.31 = (bf16[4,1,32,1024]{3,2,1,0:T(8,128)(2,1)S(1)}, bf16[4,1,32,1024]{3,2,1,0:T(8,128)(2,1)S(1)}, u32[]{:S(2)}, u32[]{:S(2)}) collective-permute-start(bf16[4,1,32,1024]{3,2,1,0:T(8,128)(2,1)S(1)} %constant_dynamic-slice_fusion.2), channel_id=1, source_target_pairs={{0,2},{1,3},{2,0},{3,1},{4,6},{5,7},{6,4},{7,5},{8,10},{9,11},{10,... | collective-permute-start | bytes 786440 | tf_op jit(solution)/shard_map/ppermute | solution.py:992
  (75 other events, 703.6 us)
Sparse Core Ops, SparseCore 0:
  11.3 93.1 all-gather.4
  145.6 75.7 all-gather.6
  246.1 97.6 reduce-scatter.6
  353.3 65.8 reduce-scatter.4

commit v3 on v2

--- a/solution.py
+++ b/solution.py
@@ -604,6 +604,8 @@
     ).astype(BF)
     head_of = lax.broadcasted_iota(jnp.int32, (CHUNK, lanes), 1) // HEAD_DIM
     zero = jnp.zeros((CHUNK, lanes), BF)
+    head_down = lax.broadcasted_iota(jnp.int32, (lanes, CHUNK), 0) // HEAD_DIM
+    zero_down = jnp.zeros((lanes, CHUNK), BF)
 
     def flip(value):
         return nt(unit, value)
@@ -619,17 +621,21 @@
         return value.astype(F32) * wide(keep_ref, at) + mm(value, turn) * (sign * wide(sine_ref, at))
 
     def by_head(value):
-        return [jnp.where(head_of == h, value, zero) for h in range(heads)]
-
-    def prepare(j, carry):
-        at = chunk_at(j)
-        inner = pl.ds(pl.multiple_of((j % blocks) * CHUNK, CHUNK), CHUNK)
-        v_raw = v_ref[j // blocks, 0, inner, :]
-        k_rot = turned(k_ref[j // blocks, 0, inner, :], at, 1.0).astype(BF)
+        return jnp.concatenate([jnp.where(head_of == h, value, zero) for h in range(heads)])
+
+    def beside(value):
+        return jnp.concatenate([jnp.where(head_down == h, value, zero_down) for h in range(heads)], axis=1)
+
+    def part_of(h):
+        return pl.ds(h * CHUNK, CHUNK)
+
+    def prepare(b, carry):
+        at = pl.ds(pl.multiple_of(b * tok, tok), tok)
+        k_rot = turned(k_ref[b, 0], at, 1.0).astype(BF)
         k_scr[at, :] = k_rot
         kt_scr[:, at] = nt_t(k_rot)
-        v_scr[at, :] = v_raw
-        vt_scr[:, at] = nt_t(v_raw)
+        v_scr[at, :] = v_ref[b, 0]
+        vt_scr[:, at] = nt_t(v_ref[b, 0])
         return carry
 
     unit_lanes = (from_lane == to_lane).astype(F32).astype(BF)
@@ -639,7 +645,7 @@
 
     lowest = scalar_ref[s * blocks]
 
-    lax.fori_loop(lowest, chunks, prepare, 0)
+    lax.fori_loop(lowest // blocks, halo + 1, prepare, 0)
 
     def clear(j, carry):
         at = chunk_at(j)
@@ -649,88 +655,111 @@
 
     lax.fori_loop(0, chunks, clear, 0)
 
+    def both(body, start):
+        low = [scalar_ref[s * blocks + b] for b in range(blocks)]
+        high = [halo * blocks + b + 1 for b in range(blocks)]
+        carry = list(start)
+        edges = [(low[b], low[b + 1], b + 1) for b in range(blocks - 1)]
+        for lower, upper, n in edges + [(low[-1], high[0], blocks)]:
+
+            def step(j, now, n=n):
+                return tuple(body(b, j, c) for b, c in enumerate(now[:n])) + now[n:]
+
+            carry = list(lax.fori_loop(lower, upper, step, tuple(carry)))
+        for b in range(1, blocks):
+
+            def tail(j, now, b=b):
+                return now[:b] + tuple(body(k, j, now[k]) for k in range(b, blocks))
+
+            carry = list(lax.fori_loop(high[b - 1], high[b], tail, tuple(carry)))
+        return carry
+
+    q_down, q_beside, starts, inners, owns = [], [], [], [], []
     for b in range(blocks):
-        lower = scalar_ref[s * blocks + b]
-        upper = halo * blocks + b + 1
         inner = pl.ds(b * CHUNK, CHUNK)
         own = pl.ds((halo * blocks + b) * CHUNK, CHUNK)
         q_rot = turned(q_ref[0, inner, :], own, 1.0).astype(BF)
-        q_head = by_head((q_rot.astype(F32) * scale).astype(BF))
-        grad_out = do_ref[0, inner, :]
-        start = start_ref[0, :, inner] - base
+        q_scaled = (q_rot.astype(F32) * scale).astype(BF)
+        q_down.append(by_head(q_scaled))
+        q_beside.append(beside(nt_t(q_scaled)))
+        starts.append(start_ref[0, :, inner] - base)
+        inners.append(inner)
+        owns.append(own)
+
+    def scores(b, j, top):
+        at = chunk_at(j)
+        k_pos = j * CHUNK + row
         q_pos = (halo * blocks + b) * CHUNK + column
-
-        def scores(j, tops):
-            at = chunk_at(j)
-            k_pos = j * CHUNK + row
-            allowed = (k_pos >= start) & (k_pos <= q_pos)
-            keys = k_scr[at, :]
-            out = []
-            for h in range(heads):
-                value = jnp.where(allowed, nt(keys, q_head[h]), -1e30)
-                s_scr[h, at, :] = value
-                out.append(
-                    jnp.maximum(tops[h], jnp.max(value.reshape(CHUNK // 8, 8, CHUNK), axis=0))
-                )
-            return tuple(out)
-
-        tops = lax.fori_loop(
-            lower, upper, scores, (jnp.full((8, CHUNK), -1e30, F32),) * heads
+        allowed = (k_pos >= starts[b]) & (k_pos <= q_pos)
+        value = mm(k_scr[at, :], q_beside[b])
+        out = []
+        for h in range(heads):
+            masked = jnp.where(allowed, value[:, h * CHUNK : (h + 1) * CHUNK], -1e30)
+            s_scr[b, at, part_of(h)] = masked
+            out.append(jnp.max(masked.reshape(CHUNK // 8, 8, CHUNK), axis=0))
+        return jnp.maximum(top, jnp.concatenate(out, axis=1))
+
+    tops = both(scores, [jnp.full((8, heads * CHUNK), -1e30, F32)] * blocks)
+    tops = [jnp.max(top, axis=0, keepdims=True) for top in tops]
+    ot_scr[...] = jnp.zeros_like(ot_scr)
+    dqt_scr[...] = jnp.zeros_like(dqt_scr)
+
+    def weigh(b, j, total):
+        at = chunk_at(j)
+        value = jnp.exp(s_scr[b, at, :] - tops[b])
+        total = total + jnp.sum(value.reshape(CHUNK // 8, 8, heads * CHUNK), axis=0)
+        value = value.astype(BF)
+        p_scr[b, at, :] = value
+        for h in range(heads):
+            rows = pl.ds(h * HEAD_DIM, HEAD_DIM)
+            ot_scr[b, rows, :] += mm(vt_scr[rows, at], value[:, h * CHUNK : (h + 1) * CHUNK])
+        return total
+
+    totals = both(weigh, [jnp.zeros((8, heads * CHUNK), F32)] * blocks)
+    do_down, do_beside, deltas = [], [], []
+    for b in range(blocks):
+        total = 1.0 / jnp.sum(totals[b], axis=0, keepdims=True)
+        inverse = [total[:, h * CHUNK : (h + 1) * CHUNK] for h in range(heads)]
+        out_t = jnp.concatenate(
+            [ot_scr[b, h * HEAD_DIM : (h + 1) * HEAD_DIM, :] * inverse[h] for h in range(heads)]
         )
-        tops = [jnp.max(t, axis=0, keepdims=True) for t in tops]
-        ot_scr[...] = jnp.zeros_like(ot_scr)
-        dqt_scr[...] = jnp.zeros_like(dqt_scr)
-
-        def weigh(j, sums):
-            at = chunk_at(j)
-            out = []
-            for h in range(heads):
-                value = jnp.exp(s_scr[h, at, :] - tops[h])
-                out.append(sums[h] + jnp.sum(value.reshape(CHUNK // 8, 8, CHUNK), axis=0))
-                value = value.astype(BF)
-                p_scr[h, at, :] = value
-                rows = pl.ds(h * HEAD_DIM, HEAD_DIM)
-                ot_scr[rows, :] += mm(vt_scr[rows, at], value)
-            return tuple(out)
-
-        sums = lax.fori_loop(lower, upper, weigh, (jnp.zeros((8, CHUNK), F32),) * heads)
-        inverse = [1.0 / jnp.sum(t, axis=0, keepdims=True) for t in sums]
-        out_t = jnp.concatenate(
-            [ot_scr[h * HEAD_DIM : (h + 1) * HEAD_DIM, :] * inverse[h] for h in range(heads)]
-        )
-        att_ref[0, inner, :] = flip(out_t.astype(BF)).astype(BF)
-        scaled = grad_out.astype(F32)
+        att_ref[0, inners[b], :] = flip(out_t.astype(BF)).astype(BF)
+        scaled = do_ref[0, inners[b], :].astype(F32)
         spread = jnp.zeros((CHUNK, lanes), F32)
         for h in range(heads):
             down = jnp.transpose(jnp.broadcast_to(inverse[h], (LANES, CHUNK)))
             down = jnp.concatenate([down] * (lanes // LANES), axis=1)
             spread = jnp.where(head_of == h, down, spread)
         scaled = (scaled * spread).astype(BF)
-        prod = out_t * nt(unit_lanes, scaled)
-        delta = [
-            jnp.sum(prod[h * HEAD_DIM : (h + 1) * HEAD_DIM], axis=0, keepdims=True)
-            for h in range(heads)
-        ]
-        do_head = by_head(scaled)
-
-        def backward(j, carry):
-            at = chunk_at(j)
-            values = v_scr[at, :]
-            dk, dv = dk_scr[at, :], dv_scr[at, :]
-            for h in range(heads):
-                prob = p_scr[h, at, :]
-                ds = (prob.astype(F32) * (nt(values, do_head[h]) - delta[h])).astype(BF)
-                dv += mm(prob, do_head[h])
-                dk += mm(ds, q_head[h])
-                rows = pl.ds(h * HEAD_DIM, HEAD_DIM)
-                dqt_scr[rows, :] += mm(kt_scr[rows, at], ds)
-            dk_scr[at, :] = dk
-            dv_scr[at, :] = dv
-            return carry
-
-        lax.fori_loop(lower, upper, backward, 0)
-        dq = (flip((dqt_scr[...] * scale).astype(BF))).astype(BF)
-        dq_ref[0, inner, :] = turned(dq, own, -1.0).astype(BF)
+        scaled_t = nt(unit_lanes, scaled)
+        prod = out_t * scaled_t
+        do_down.append(by_head(scaled))
+        do_beside.append(beside(scaled_t.astype(BF)))
+        deltas.append(
+            jnp.concatenate(
+                [
+                    jnp.sum(prod[h * HEAD_DIM : (h + 1) * HEAD_DIM], axis=0, keepdims=True)
+                    for h in range(heads)
+                ],
+                axis=1,
+            )
+        )
+
+    def backward(b, j, carry):
+        at = chunk_at(j)
+        prob = p_scr[b, at, :]
+        ds = (prob.astype(F32) * (mm(v_scr[at, :], do_beside[b]) - deltas[b])).astype(BF)
+        dv_scr[at, :] += mm(prob, do_down[b])
+        dk_scr[at, :] += mm(ds, q_down[b])
+        for h in range(heads):
+            rows = pl.ds(h * HEAD_DIM, HEAD_DIM)
+            dqt_scr[b, rows, :] += mm(kt_scr[rows, at], ds[:, h * CHUNK : (h + 1) * CHUNK])
+        return carry
+
+    both(backward, [0] * blocks)
+    for b in range(blocks):
+        dq = flip((dqt_scr[b] * scale).astype(BF)).astype(BF)
+        dq_ref[0, inners[b], :] = turned(dq, owns[b], -1.0).astype(BF)
 
     for j in range(chunks):
         at = pl.ds(j * CHUNK, CHUNK)
@@ -772,16 +801,16 @@
                 pl.BlockSpec((spans, 1, tok, width), lambda s, p, _: (0, s, 0, 0)),
             ],
             scratch_shapes=[
-                pltpu.VMEM((heads, keys, CHUNK), F32),
-                pltpu.VMEM((heads, keys, CHUNK), BF),
+                pltpu.VMEM((tok // CHUNK, keys, heads * CHUNK), F32),
+                pltpu.VMEM((tok // CHUNK, keys, heads * CHUNK), BF),
                 pltpu.VMEM((keys, lanes), BF),
                 pltpu.VMEM((keys, lanes), BF),
                 pltpu.VMEM((lanes, keys), BF),
                 pltpu.VMEM((lanes, keys), BF),
                 pltpu.VMEM((keys, lanes), F32),
                 pltpu.VMEM((keys, lanes), F32),
-                pltpu.VMEM((lanes, CHUNK), F32),
-                pltpu.VMEM((lanes, CHUNK), F32),
+                pltpu.VMEM((tok // CHUNK, lanes, CHUNK), F32),
+                pltpu.VMEM((tok // CHUNK, lanes, CHUNK), F32),
             ],
         ),
         out_shape=[
@@ -985,13 +1014,15 @@
 
 
 def z_scatter(parts, axis, zi, nz):
+    steps = []
     for k, pairs in enumerate(z_pairs(nz)):
         shape = parts.shape
         blocks = parts.reshape(shape[:axis] + (shape[axis] // 2, 2) + shape[axis + 1 :])
         bit = (zi >> k) & 1
         come = lax.ppermute(pick(blocks, 1 - bit, axis + 1), "z", pairs)
         parts = summed(pick(blocks, bit, axis + 1), come)
-    return lax.squeeze(parts, (axis,))
+        steps.append(parts)
+    return steps[:-1] + [lax.squeeze(parts, (axis,))]
 
 
 def normalise(tokens):
@@ -1183,6 +1214,9 @@
 
     s_in = summed(pick(g_in, yi, 0), held(in_y, br_send)).reshape(4, nz, rows, units)
     dn_x = held(dn_x, s_in)
+    s_in_steps = z_scatter(s_in, 1, zi, nz)
+    s_in = s_in_steps[-1].reshape(2, 2, rows, units)
+    in_x = over_x(pick(s_in, 1 - xi, 0))
     dn_parts = [dn_ff[0, 0], dn_att[0], dn_come[0]]
     br_parts = [branch[0, 0], branch_att[0], br_come[0]]
 
@@ -1197,9 +1231,8 @@
         - xhat * jnp.mean(scaled * xhat, axis=1, keepdims=True)
     )
     out_y, br_x = held(out_y, grad_input), held(br_x, grad_input)
-    s_in = z_scatter(s_in, 1, zi, nz)
     s_out = summed(pick(g_out, yi, 0), out_y).reshape(nz, out_rows, width)
-    grad_w_out = z_scatter(s_out, 0, zi, nz).astype(F32)
+    grad_w_out = z_scatter(s_out, 0, zi, nz)[-1].astype(F32)
     hidden_out = (
         x + sum(v.astype(F32) for v in (*br_parts, br_x)) + dense_bias + out_bias
     ).astype(BF)
@@ -1221,9 +1254,10 @@
         ),
     ]
     small_sizes = [g.shape[0] for g in small_grads]
-    total = jnp.concatenate(small_grads)
-    for move in (other_core, over_x, over_y):
-        total = total + move(total)
+    total = held(jnp.concatenate(small_grads), s_in_steps[0])
+    total = total + other_core(total)
+    total = held(total + over_x(total), s_in)
+    total = held(total + over_y(total), in_x)
     for pairs in z_pairs(nz):
         total = total + lax.ppermute(total, "z", pairs)
     device = (chip * 2 + core) * nz + zi
@@ -1241,8 +1275,7 @@
     grad_w_dense = s_att[:, :, 3 * part :].transpose(1, 0, 2).reshape(rows, width).astype(F32)
     s_qkv = home_core(s_att[:, :, : 3 * part])
     grad_w_qkv = s_qkv.reshape(2, rows, 3, 4, -1).transpose(1, 2, 3, 0, 4).reshape(rows, -1)
-    s_in = s_in.reshape(2, 2, rows, units)
-    s_in = home_core(by_place(xi, pick(s_in, xi, 0), over_x(pick(s_in, 1 - xi, 0))))
+    s_in = home_core(by_place(xi, pick(s_in, xi, 0), in_x))
     grad_w_in = s_in.reshape(2, 2, rows, 2, -1).transpose(2, 3, 1, 0, 4).reshape(rows, -1)
     return (
         hidden_out[None],

time: 503 us -> 465 us (0.924)
  waiting for transfers between devices: 183 us -> 119 us
  starting transfers between devices: 45.3 us -> 78.7 us
  Pallas kernels: 116 us -> 105 us
    ppermute x1, waiting for transfers between devices: 31.5 us -> 2.77 us  [local_plane(): dn_back = lax.ppermute(passed, 'z', down)]
    ppermute x4, waiting for transfers between devices: 27.8 us -> 0.45 us  [z_scatter(): come = lax.ppermute(pick(blocks, 1 - bit, axis + 1), 'z', pairs)]
    ppermute x7, starting transfers between devices: 7.3 us -> 30.8 us  [over_x(): return lax.ppermute(value, 'x', SWAP)]
    ppermute x4, starting transfers between devices: 2.25 us -> 25.3 us  [z_scatter(): come = lax.ppermute(pick(blocks, 1 - bit, axis + 1), 'z', pairs)]
    pallas_call x1, Pallas kernels: 39.7 us -> 27.6 us  [attention(): pl.pallas_call(functools.partial(attention_kernel, halo, tok, heads), gri...]
    ppermute x1, waiting for transfers between devices: 20.2 us -> 8.98 us  [local_plane(): come = held(lax.ppermute(passed, 'z', down), pre_sum)]
    reduce_scatter x1, waiting for transfers between devices: 0.01 us -> 11 us  [local_plane(): s_att = lax.psum_scatter(s_att, 'z', scatter_dimension=0, tiled=False)]
    ppermute x2, starting transfers between devices: 9.68 us -> 0.07 us  [local_plane(): total = total + lax.ppermute(total, 'z', pairs)]
  transfers between devices with their start and end apart: 41 -> 41, of which waited for: 17 -> 14; matrix products, arithmetic and copies ran while one was open for 20% -> 22% of each run, Pallas kernels for 23% -> 23%
where the time goes in v3:
time: 465 us; the launch traced here: 457 us
  waiting for transfers between devices  119 us (26%)
  Pallas kernels  105 us (23%)
  starting transfers between devices  78.7 us (17%)
  local copies, waits for them, and re-layouts  58 us (12%)
  other arithmetic  50 us (11%)
  matrix products  31.8 us (7%)
  between operations  15.6 us (3%)
    ppermute x7, waiting for transfers between devices, over_x(): return lax.ppermute(value, 'x', SWAP)  44.2 us
    unnamed x127, local copies, waits for them, and re-layouts  35.2 us
    ppermute x7, starting transfers between devices, over_x(): return lax.ppermute(value, 'x', SWAP)  30.8 us
    pallas_call x1, Pallas kernels, attention(): pl.pallas_call(functools.partial(attention_kernel, halo, tok, heads), gri...  27.6 us
    ppermute x4, starting transfers between devices, z_scatter(): come = lax.ppermute(pick(blocks, 1 - bit, axis + 1), 'z', pairs)  25.3 us
    pallas_call x6, Pallas kernels, matmul(): pl.pallas_call(body, grid=(rows // block,), in_specs=[left_spec, whole] +...  24.9 us
    ppermute x2, waiting for transfers between devices, local_plane(): before.append(lax.ppermute(before[-1], 'z', up))  23.5 us
    convert_element_type x12, other arithmetic, summed(): return sum((v.astype(F32) for v in values)).astype(BF)  20.1 us
  transfers between devices with their start and end apart: 41, of which 14 were waited for; matrix products, arithmetic and copies ran while one was open for 22% of the time, Pallas kernels for 23%

profile of v3, /device:TPU:0, one launch (start us, length us, event | category | flops | bytes accessed | tf_op | source)
XLA Modules:
  0.0 457.3 jit_solution(5215552584105352865)
XLA Ops:
  22.7 4.5 collective-permute-start.12
  28.0 42.7 %collective-permute-done.4 = bf16[2,352]{1,0:T(2,128)(2,1)S(1)} collective-permute-done((bf16[2,352]{1,0:T(2,128)(2,1)S(1)}, bf16[2,352]{1,0:T(2,128)(2,1)S(1)}, u32[]{:S(2)}, u32[]{:S(2)}) %collective-permute-start.4) | collective-permute-done | bytes 1440 | tf_op jit(solution)/shard_map/ppermute | solution.py:469
  93.3 23.5 %collective-permute-done.13 = bf16[512,1024]{1,0:T(8,128)(2,1)} collective-permute-done((bf16[512,1024]{1,0:T(8,128)(2,1)}, bf16[512,1024]{1,0:T(8,128)(2,1)}, u32[]{:S(2)}, u32[]{:S(2)}) %collective-permute-start.13) | collective-permute-done | bytes 1048608 | tf_op jit(solution)/shard_map/ppermute | solution.py:1099
  124.0 6.2 %layer_norm.2 = (bf16[3072,1024]{1,0:T(8,128)(2,1)S(1)}, bf16[2048,1024]{1,0:T(8,128)(2,1)S(1)}) custom-call(bf16[2,512,1024]{2,1,0:T(8,128)(2,1)} %constant_dynamic-update-slice_fusion.refs_0_, bf16[2,512,1024]{2,1,0:T(8,128)(2,1)} %collective-permute-done.refs_1_, bf16[2,512,1024]{2,1,0:T(8,128)(2,1)S(1)} %collective-permute-done.1.refs_2_, ...), custom_call_target="tpu_custom_call" | custom-call | bytes 1048576 | tf_op jit(solution)/shard_map/layer_norm/pallas_call | solution.py:960
  130.2 8.4 %layer_norm.3.n_ref = bf16[3072,1024]{1,0:T(8,128)(2,1)S(1)} custom-call(bf16[1,512,1024]{2,1,0:T(8,128)(2,1)} %bitcast.35.refs_0_, bf16[1,512,1024]{2,1,0:T(8,128)(2,1)} %bitcast.36.refs_1_, bf16[1,512,1024]{2,1,0:T(8,128)(2,1)} %bitcast.37.refs_2_, bf16[1,512,1024]{2,1,0:T(8,128)(2,1)} %bitcast.38.refs_3_, ...), custom_call_target="tpu_custom_call", output_to_operand_aliasing={{}: (6, {})} | custom-call | bytes 1048576 | tf_op jit(solution)/shard_map/layer_norm/pallas_call | solution.py:960
  157.5 8.6 %add_convert_fusion = bf16[3072,1024]{1,0:T(8,128)(2,1)} fusion(f32[1024]{0:T(1024)S(1)} %bitcast.331, bf16[3072,1024]{1,0:T(8,128)(2,1)S(1)} %bitcast.271, bf16[1024,1024]{1,0:T(8,128)(2,1)S(1)} %get-tuple-element.30), kind=kOutput, calls=%fused_computation.1 | convolution fusion | flops 6448742400 | bytes 14684160 | tf_op jit(solution)/shard_map/dot_general | solution.py:461
  166.1 27.6 %attention.1 = (bf16[2,512,512]{2,1,0:T(8,128)(2,1)S(1)}, bf16[2,512,512]{2,1,0:T(8,128)(2,1)S(1)}, bf16[3,2,512,1024]{3,2,1,0:T(8,128)(2,1)}) custom-call(s32[5]{0:T(128)S(1)} %pad_add_fusion.1.scalar_ref, bf16[2,512,512]{2,1,0:T(8,128)(2,1)S(1)} %bitcast.287, bf16[3,2,512,1024]{3,2,1,0:T(8,128)(2,1)} %bitcast.297, bf16[3,2,512,1024]{3,2,1,0:T(8,128)(2,1)} %bitcast.298, ...), custom_call_target="tpu_custom_call" | custom-call | bytes 1048576 | tf_op jit(solution)/shard_map/attention/pallas_call | solution.py:783
  193.7 10.2 %convolution_convert_fusion = bf16[3072,1024]{1,0:T(8,128)(2,1)S(1)} fusion(bf16[3072,1024]{1,0:T(8,128)(2,1)} %bitcast.295, bf16[1024,1024]{1,0:T(8,128)(2,1)S(1)} %get-tuple-element.30), kind=kOutput, calls=%fused_computation.4 | convolution fusion | flops 6445596672 | bytes 14680064 | tf_op jit(solution)/shard_map/dot_general | solution.py:477
  208.0 14.5 %attention_weight_grads.1.refs_1_ = bf16[4,4,2,32,2048]{4,3,2,1,0:T(8,128)(2,1)} custom-call(bf16[3072,1024]{1,0:T(8,128)(2,1)} %copy-done.5, bf16[1024,512]{1,0:T(8,128)(2,1)S(1)} %bitcast.283, bf16[1024,512]{1,0:T(8,128)(2,1)S(1)} %bitcast.276, bf16[3072,1024]{1,0:T(8,128)(2,1)} %bitcast.296, bf16[2048,1024]{1,0:T(8,128)(2,1)} %pad_maximum_fusion.left_ref.g_ref.right_ref), custom_call_target="tpu_custom_call" | custom-call | bytes 1048576 | tf_op jit(solution)/shard_map/attention_weight_grads/pallas_call | solution.py:994
  233.9 3.9 add_convert_fusion.3
  240.5 17.6 %feed_forward.1 = (bf16[2048,1024]{1,0:T(8,128)(2,1)}, bf16[2048,1024]{1,0:T(8,128)(2,1)}, f32[8,1024]{1,0:T(8,128)S(1)}) custom-call(bf16[2048,1024]{1,0:T(8,128)(2,1)} %copy-done.3, bf16[2048,1024]{1,0:T(8,128)(2,1)} %pad_maximum_fusion.left_ref.g_ref.right_ref, bf16[1024,1024]{1,0:T(8,128)(2,1)S(1)} %get-tuple-element.26.wi_ref, f32[1,1024]{1,0:T(1,128)S(1)} %bitcast.291, ...), custom_call_target="tpu_custom_call" | custom-call | bytes 1048576 | tf_op jit(solution)/shard_map/feed_forward/pallas_call | solution.py:567
  258.1 9.0 %collective-permute-done.17.refs_0_ = bf16[512,1024]{1,0:T(8,128)(2,1)} collective-permute-done((bf16[512,1024]{1,0:T(8,128)(2,1)}, bf16[512,1024]{1,0:T(8,128)(2,1)}, u32[]{:S(2)}, u32[]{:S(2)}) %collective-permute-start.17) | collective-permute-done | bytes 1048608 | tf_op jit(solution)/shard_map/ppermute | solution.py:1190
  268.7 8.0 %matmul_tn.2 = bf16[1024,1024]{1,0:T(8,128)(2,1)S(1)} custom-call(bf16[2048,1024]{1,0:T(8,128)(2,1)} %copy-done.3, bf16[2048,1024]{1,0:T(8,128)(2,1)} %get-tuple-element.36.right_ref, bf16[512,1024]{1,0:T(8,128)(2,1)S(1)} %fusion.23.rest_0_), custom_call_target="tpu_custom_call" | custom-call | bytes 1048576 | tf_op jit(solution)/shard_map/matmul_tn/pallas_call | solution.py:504
  276.8 8.2 %add_convert_fusion.2 = bf16[2048,1024]{1,0:T(8,128)(2,1)S(1)} fusion(f32[1024]{0:T(1024)S(1)} %bitcast.292, bf16[2048,1024]{1,0:T(8,128)(2,1)} %get-tuple-element.36.right_ref, bf16[1024,1024]{1,0:T(8,128)(2,1)S(1)} %get-tuple-element.26.wi_ref), kind=kOutput, calls=%fused_computation.3 | convolution fusion | flops 4299161600 | bytes 10489856 | tf_op jit(solution)/shard_map/dot_general | solution.py:477
  291.6 7.7 %matmul_tn.3 = bf16[1024,1024]{1,0:T(8,128)(2,1)S(1)} custom-call(bf16[2048,1024]{1,0:T(8,128)(2,1)} %get-tuple-element.35.left_ref, bf16[2048,1024]{1,0:T(8,128)(2,1)} %pad_maximum_fusion.left_ref.g_ref.right_ref, bf16[2,512,1024]{2,1,0:T(8,128)(2,1)} %pad_maximum_fusion.1.rest_0_), custom_call_target="tpu_custom_call" | custom-call | bytes 1048576 | tf_op jit(solution)/shard_map/matmul_tn/pallas_call | solution.py:504
  308.8 4.9 %add_convert_fusion.1 = bf16[2048,1024]{1,0:T(8,128)(2,1)S(1)} fusion(f32[1024]{0:T(1024)S(1)} %bitcast.293, bf16[2048,1024]{1,0:T(8,128)(2,1)S(1)} %copy-done.40, bf16[1024,1024]{1,0:T(8,128)(2,1)S(1)} %copy-done.28), kind=kOutput, calls=%fused_computation.2 | convolution fusion | flops 4299161600 | bytes 10489856 | tf_op jit(solution)/shard_map/dot_general | solution.py:461
  325.5 6.9 %collective-permute-start.21 = (bf16[512,1024]{1,0:T(8,128)(2,1)S(1)}, bf16[512,1024]{1,0:T(8,128)(2,1)S(1)}, u32[]{:S(2)}, u32[]{:S(2)}) collective-permute-start(bf16[512,1024]{1,0:T(8,128)(2,1)S(1)} %fusion.21.refs_2_.rest_0_), channel_id=1, source_target_pairs={{0,8},{8,0},{1,9},{9,1},{2,10},{10,2},{3,11},{11,3},{4,12},{12,4},... | collective-permute-start | bytes 3145736 | tf_op jit(solution)/shard_map/ppermute | solution.py:469
  336.0 8.7 %collective-permute-done.22.refs_0_ = bf16[512,1024]{1,0:T(8,128)(2,1)S(1)} collective-permute-done((bf16[512,1024]{1,0:T(8,128)(2,1)}, bf16[512,1024]{1,0:T(8,128)(2,1)S(1)}, u32[]{:S(2)}, u32[]{:S(2)}) %collective-permute-start.22) | collective-permute-done | bytes 1048608 | tf_op jit(solution)/shard_map/ppermute | solution.py:473
  348.4 12.7 %collective-permute-start.24 = (bf16[4,2,32,1024]{3,2,1,0:T(8,128)(2,1)}, bf16[4,2,32,1024]{3,2,1,0:T(8,128)(2,1)}, u32[]{:S(2)}, u32[]{:S(2)}) collective-permute-start(bf16[4,2,32,1024]{3,2,1,0:T(8,128)(2,1)} %dynamic-slice_bitcast_fusion.3), channel_id=1, source_target_pairs={{0,1},{1,0},{2,3},{3,2},{4,5},{5,4},{6,7},{7,6},{8,9},{9,8},{10,11... | collective-permute-start | bytes 1572872 | tf_op jit(solution)/shard_map/ppermute | solution.py:1022
  372.9 10.5 %collective-permute-start.35 = (bf16[2,128,1024]{2,1,0:T(8,128)(2,1)}, bf16[2,128,1024]{2,1,0:T(8,128)(2,1)}, u32[]{:S(2)}, u32[]{:S(2)}) collective-permute-start(bf16[2,128,1024]{2,1,0:T(8,128)(2,1)} %dynamic-slice_bitcast_fusion.2), channel_id=1, source_target_pairs={{0,1},{1,0},{2,3},{3,2},{4,5},{5,4},{6,7},{7,6},{8,9},{9,8},{10,11... | collective-permute-start | bytes 1572872 | tf_op jit(solution)/shard_map/ppermute | solution.py:1022
  383.5 11.0 %reduce-scatter.5.cloned.1.call-done = bf16[1,2,32,2048]{3,2,1,0:T(8,128)(2,1)} async-done(((bf16[4,2,32,2048]{3,2,1,0:T(8,128)(2,1)}), bf16[1,2,32,2048]{3,2,1,0:T(8,128)(2,1)}) %reduce-scatter.5.cloned.1.call-update) | async-done | bytes 262160 | tf_op jit(solution)/shard_map/reduce_scatter | solution.py:1182
  402.2 17.1 %collective-permute-start.26 = (f32[10240]{0:T(1024)S(1)}, f32[10240]{0:T(1024)S(1)}, u32[]{:S(2)}, u32[]{:S(2)}) collective-permute-start(f32[10240]{0:T(1024)S(1)} %add.344), channel_id=1, source_target_pairs={{0,8},{8,0},{1,9},{9,1},{2,10},{10,2},{3,11},{11,3},{4,12},{12,4},... | collective-permute-start | bytes 122888 | tf_op jit(solution)/shard_map/ppermute | solution.py:469
  428.5 6.6 %collective-permute-done.30 = f32[10240]{0:T(1024)S(1)} collective-permute-done((f32[10240]{0:T(1024)S(1)}, f32[10240]{0:T(1024)S(1)}, u32[]{:S(2)}, u32[]{:S(2)}) %collective-permute-start.30) | collective-permute-done | bytes 40992 | tf_op jit(solution)/shard_map/ppermute | solution.py:1262
  445.8 4.0 fusion.25
  (354 shorter events, 158.8 us)
Async XLA Ops:
  7.2 109.8 %all-gather.5.cloned.1.call-start = ((), (), s32[]{:S(2)}) async-start(), calls=%async_computation.3 | async-start | bytes 4456448 | tf_op jit(solution)/shard_map/all_gather | solution.py:1081
  9.1 228.7 %all-gather.7.cloned.1.call-start = ((), (), s32[]{:S(2)}) async-start(), calls=%async_computation.4 | async-start | bytes 4718592 | tf_op jit(solution)/shard_map/all_gather | solution.py:1134
  12.5 75.5 %collective-permute-start.1 = (bf16[2,512,1024]{2,1,0:T(8,128)(2,1)}, bf16[2,512,1024]{2,1,0:T(8,128)(2,1)S(1)}, u32[]{:S(2)}, u32[]{:S(2)}) collective-permute-start(bf16[2,512,1024]{2,1,0:T(8,128)(2,1)} %constant_dynamic-update-slice_fusion.refs_0_), channel_id=1, source_target_pairs={{0,8},{8,0},{1,9},{9,1},{2,10},{10,2},{3,11},{11,3},{4,12},{12,4},... | collective-permute-start | bytes 6291464 | tf_op jit(solution)/shard_map/ppermute | solution.py:469
  15.5 107.2 %collective-permute-start = (bf16[2,512,1024]{2,1,0:T(8,128)(2,1)}, bf16[2,512,1024]{2,1,0:T(8,128)(2,1)}, u32[]{:S(2)}, u32[]{:S(2)}) collective-permute-start(bf16[2,512,1024]{2,1,0:T(8,128)(2,1)} %constant_dynamic-update-slice_fusion.refs_0_), channel_id=1, source_target_pairs={{0,4},{4,0},{1,5},{5,1},{2,6},{6,2},{3,7},{7,3},{8,12},{12,8},{9,1... | collective-permute-start | bytes 6291464 | tf_op jit(solution)/shard_map/ppermute | solution.py:465
  18.0 70.2 %collective-permute-start.8 = (bf16[32,2048]{1,0:T(8,128)(2,1)S(1)}, bf16[32,2048]{1,0:T(8,128)(2,1)S(1)}, u32[]{:S(2)}, u32[]{:S(2)}) collective-permute-start(bf16[32,2048]{1,0:T(8,128)(2,1)S(1)} %bitcast.323), channel_id=1, source_target_pairs={{0,4},{4,0},{1,5},{5,1},{2,6},{6,2},{3,7},{7,3},{8,12},{12,8},{9,1... | collective-permute-start | bytes 393224 | tf_op jit(solution)/shard_map/ppermute | solution.py:465
  22.7 61.7 %collective-permute-start.12 = (bf16[512,1024]{1,0:T(8,128)(2,1)}, bf16[512,1024]{1,0:T(8,128)(2,1)}, u32[]{:S(2)}, u32[]{:S(2)}) collective-permute-start(bf16[512,1024]{1,0:T(8,128)(2,1)} %bitcast.294), channel_id=1, source_target_pairs={{0,1},{1,2},{2,3},{4,5},{5,6},{6,7},{8,9},{9,10},{10,11},{12,13},{... | collective-permute-start | bytes 3145736 | tf_op jit(solution)/shard_map/ppermute | solution.py:1099
  27.3 43.4 %collective-permute-start.4 = (bf16[2,352]{1,0:T(2,128)(2,1)S(1)}, bf16[2,352]{1,0:T(2,128)(2,1)S(1)}, u32[]{:S(2)}, u32[]{:S(2)}) collective-permute-start(bf16[2,352]{1,0:T(2,128)(2,1)S(1)} %maximum_bitcast_fusion.1), channel_id=1, source_target_pairs={{0,8},{8,0},{1,9},{9,1},{2,10},{10,2},{3,11},{11,3},{4,12},{12,4},... | collective-permute-start | bytes 4232 | tf_op jit(solution)/shard_map/ppermute | solution.py:469
  84.4 32.4 %collective-permute-start.13 = (bf16[512,1024]{1,0:T(8,128)(2,1)}, bf16[512,1024]{1,0:T(8,128)(2,1)}, u32[]{:S(2)}, u32[]{:S(2)}) collective-permute-start(bf16[512,1024]{1,0:T(8,128)(2,1)} %collective-permute-done.12), channel_id=1, source_target_pairs={{0,1},{1,2},{2,3},{4,5},{5,6},{6,7},{8,9},{9,10},{10,11},{12,13},{... | collective-permute-start | bytes 3145736 | tf_op jit(solution)/shard_map/ppermute | solution.py:1099
  88.0 36.0 %collective-permute-start.2 = (bf16[2,512,1024]{2,1,0:T(8,128)(2,1)S(1)}, bf16[2,512,1024]{2,1,0:T(8,128)(2,1)}, u32[]{:S(2)}, u32[]{:S(2)}) collective-permute-start(bf16[2,512,1024]{2,1,0:T(8,128)(2,1)S(1)} %collective-permute-done.1.refs_2_), channel_id=1, source_target_pairs={{0,4},{4,0},{1,5},{5,1},{2,6},{6,2},{3,7},{7,3},{8,12},{12,8},{9,1... | collective-permute-start | bytes 6291464 | tf_op jit(solution)/shard_map/ppermute | solution.py:465
  91.0 30.2 %collective-permute-start.9 = (bf16[64,1024]{1,0:T(8,128)(2,1)}, bf16[64,1024]{1,0:T(8,128)(2,1)S(1)}, u32[]{:S(2)}, u32[]{:S(2)}) collective-permute-start(bf16[64,1024]{1,0:T(8,128)(2,1)} %bitcast.142), channel_id=1, source_target_pairs={{0,8},{8,0},{1,9},{9,1},{2,10},{10,2},{3,11},{11,3},{4,12},{12,4},... | collective-permute-start | bytes 393224 | tf_op jit(solution)/shard_map/ppermute | solution.py:469
  93.1 37.1 %collective-permute-start.15 = (bf16[512,1024]{1,0:T(8,128)(2,1)}, bf16[512,1024]{1,0:T(8,128)(2,1)}, u32[]{:S(2)}, u32[]{:S(2)}) collective-permute-start(bf16[512,1024]{1,0:T(8,128)(2,1)} %collective-permute-done.12), channel_id=1, source_target_pairs={{0,4},{4,0},{1,5},{5,1},{2,6},{6,2},{3,7},{7,3},{8,12},{12,8},{9,1... | collective-permute-start | bytes 3145736 | tf_op jit(solution)/shard_map/ppermute | solution.py:465
  121.2 24.8 %collective-permute-start.11 = (bf16[16,32,1536]{2,1,0:T(8,128)(2,1)}, bf16[16,32,1536]{2,1,0:T(8,128)(2,1)}, u32[]{:S(2)}, u32[]{:S(2)}) collective-permute-start(bf16[16,32,1536]{2,1,0:T(8,128)(2,1)} %away_columns.1), channel_id=1, source_target_pairs={{0,4},{4,0},{1,5},{5,1},{2,6},{6,2},{3,7},{7,3},{8,12},{12,8},{9,1... | collective-permute-start | bytes 4718600 | tf_op jit(solution)/shard_map/ppermute | solution.py:465
  145.5 187.5 %reduce-scatter.7.cloned.1.call-start = ((), (), s32[]{:S(2)}) async-start(), calls=%async_computation.5 | async-start | bytes 5242880
  229.6 37.5 %collective-permute-start.17 = (bf16[512,1024]{1,0:T(8,128)(2,1)}, bf16[512,1024]{1,0:T(8,128)(2,1)}, u32[]{:S(2)}, u32[]{:S(2)}) collective-permute-start(bf16[512,1024]{1,0:T(8,128)(2,1)} %slice_bitcast_fusion.15), channel_id=1, source_target_pairs={{1,0},{2,1},{3,2},{5,4},{6,5},{7,6},{9,8},{10,9},{11,10},{13,12},{... | collective-permute-start | bytes 3145736 | tf_op jit(solution)/shard_map/ppermute | solution.py:1190
  233.8 160.7 %reduce-scatter.5.cloned.1.call-start = ((), (), s32[]{:S(2)}) async-start(), calls=%async_computation.2 | async-start | bytes 1310720 | tf_op jit(solution)/shard_map/reduce_scatter | solution.py:1182
  318.5 26.2 %collective-permute-start.22 = (bf16[512,1024]{1,0:T(8,128)(2,1)}, bf16[512,1024]{1,0:T(8,128)(2,1)S(1)}, u32[]{:S(2)}, u32[]{:S(2)}) collective-permute-start(bf16[512,1024]{1,0:T(8,128)(2,1)} %copy-done.18), channel_id=1, source_target_pairs={{0,16},{16,0},{1,17},{17,1},{2,18},{18,2},{3,19},{19,3},{4,20},{20... | collective-permute-start | bytes 3145736 | tf_op jit(solution)/shard_map/ppermute | solution.py:473
  324.2 39.8 %collective-permute-start.23 = (bf16[512,1024]{1,0:T(8,128)(2,1)}, bf16[512,1024]{1,0:T(8,128)(2,1)}, u32[]{:S(2)}, u32[]{:S(2)}) collective-permute-start(bf16[512,1024]{1,0:T(8,128)(2,1)} %copy-done.23), channel_id=1, source_target_pairs={{1,0},{2,1},{3,2},{5,4},{6,5},{7,6},{9,8},{10,9},{11,10},{13,12},{... | collective-permute-start | bytes 3145736 | tf_op jit(solution)/shard_map/ppermute | solution.py:1192
  325.5 35.7 %collective-permute-start.21 = (bf16[512,1024]{1,0:T(8,128)(2,1)S(1)}, bf16[512,1024]{1,0:T(8,128)(2,1)S(1)}, u32[]{:S(2)}, u32[]{:S(2)}) collective-permute-start(bf16[512,1024]{1,0:T(8,128)(2,1)S(1)} %fusion.21.refs_2_.rest_0_), channel_id=1, source_target_pairs={{0,8},{8,0},{1,9},{9,1},{2,10},{10,2},{3,11},{11,3},{4,12},{12,4},... | collective-permute-start | bytes 3145736 | tf_op jit(solution)/shard_map/ppermute | solution.py:469
  332.5 35.5 %collective-permute-start.34 = (bf16[512,1024]{1,0:T(8,128)(2,1)}, bf16[512,1024]{1,0:T(8,128)(2,1)}, u32[]{:S(2)}, u32[]{:S(2)}) collective-permute-start(bf16[512,1024]{1,0:T(8,128)(2,1)} %copy-done.19), channel_id=1, source_target_pairs={{0,16},{16,0},{1,17},{17,1},{2,18},{18,2},{3,19},{19,3},{4,20},{20... | collective-permute-start | bytes 3145736 | tf_op jit(solution)/shard_map/ppermute | solution.py:473
  336.0 108.0 %collective-permute-start.20 = (bf16[512,1024]{1,0:T(8,128)(2,1)}, bf16[512,1024]{1,0:T(8,128)(2,1)}, u32[]{:S(2)}, u32[]{:S(2)}) collective-permute-start(bf16[512,1024]{1,0:T(8,128)(2,1)} %fusion.18.refs_1_), channel_id=1, source_target_pairs={{0,8},{8,0},{1,9},{9,1},{2,10},{10,2},{3,11},{11,3},{4,12},{12,4},... | collective-permute-start | bytes 3145736 | tf_op jit(solution)/shard_map/ppermute | solution.py:469
  348.4 47.1 %collective-permute-start.24 = (bf16[4,2,32,1024]{3,2,1,0:T(8,128)(2,1)}, bf16[4,2,32,1024]{3,2,1,0:T(8,128)(2,1)}, u32[]{:S(2)}, u32[]{:S(2)}) collective-permute-start(bf16[4,2,32,1024]{3,2,1,0:T(8,128)(2,1)} %dynamic-slice_bitcast_fusion.3), channel_id=1, source_target_pairs={{0,1},{1,0},{2,3},{3,2},{4,5},{5,4},{6,7},{7,6},{8,9},{9,8},{10,11... | collective-permute-start | bytes 1572872 | tf_op jit(solution)/shard_map/ppermute | solution.py:1022
  372.9 27.4 %collective-permute-start.35 = (bf16[2,128,1024]{2,1,0:T(8,128)(2,1)}, bf16[2,128,1024]{2,1,0:T(8,128)(2,1)}, u32[]{:S(2)}, u32[]{:S(2)}) collective-permute-start(bf16[2,128,1024]{2,1,0:T(8,128)(2,1)} %dynamic-slice_bitcast_fusion.2), channel_id=1, source_target_pairs={{0,1},{1,0},{2,3},{3,2},{4,5},{5,4},{6,7},{7,6},{8,9},{9,8},{10,11... | collective-permute-start | bytes 1572872 | tf_op jit(solution)/shard_map/ppermute | solution.py:1022
  397.0 24.6 %collective-permute-start.27 = (bf16[4,1,32,1024]{3,2,1,0:T(8,128)(2,1)S(1)}, bf16[4,1,32,1024]{3,2,1,0:T(8,128)(2,1)S(1)}, u32[]{:S(2)}, u32[]{:S(2)}) collective-permute-start(bf16[4,1,32,1024]{3,2,1,0:T(8,128)(2,1)S(1)} %constant_dynamic-slice_fusion.2), channel_id=1, source_target_pairs={{0,2},{1,3},{2,0},{3,1},{4,6},{5,7},{6,4},{7,5},{8,10},{9,11},{10,... | collective-permute-start | bytes 786440 | tf_op jit(solution)/shard_map/ppermute | solution.py:1022
  402.2 21.9 %collective-permute-start.32 = (bf16[32,1536]{1,0:T(8,128)(2,1)S(1)}, bf16[32,1536]{1,0:T(8,128)(2,1)S(1)}, u32[]{:S(2)}, u32[]{:S(2)}) collective-permute-start(bf16[32,1536]{1,0:T(8,128)(2,1)S(1)} %dynamic-slice_bitcast_fusion.5), channel_id=1, source_target_pairs={{0,4},{4,0},{1,5},{5,1},{2,6},{6,2},{3,7},{7,3},{8,12},{12,8},{9,1... | collective-permute-start | bytes 294920 | tf_op jit(solution)/shard_map/ppermute | solution.py:465
  (75 other events, 568.5 us)
Sparse Core Ops, SparseCore 0:
  11.3 93.1 all-gather.4
  145.6 75.7 all-gather.6
  233.9 84.2 reduce-scatter.6
  333.2 61.2 reduce-scatter.4

commit v4 on v3

--- a/solution.py
+++ b/solution.py
@@ -541,7 +541,7 @@
     return value * below, below + value * density * (1.0 / math.sqrt(2.0 * math.pi))
 
 
-def feed_forward(normed, grads, w_in, bias, w_out, deps=(), block=256):
+def feed_forward(normed, grads, w_in, bias, w_out, deps=(), block=512):
     tokens, width = normed.shape
     units = w_in.shape[1]
 

time: 465 us -> 464 us (level)
  no operation moved by 1% of the time
where the time goes in v4:
time: 464 us; the launch traced here: 456 us
  waiting for transfers between devices  121 us (26%)
  Pallas kernels  104 us (22%)
  starting transfers between devices  76.3 us (16%)
  local copies, waits for them, and re-layouts  58.1 us (13%)
  other arithmetic  50 us (11%)
  matrix products  31.8 us (7%)
  between operations  15.5 us (3%)
    ppermute x7, waiting for transfers between devices, over_x(): return lax.ppermute(value, 'x', SWAP)  44.2 us
    unnamed x127, local copies, waits for them, and re-layouts  35.3 us
    ppermute x7, starting transfers between devices, over_x(): return lax.ppermute(value, 'x', SWAP)  31.6 us
    pallas_call x1, Pallas kernels, attention(): pl.pallas_call(functools.partial(attention_kernel, halo, tok, heads), gri...  27.6 us
    pallas_call x6, Pallas kernels, matmul(): pl.pallas_call(body, grid=(rows // block,), in_specs=[left_spec, whole] +...  24.8 us
    ppermute x4, starting transfers between devices, z_scatter(): come = lax.ppermute(pick(blocks, 1 - bit, axis + 1), 'z', pairs)  24.6 us
    ppermute x2, waiting for transfers between devices, local_plane(): before.append(lax.ppermute(before[-1], 'z', up))  23.5 us
    convert_element_type x12, other arithmetic, summed(): return sum((v.astype(F32) for v in values)).astype(BF)  20 us
  transfers between devices with their start and end apart: 41, of which 14 were waited for; matrix products, arithmetic and copies ran while one was open for 22% of the time, Pallas kernels for 23%

profile of v4, /device:TPU:0, one launch (start us, length us, event | category | flops | bytes accessed | tf_op | source)
XLA Modules:
  0.0 456.0 jit_solution(6181951169883850692)
XLA Ops:
  22.7 4.5 collective-permute-start.12
  28.0 42.7 %collective-permute-done.4 = bf16[2,352]{1,0:T(2,128)(2,1)S(1)} collective-permute-done((bf16[2,352]{1,0:T(2,128)(2,1)S(1)}, bf16[2,352]{1,0:T(2,128)(2,1)S(1)}, u32[]{:S(2)}, u32[]{:S(2)}) %collective-permute-start.4) | collective-permute-done | bytes 1440 | tf_op jit(solution)/shard_map/ppermute | solution.py:469
  93.3 23.5 %collective-permute-done.13 = bf16[512,1024]{1,0:T(8,128)(2,1)} collective-permute-done((bf16[512,1024]{1,0:T(8,128)(2,1)}, bf16[512,1024]{1,0:T(8,128)(2,1)}, u32[]{:S(2)}, u32[]{:S(2)}) %collective-permute-start.13) | collective-permute-done | bytes 1048608 | tf_op jit(solution)/shard_map/ppermute | solution.py:1099
  124.0 6.2 %layer_norm.2 = (bf16[3072,1024]{1,0:T(8,128)(2,1)S(1)}, bf16[2048,1024]{1,0:T(8,128)(2,1)S(1)}) custom-call(bf16[2,512,1024]{2,1,0:T(8,128)(2,1)} %constant_dynamic-update-slice_fusion.refs_0_, bf16[2,512,1024]{2,1,0:T(8,128)(2,1)} %collective-permute-done.refs_1_, bf16[2,512,1024]{2,1,0:T(8,128)(2,1)S(1)} %collective-permute-done.1.refs_2_, ...), custom_call_target="tpu_custom_call" | custom-call | bytes 1048576 | tf_op jit(solution)/shard_map/layer_norm/pallas_call | solution.py:960
  130.2 8.4 %layer_norm.3.n_ref = bf16[3072,1024]{1,0:T(8,128)(2,1)S(1)} custom-call(bf16[1,512,1024]{2,1,0:T(8,128)(2,1)} %bitcast.35.refs_0_, bf16[1,512,1024]{2,1,0:T(8,128)(2,1)} %bitcast.36.refs_1_, bf16[1,512,1024]{2,1,0:T(8,128)(2,1)} %bitcast.37.refs_2_, bf16[1,512,1024]{2,1,0:T(8,128)(2,1)} %bitcast.38.refs_3_, ...), custom_call_target="tpu_custom_call", output_to_operand_aliasing={{}: (6, {})} | custom-call | bytes 1048576 | tf_op jit(solution)/shard_map/layer_norm/pallas_call | solution.py:960
  157.3 8.6 %add_convert_fusion = bf16[3072,1024]{1,0:T(8,128)(2,1)} fusion(f32[1024]{0:T(1024)S(1)} %bitcast.331, bf16[3072,1024]{1,0:T(8,128)(2,1)S(1)} %bitcast.271, bf16[1024,1024]{1,0:T(8,128)(2,1)S(1)} %get-tuple-element.30), kind=kOutput, calls=%fused_computation.1 | convolution fusion | flops 6448742400 | bytes 14684160 | tf_op jit(solution)/shard_map/dot_general | solution.py:461
  165.9 27.6 %attention.1 = (bf16[2,512,512]{2,1,0:T(8,128)(2,1)S(1)}, bf16[2,512,512]{2,1,0:T(8,128)(2,1)S(1)}, bf16[3,2,512,1024]{3,2,1,0:T(8,128)(2,1)}) custom-call(s32[5]{0:T(128)S(1)} %pad_add_fusion.1.scalar_ref, bf16[2,512,512]{2,1,0:T(8,128)(2,1)S(1)} %bitcast.287, bf16[3,2,512,1024]{3,2,1,0:T(8,128)(2,1)} %bitcast.297, bf16[3,2,512,1024]{3,2,1,0:T(8,128)(2,1)} %bitcast.298, ...), custom_call_target="tpu_custom_call" | custom-call | bytes 1048576 | tf_op jit(solution)/shard_map/attention/pallas_call | solution.py:783
  193.5 10.2 %convolution_convert_fusion = bf16[3072,1024]{1,0:T(8,128)(2,1)S(1)} fusion(bf16[3072,1024]{1,0:T(8,128)(2,1)} %bitcast.295, bf16[1024,1024]{1,0:T(8,128)(2,1)S(1)} %get-tuple-element.30), kind=kOutput, calls=%fused_computation.4 | convolution fusion | flops 6445596672 | bytes 14680064 | tf_op jit(solution)/shard_map/dot_general | solution.py:477
  207.7 14.5 %attention_weight_grads.1.refs_1_ = bf16[4,4,2,32,2048]{4,3,2,1,0:T(8,128)(2,1)} custom-call(bf16[3072,1024]{1,0:T(8,128)(2,1)} %copy-done.5, bf16[1024,512]{1,0:T(8,128)(2,1)S(1)} %bitcast.283, bf16[1024,512]{1,0:T(8,128)(2,1)S(1)} %bitcast.276, bf16[3072,1024]{1,0:T(8,128)(2,1)} %bitcast.296, bf16[2048,1024]{1,0:T(8,128)(2,1)} %pad_maximum_fusion.left_ref.g_ref.right_ref), custom_call_target="tpu_custom_call" | custom-call | bytes 1048576 | tf_op jit(solution)/shard_map/attention_weight_grads/pallas_call | solution.py:994
  240.2 16.9 %feed_forward.1 = (bf16[2048,1024]{1,0:T(8,128)(2,1)}, bf16[2048,1024]{1,0:T(8,128)(2,1)}, f32[8,1024]{1,0:T(8,128)S(1)}) custom-call(bf16[2048,1024]{1,0:T(8,128)(2,1)} %copy-done.3, bf16[2048,1024]{1,0:T(8,128)(2,1)} %pad_maximum_fusion.left_ref.g_ref.right_ref, bf16[1024,1024]{1,0:T(8,128)(2,1)S(1)} %get-tuple-element.26.wi_ref, f32[1,1024]{1,0:T(1,128)S(1)} %bitcast.291, ...), custom_call_target="tpu_custom_call" | custom-call | bytes 1048576 | tf_op jit(solution)/shard_map/feed_forward/pallas_call | solution.py:567
  257.0 9.8 %collective-permute-done.17.refs_0_ = bf16[512,1024]{1,0:T(8,128)(2,1)} collective-permute-done((bf16[512,1024]{1,0:T(8,128)(2,1)}, bf16[512,1024]{1,0:T(8,128)(2,1)}, u32[]{:S(2)}, u32[]{:S(2)}) %collective-permute-start.17) | collective-permute-done | bytes 1048608 | tf_op jit(solution)/shard_map/ppermute | solution.py:1190
  268.5 7.9 %matmul_tn.2 = bf16[1024,1024]{1,0:T(8,128)(2,1)S(1)} custom-call(bf16[2048,1024]{1,0:T(8,128)(2,1)} %copy-done.3, bf16[2048,1024]{1,0:T(8,128)(2,1)} %get-tuple-element.36.right_ref, bf16[512,1024]{1,0:T(8,128)(2,1)S(1)} %fusion.23.rest_0_), custom_call_target="tpu_custom_call" | custom-call | bytes 1048576 | tf_op jit(solution)/shard_map/matmul_tn/pallas_call | solution.py:504
  276.6 8.2 %add_convert_fusion.2 = bf16[2048,1024]{1,0:T(8,128)(2,1)S(1)} fusion(f32[1024]{0:T(1024)S(1)} %bitcast.292, bf16[2048,1024]{1,0:T(8,128)(2,1)} %get-tuple-element.36.right_ref, bf16[1024,1024]{1,0:T(8,128)(2,1)S(1)} %get-tuple-element.26.wi_ref), kind=kOutput, calls=%fused_computation.3 | convolution fusion | flops 4299161600 | bytes 10489856 | tf_op jit(solution)/shard_map/dot_general | solution.py:477
  291.3 7.7 %matmul_tn.3 = bf16[1024,1024]{1,0:T(8,128)(2,1)S(1)} custom-call(bf16[2048,1024]{1,0:T(8,128)(2,1)} %get-tuple-element.35.left_ref, bf16[2048,1024]{1,0:T(8,128)(2,1)} %pad_maximum_fusion.left_ref.g_ref.right_ref, bf16[2,512,1024]{2,1,0:T(8,128)(2,1)} %pad_maximum_fusion.1.rest_0_), custom_call_target="tpu_custom_call" | custom-call | bytes 1048576 | tf_op jit(solution)/shard_map/matmul_tn/pallas_call | solution.py:504
  308.5 4.9 %add_convert_fusion.1 = bf16[2048,1024]{1,0:T(8,128)(2,1)S(1)} fusion(f32[1024]{0:T(1024)S(1)} %bitcast.293, bf16[2048,1024]{1,0:T(8,128)(2,1)S(1)} %copy-done.40, bf16[1024,1024]{1,0:T(8,128)(2,1)S(1)} %copy-done.28), kind=kOutput, calls=%fused_computation.2 | convolution fusion | flops 4299161600 | bytes 10489856 | tf_op jit(solution)/shard_map/dot_general | solution.py:461
  323.5 8.6 %collective-permute-start.21 = (bf16[512,1024]{1,0:T(8,128)(2,1)S(1)}, bf16[512,1024]{1,0:T(8,128)(2,1)S(1)}, u32[]{:S(2)}, u32[]{:S(2)}) collective-permute-start(bf16[512,1024]{1,0:T(8,128)(2,1)S(1)} %fusion.21.refs_2_.rest_0_), channel_id=1, source_target_pairs={{0,8},{8,0},{1,9},{9,1},{2,10},{10,2},{3,11},{11,3},{4,12},{12,4},... | collective-permute-start | bytes 3145736 | tf_op jit(solution)/shard_map/ppermute | solution.py:469
  335.3 9.1 %collective-permute-done.22.refs_0_ = bf16[512,1024]{1,0:T(8,128)(2,1)S(1)} collective-permute-done((bf16[512,1024]{1,0:T(8,128)(2,1)}, bf16[512,1024]{1,0:T(8,128)(2,1)S(1)}, u32[]{:S(2)}, u32[]{:S(2)}) %collective-permute-start.22) | collective-permute-done | bytes 1048608 | tf_op jit(solution)/shard_map/ppermute | solution.py:473
  348.2 12.7 %collective-permute-start.24 = (bf16[4,2,32,1024]{3,2,1,0:T(8,128)(2,1)}, bf16[4,2,32,1024]{3,2,1,0:T(8,128)(2,1)}, u32[]{:S(2)}, u32[]{:S(2)}) collective-permute-start(bf16[4,2,32,1024]{3,2,1,0:T(8,128)(2,1)} %dynamic-slice_bitcast_fusion.3), channel_id=1, source_target_pairs={{0,1},{1,0},{2,3},{3,2},{4,5},{5,4},{6,7},{7,6},{8,9},{9,8},{10,11... | collective-permute-start | bytes 1572872 | tf_op jit(solution)/shard_map/ppermute | solution.py:1022
  360.9 4.0 collective-permute-done.23
  373.9 9.3 %collective-permute-start.35 = (bf16[2,128,1024]{2,1,0:T(8,128)(2,1)}, bf16[2,128,1024]{2,1,0:T(8,128)(2,1)}, u32[]{:S(2)}, u32[]{:S(2)}) collective-permute-start(bf16[2,128,1024]{2,1,0:T(8,128)(2,1)} %dynamic-slice_bitcast_fusion.2), channel_id=1, source_target_pairs={{0,1},{1,0},{2,3},{3,2},{4,5},{5,4},{6,7},{7,6},{8,9},{9,8},{10,11... | collective-permute-start | bytes 1572872 | tf_op jit(solution)/shard_map/ppermute | solution.py:1022
  383.2 10.4 %reduce-scatter.5.cloned.1.call-done = bf16[1,2,32,2048]{3,2,1,0:T(8,128)(2,1)} async-done(((bf16[4,2,32,2048]{3,2,1,0:T(8,128)(2,1)}), bf16[1,2,32,2048]{3,2,1,0:T(8,128)(2,1)}) %reduce-scatter.5.cloned.1.call-update) | async-done | bytes 262160 | tf_op jit(solution)/shard_map/reduce_scatter | solution.py:1182
  402.0 16.1 %collective-permute-start.26 = (f32[10240]{0:T(1024)S(1)}, f32[10240]{0:T(1024)S(1)}, u32[]{:S(2)}, u32[]{:S(2)}) collective-permute-start(f32[10240]{0:T(1024)S(1)} %add.344), channel_id=1, source_target_pairs={{0,8},{8,0},{1,9},{9,1},{2,10},{10,2},{3,11},{11,3},{4,12},{12,4},... | collective-permute-start | bytes 122888 | tf_op jit(solution)/shard_map/ppermute | solution.py:469
  427.3 6.6 %collective-permute-done.30 = f32[10240]{0:T(1024)S(1)} collective-permute-done((f32[10240]{0:T(1024)S(1)}, f32[10240]{0:T(1024)S(1)}, u32[]{:S(2)}, u32[]{:S(2)}) %collective-permute-start.30) | collective-permute-done | bytes 40992 | tf_op jit(solution)/shard_map/ppermute | solution.py:1262
  444.6 4.0 fusion.25
  (354 shorter events, 158.1 us)
Async XLA Ops:
  7.2 109.8 %all-gather.5.cloned.1.call-start = ((), (), s32[]{:S(2)}) async-start(), calls=%async_computation.3 | async-start | bytes 4456448 | tf_op jit(solution)/shard_map/all_gather | solution.py:1081
  9.1 228.4 %all-gather.7.cloned.1.call-start = ((), (), s32[]{:S(2)}) async-start(), calls=%async_computation.4 | async-start | bytes 4718592 | tf_op jit(solution)/shard_map/all_gather | solution.py:1134
  12.5 75.5 %collective-permute-start.1 = (bf16[2,512,1024]{2,1,0:T(8,128)(2,1)}, bf16[2,512,1024]{2,1,0:T(8,128)(2,1)S(1)}, u32[]{:S(2)}, u32[]{:S(2)}) collective-permute-start(bf16[2,512,1024]{2,1,0:T(8,128)(2,1)} %constant_dynamic-update-slice_fusion.refs_0_), channel_id=1, source_target_pairs={{0,8},{8,0},{1,9},{9,1},{2,10},{10,2},{3,11},{11,3},{4,12},{12,4},... | collective-permute-start | bytes 6291464 | tf_op jit(solution)/shard_map/ppermute | solution.py:469
  15.5 107.2 %collective-permute-start = (bf16[2,512,1024]{2,1,0:T(8,128)(2,1)}, bf16[2,512,1024]{2,1,0:T(8,128)(2,1)}, u32[]{:S(2)}, u32[]{:S(2)}) collective-permute-start(bf16[2,512,1024]{2,1,0:T(8,128)(2,1)} %constant_dynamic-update-slice_fusion.refs_0_), channel_id=1, source_target_pairs={{0,4},{4,0},{1,5},{5,1},{2,6},{6,2},{3,7},{7,3},{8,12},{12,8},{9,1... | collective-permute-start | bytes 6291464 | tf_op jit(solution)/shard_map/ppermute | solution.py:465
  18.0 70.2 %collective-permute-start.8 = (bf16[32,2048]{1,0:T(8,128)(2,1)S(1)}, bf16[32,2048]{1,0:T(8,128)(2,1)S(1)}, u32[]{:S(2)}, u32[]{:S(2)}) collective-permute-start(bf16[32,2048]{1,0:T(8,128)(2,1)S(1)} %bitcast.323), channel_id=1, source_target_pairs={{0,4},{4,0},{1,5},{5,1},{2,6},{6,2},{3,7},{7,3},{8,12},{12,8},{9,1... | collective-permute-start | bytes 393224 | tf_op jit(solution)/shard_map/ppermute | solution.py:465
  22.7 61.7 %collective-permute-start.12 = (bf16[512,1024]{1,0:T(8,128)(2,1)}, bf16[512,1024]{1,0:T(8,128)(2,1)}, u32[]{:S(2)}, u32[]{:S(2)}) collective-permute-start(bf16[512,1024]{1,0:T(8,128)(2,1)} %bitcast.294), channel_id=1, source_target_pairs={{0,1},{1,2},{2,3},{4,5},{5,6},{6,7},{8,9},{9,10},{10,11},{12,13},{... | collective-permute-start | bytes 3145736 | tf_op jit(solution)/shard_map/ppermute | solution.py:1099
  27.3 43.4 %collective-permute-start.4 = (bf16[2,352]{1,0:T(2,128)(2,1)S(1)}, bf16[2,352]{1,0:T(2,128)(2,1)S(1)}, u32[]{:S(2)}, u32[]{:S(2)}) collective-permute-start(bf16[2,352]{1,0:T(2,128)(2,1)S(1)} %maximum_bitcast_fusion.1), channel_id=1, source_target_pairs={{0,8},{8,0},{1,9},{9,1},{2,10},{10,2},{3,11},{11,3},{4,12},{12,4},... | collective-permute-start | bytes 4232 | tf_op jit(solution)/shard_map/ppermute | solution.py:469
  84.4 32.4 %collective-permute-start.13 = (bf16[512,1024]{1,0:T(8,128)(2,1)}, bf16[512,1024]{1,0:T(8,128)(2,1)}, u32[]{:S(2)}, u32[]{:S(2)}) collective-permute-start(bf16[512,1024]{1,0:T(8,128)(2,1)} %collective-permute-done.12), channel_id=1, source_target_pairs={{0,1},{1,2},{2,3},{4,5},{5,6},{6,7},{8,9},{9,10},{10,11},{12,13},{... | collective-permute-start | bytes 3145736 | tf_op jit(solution)/shard_map/ppermute | solution.py:1099
  88.0 36.0 %collective-permute-start.2 = (bf16[2,512,1024]{2,1,0:T(8,128)(2,1)S(1)}, bf16[2,512,1024]{2,1,0:T(8,128)(2,1)}, u32[]{:S(2)}, u32[]{:S(2)}) collective-permute-start(bf16[2,512,1024]{2,1,0:T(8,128)(2,1)S(1)} %collective-permute-done.1.refs_2_), channel_id=1, source_target_pairs={{0,4},{4,0},{1,5},{5,1},{2,6},{6,2},{3,7},{7,3},{8,12},{12,8},{9,1... | collective-permute-start | bytes 6291464 | tf_op jit(solution)/shard_map/ppermute | solution.py:465
  91.0 30.2 %collective-permute-start.9 = (bf16[64,1024]{1,0:T(8,128)(2,1)}, bf16[64,1024]{1,0:T(8,128)(2,1)S(1)}, u32[]{:S(2)}, u32[]{:S(2)}) collective-permute-start(bf16[64,1024]{1,0:T(8,128)(2,1)} %bitcast.142), channel_id=1, source_target_pairs={{0,8},{8,0},{1,9},{9,1},{2,10},{10,2},{3,11},{11,3},{4,12},{12,4},... | collective-permute-start | bytes 393224 | tf_op jit(solution)/shard_map/ppermute | solution.py:469
  93.1 37.1 %collective-permute-start.15 = (bf16[512,1024]{1,0:T(8,128)(2,1)}, bf16[512,1024]{1,0:T(8,128)(2,1)}, u32[]{:S(2)}, u32[]{:S(2)}) collective-permute-start(bf16[512,1024]{1,0:T(8,128)(2,1)} %collective-permute-done.12), channel_id=1, source_target_pairs={{0,4},{4,0},{1,5},{5,1},{2,6},{6,2},{3,7},{7,3},{8,12},{12,8},{9,1... | collective-permute-start | bytes 3145736 | tf_op jit(solution)/shard_map/ppermute | solution.py:465
  121.2 24.5 %collective-permute-start.11 = (bf16[16,32,1536]{2,1,0:T(8,128)(2,1)}, bf16[16,32,1536]{2,1,0:T(8,128)(2,1)}, u32[]{:S(2)}, u32[]{:S(2)}) collective-permute-start(bf16[16,32,1536]{2,1,0:T(8,128)(2,1)} %away_columns.1), channel_id=1, source_target_pairs={{0,4},{4,0},{1,5},{5,1},{2,6},{6,2},{3,7},{7,3},{8,12},{12,8},{9,1... | collective-permute-start | bytes 4718600 | tf_op jit(solution)/shard_map/ppermute | solution.py:465
  145.5 186.9 %reduce-scatter.7.cloned.1.call-start = ((), (), s32[]{:S(2)}) async-start(), calls=%async_computation.5 | async-start | bytes 5242880
  229.4 37.5 %collective-permute-start.17 = (bf16[512,1024]{1,0:T(8,128)(2,1)}, bf16[512,1024]{1,0:T(8,128)(2,1)}, u32[]{:S(2)}, u32[]{:S(2)}) collective-permute-start(bf16[512,1024]{1,0:T(8,128)(2,1)} %slice_bitcast_fusion.15), channel_id=1, source_target_pairs={{1,0},{2,1},{3,2},{5,4},{6,5},{7,6},{9,8},{10,9},{11,10},{13,12},{... | collective-permute-start | bytes 3145736 | tf_op jit(solution)/shard_map/ppermute | solution.py:1190
  233.6 160.1 %reduce-scatter.5.cloned.1.call-start = ((), (), s32[]{:S(2)}) async-start(), calls=%async_computation.2 | async-start | bytes 1310720 | tf_op jit(solution)/shard_map/reduce_scatter | solution.py:1182
  318.2 26.2 %collective-permute-start.22 = (bf16[512,1024]{1,0:T(8,128)(2,1)}, bf16[512,1024]{1,0:T(8,128)(2,1)S(1)}, u32[]{:S(2)}, u32[]{:S(2)}) collective-permute-start(bf16[512,1024]{1,0:T(8,128)(2,1)} %copy-done.18), channel_id=1, source_target_pairs={{0,16},{16,0},{1,17},{17,1},{2,18},{18,2},{3,19},{19,3},{4,20},{20... | collective-permute-start | bytes 3145736 | tf_op jit(solution)/shard_map/ppermute | solution.py:473
  322.2 42.7 %collective-permute-start.23 = (bf16[512,1024]{1,0:T(8,128)(2,1)}, bf16[512,1024]{1,0:T(8,128)(2,1)}, u32[]{:S(2)}, u32[]{:S(2)}) collective-permute-start(bf16[512,1024]{1,0:T(8,128)(2,1)} %copy-done.23), channel_id=1, source_target_pairs={{1,0},{2,1},{3,2},{5,4},{6,5},{7,6},{9,8},{10,9},{11,10},{13,12},{... | collective-permute-start | bytes 3145736 | tf_op jit(solution)/shard_map/ppermute | solution.py:1192
  323.5 37.4 %collective-permute-start.21 = (bf16[512,1024]{1,0:T(8,128)(2,1)S(1)}, bf16[512,1024]{1,0:T(8,128)(2,1)S(1)}, u32[]{:S(2)}, u32[]{:S(2)}) collective-permute-start(bf16[512,1024]{1,0:T(8,128)(2,1)S(1)} %fusion.21.refs_2_.rest_0_), channel_id=1, source_target_pairs={{0,8},{8,0},{1,9},{9,1},{2,10},{10,2},{3,11},{11,3},{4,12},{12,4},... | collective-permute-start | bytes 3145736 | tf_op jit(solution)/shard_map/ppermute | solution.py:469
  332.2 36.8 %collective-permute-start.34 = (bf16[512,1024]{1,0:T(8,128)(2,1)}, bf16[512,1024]{1,0:T(8,128)(2,1)}, u32[]{:S(2)}, u32[]{:S(2)}) collective-permute-start(bf16[512,1024]{1,0:T(8,128)(2,1)} %copy-done.19), channel_id=1, source_target_pairs={{0,16},{16,0},{1,17},{17,1},{2,18},{18,2},{3,19},{19,3},{4,20},{20... | collective-permute-start | bytes 3145736 | tf_op jit(solution)/shard_map/ppermute | solution.py:473
  335.3 107.4 %collective-permute-start.20 = (bf16[512,1024]{1,0:T(8,128)(2,1)}, bf16[512,1024]{1,0:T(8,128)(2,1)}, u32[]{:S(2)}, u32[]{:S(2)}) collective-permute-start(bf16[512,1024]{1,0:T(8,128)(2,1)} %fusion.18.refs_1_), channel_id=1, source_target_pairs={{0,8},{8,0},{1,9},{9,1},{2,10},{10,2},{3,11},{11,3},{4,12},{12,4},... | collective-permute-start | bytes 3145736 | tf_op jit(solution)/shard_map/ppermute | solution.py:469
  348.2 46.6 %collective-permute-start.24 = (bf16[4,2,32,1024]{3,2,1,0:T(8,128)(2,1)}, bf16[4,2,32,1024]{3,2,1,0:T(8,128)(2,1)}, u32[]{:S(2)}, u32[]{:S(2)}) collective-permute-start(bf16[4,2,32,1024]{3,2,1,0:T(8,128)(2,1)} %dynamic-slice_bitcast_fusion.3), channel_id=1, source_target_pairs={{0,1},{1,0},{2,3},{3,2},{4,5},{5,4},{6,7},{7,6},{8,9},{9,8},{10,11... | collective-permute-start | bytes 1572872 | tf_op jit(solution)/shard_map/ppermute | solution.py:1022
  373.9 26.1 %collective-permute-start.35 = (bf16[2,128,1024]{2,1,0:T(8,128)(2,1)}, bf16[2,128,1024]{2,1,0:T(8,128)(2,1)}, u32[]{:S(2)}, u32[]{:S(2)}) collective-permute-start(bf16[2,128,1024]{2,1,0:T(8,128)(2,1)} %dynamic-slice_bitcast_fusion.2), channel_id=1, source_target_pairs={{0,1},{1,0},{2,3},{3,2},{4,5},{5,4},{6,7},{7,6},{8,9},{9,8},{10,11... | collective-permute-start | bytes 1572872 | tf_op jit(solution)/shard_map/ppermute | solution.py:1022
  396.2 24.2 %collective-permute-start.27 = (bf16[4,1,32,1024]{3,2,1,0:T(8,128)(2,1)S(1)}, bf16[4,1,32,1024]{3,2,1,0:T(8,128)(2,1)S(1)}, u32[]{:S(2)}, u32[]{:S(2)}) collective-permute-start(bf16[4,1,32,1024]{3,2,1,0:T(8,128)(2,1)S(1)} %constant_dynamic-slice_fusion.2), channel_id=1, source_target_pairs={{0,2},{1,3},{2,0},{3,1},{4,6},{5,7},{6,4},{7,5},{8,10},{9,11},{10,... | collective-permute-start | bytes 786440 | tf_op jit(solution)/shard_map/ppermute | solution.py:1022
  402.0 20.9 %collective-permute-start.32 = (bf16[32,1536]{1,0:T(8,128)(2,1)S(1)}, bf16[32,1536]{1,0:T(8,128)(2,1)S(1)}, u32[]{:S(2)}, u32[]{:S(2)}) collective-permute-start(bf16[32,1536]{1,0:T(8,128)(2,1)S(1)} %dynamic-slice_bitcast_fusion.5), channel_id=1, source_target_pairs={{0,4},{4,0},{1,5},{5,1},{2,6},{6,2},{3,7},{7,3},{8,12},{12,8},{9,1... | collective-permute-start | bytes 294920 | tf_op jit(solution)/shard_map/ppermute | solution.py:465
  (75 other events, 570.1 us)
Sparse Core Ops, SparseCore 0:
  11.3 93.1 all-gather.4
  145.6 75.7 all-gather.6
  233.7 84.3 reduce-scatter.6
  332.5 61.1 reduce-scatter.4

commit v5 on v4

--- a/solution.py
+++ b/solution.py
@@ -1166,9 +1166,6 @@
     dq = dq.reshape(both, part)
     dkv = dkv.reshape(kv_rows, 2 * part)
 
-    def after(*deps):
-        return held(jnp.zeros((1, width), F32), *deps)
-
     dn_kv = nt(dkv, w_kv_f).astype(BF).reshape(halo + 1, 2, tok, width)
     dn_come = other_core(dn_kv[:halo, 1])
     g_att = attention_weight_grads(normed_kv, attended, dq, dkv, grads_all, nz)
@@ -1197,7 +1194,7 @@
     g_in = matmul(normed_all, grad_pre, "tn", deps=(passed,)).reshape(2, -1, units)
     in_away = pick(g_in, 1 - yi, 0)
     in_y = over_y(in_away)
-    dn_ff = (nt(grad_pre, w_in_f) + after(in_away)).astype(BF).reshape(2, 2, tok, width)
+    dn_ff = matmul(grad_pre, w_in_f, "nt", deps=(in_away,)).reshape(2, 2, tok, width)
     dn_away = away_tokens(dn_ff, dn_att)
     g_out = matmul(activated, grads_all, "tn", deps=(dn_away,)).reshape(2, -1, width)
     out_away = pick(g_out, 1 - yi, 0)
@@ -1205,7 +1202,7 @@
     dn_come = held(other_core(dn_away), g_out)
     dn_send = summed(dn_ff[1, 0], dn_come[1])
     dn_x = over_x(dn_send)
-    branch = (mm(activated, w_out_f) + after(out_away, dn_send)).astype(BF)
+    branch = matmul(activated, w_out_f, "nn", deps=(out_away, dn_send))
     branch = branch.reshape(2, 2, tok, width)
     branch_att = matmul(attended, w_dense_f, "nn", deps=(dn_send,)).reshape(2, tok, width)
     br_come = other_core(away_tokens(branch, branch_att))

time: 464 us -> 463 us (level)
  starting transfers between devices: 76.3 us -> 58.6 us
  Pallas kernels: 104 us -> 119 us
  matrix products: 31.8 us -> 18.4 us
  waiting for transfers between devices: 121 us -> 133 us
    ppermute x7, starting transfers between devices: 31.6 us -> 14.5 us  [over_x(): return lax.ppermute(value, 'x', SWAP)]
    pallas_call x6 -> x8, Pallas kernels: 24.8 us -> 41.5 us  [matmul(): pl.pallas_call(body, grid=(rows // block,), in_specs=[left_spec, whole] +...]
    ppermute x1, waiting for transfers between devices: 4.04 us -> 16.6 us  [local_plane(): dn_back = lax.ppermute(passed, 'z', down)]
    reduce_scatter x1, waiting for transfers between devices: 10.4 us -> 0.02 us  [local_plane(): s_att = lax.psum_scatter(s_att, 'z', scatter_dimension=0, tiled=False)]
    dot_general x2 -> x1, matrix products: 18.3 us -> 9.76 us  [nt(): lax.dot_general(left, right, (((1,), (1,)), ((), ())), preferred_element_...]
    ppermute x4, waiting for transfers between devices: 0.51 us -> 8.17 us  [z_scatter(): come = lax.ppermute(pick(blocks, 1 - bit, axis + 1), 'z', pairs)]
    unnamed x127 -> x111, local copies, waits for them, and re-layouts: 35.3 us -> 27.8 us
    dot_general x2 -> x1, matrix products: 13.5 us -> 8.66 us  [mm(): return jnp.dot(left, right, preferred_element_type=F32)]
  transfers between devices with their start and end apart: 41 -> 41, of which waited for: 14 -> 13; matrix products, arithmetic and copies ran while one was open for 22% -> 22% of each run, Pallas kernels for 23% -> 26%
where the time goes in v5:
time: 463 us; the launch traced here: 454 us
  waiting for transfers between devices  133 us (29%)
  Pallas kernels  119 us (26%)
  starting transfers between devices  58.6 us (13%)
  local copies, waits for them, and re-layouts  56.8 us (12%)
  other arithmetic  52.2 us (11%)
  matrix products  18.4 us (4%)
  between operations  15.2 us (3%)
    ppermute x7, waiting for transfers between devices, over_x(): return lax.ppermute(value, 'x', SWAP)  44.1 us
    pallas_call x8, Pallas kernels, matmul(): pl.pallas_call(body, grid=(rows // block,), in_specs=[left_spec, whole] +...  41.5 us
    pallas_call x1, Pallas kernels, attention(): pl.pallas_call(functools.partial(attention_kernel, halo, tok, heads), gri...  28 us
    unnamed x111, local copies, waits for them, and re-layouts  27.8 us
    convert_element_type x12, other arithmetic, summed(): return sum((v.astype(F32) for v in values)).astype(BF)  21.5 us
    ppermute x2, waiting for transfers between devices, local_plane(): before.append(lax.ppermute(before[-1], 'z', up))  20.8 us
    ppermute x4, starting transfers between devices, z_scatter(): come = lax.ppermute(pick(blocks, 1 - bit, axis + 1), 'z', pairs)  19.9 us
    pallas_call x1, Pallas kernels, feed_forward(): pl.pallas_call(body, grid=(tokens // block,), in_specs=[rows(width), rows...  16.8 us
  transfers between devices with their start and end apart: 41, of which 13 were waited for; matrix products, arithmetic and copies ran while one was open for 22% of the time, Pallas kernels for 26%

profile of v5, /device:TPU:0, one launch (start us, length us, event | category | flops | bytes accessed | tf_op | source)
XLA Modules:
  0.0 454.0 jit_solution(2324149951041463987)
XLA Ops:
  19.4 4.3 fusion.29
  28.1 42.6 %collective-permute-done.4 = bf16[2,352]{1,0:T(2,128)(2,1)S(1)} collective-permute-done((bf16[2,352]{1,0:T(2,128)(2,1)S(1)}, bf16[2,352]{1,0:T(2,128)(2,1)S(1)}, u32[]{:S(2)}, u32[]{:S(2)}) %collective-permute-start.4) | collective-permute-done | bytes 1440 | tf_op jit(solution)/shard_map/ppermute | solution.py:469
  83.5 4.6 %collective-permute-start.13 = (bf16[512,1024]{1,0:T(8,128)(2,1)S(1)}, bf16[512,1024]{1,0:T(8,128)(2,1)}, u32[]{:S(2)}, u32[]{:S(2)}) collective-permute-start(bf16[512,1024]{1,0:T(8,128)(2,1)S(1)} %collective-permute-done.12), channel_id=1, source_target_pairs={{0,1},{1,2},{2,3},{4,5},{5,6},{6,7},{8,9},{9,10},{10,11},{12,13},{... | collective-permute-start | bytes 3145736 | tf_op jit(solution)/shard_map/ppermute | solution.py:1099
  96.6 20.8 %collective-permute-done.13 = bf16[512,1024]{1,0:T(8,128)(2,1)} collective-permute-done((bf16[512,1024]{1,0:T(8,128)(2,1)S(1)}, bf16[512,1024]{1,0:T(8,128)(2,1)}, u32[]{:S(2)}, u32[]{:S(2)}) %collective-permute-start.13) | collective-permute-done | bytes 1048608 | tf_op jit(solution)/shard_map/ppermute | solution.py:1099
  127.0 6.2 %layer_norm.2 = (bf16[3072,1024]{1,0:T(8,128)(2,1)S(1)}, bf16[2048,1024]{1,0:T(8,128)(2,1)S(1)}) custom-call(bf16[2,512,1024]{2,1,0:T(8,128)(2,1)} %constant_dynamic-update-slice_fusion.refs_0_, bf16[2,512,1024]{2,1,0:T(8,128)(2,1)} %collective-permute-done.refs_1_, bf16[2,512,1024]{2,1,0:T(8,128)(2,1)S(1)} %collective-permute-done.1.refs_2_, ...), custom_call_target="tpu_custom_call" | custom-call | bytes 1048576 | tf_op jit(solution)/shard_map/layer_norm/pallas_call | solution.py:960
  133.3 7.4 %layer_norm.3.n_ref = bf16[3072,1024]{1,0:T(8,128)(2,1)S(1)} custom-call(bf16[1,512,1024]{2,1,0:T(8,128)(2,1)} %bitcast.35.refs_0_, bf16[1,512,1024]{2,1,0:T(8,128)(2,1)} %bitcast.36.refs_1_, bf16[1,512,1024]{2,1,0:T(8,128)(2,1)S(1)} %bitcast.283, bf16[1,512,1024]{2,1,0:T(8,128)(2,1)} %bitcast.38.refs_3_, ...), custom_call_target="tpu_custom_call", output_to_operand_aliasing={{}: (6, {})} | custom-call | bytes 1048576 | tf_op jit(solution)/shard_map/layer_norm/pallas_call | solution.py:960
  157.5 8.7 %add_convert_fusion = bf16[3072,1024]{1,0:T(8,128)(2,1)} fusion(f32[1024]{0:T(1024)S(1)} %bitcast.321, bf16[3072,1024]{1,0:T(8,128)(2,1)S(1)} %layer_norm.3.n_ref, bf16[1024,1024]{1,0:T(8,128)(2,1)S(1)} %get-tuple-element.30), kind=kOutput, calls=%fused_computation.1 | convolution fusion | flops 6448742400 | bytes 14684160 | tf_op jit(solution)/shard_map/dot_general | solution.py:461
  166.2 28.0 %attention.1 = (bf16[2,512,512]{2,1,0:T(8,128)(2,1)S(1)}, bf16[2,512,512]{2,1,0:T(8,128)(2,1)S(1)}, bf16[3,2,512,1024]{3,2,1,0:T(8,128)(2,1)}) custom-call(s32[5]{0:T(128)S(1)} %pad_add_fusion.1.scalar_ref, bf16[2,512,512]{2,1,0:T(8,128)(2,1)S(1)} %bitcast.279, bf16[3,2,512,1024]{3,2,1,0:T(8,128)(2,1)} %bitcast.288, bf16[3,2,512,1024]{3,2,1,0:T(8,128)(2,1)} %bitcast.289, ...), custom_call_target="tpu_custom_call" | custom-call | bytes 1048576 | tf_op jit(solution)/shard_map/attention/pallas_call | solution.py:783
  194.1 9.8 %convolution_convert_fusion = bf16[3072,1024]{1,0:T(8,128)(2,1)S(1)} fusion(bf16[3072,1024]{1,0:T(8,128)(2,1)} %bitcast.286, bf16[1024,1024]{1,0:T(8,128)(2,1)S(1)} %get-tuple-element.30), kind=kOutput, calls=%fused_computation.2 | convolution fusion | flops 6445596672 | bytes 14680064 | tf_op jit(solution)/shard_map/dot_general | solution.py:477
  208.0 14.5 %attention_weight_grads.1.refs_1_ = bf16[4,4,2,32,2048]{4,3,2,1,0:T(8,128)(2,1)} custom-call(bf16[3072,1024]{1,0:T(8,128)(2,1)} %copy-done.4, bf16[1024,512]{1,0:T(8,128)(2,1)S(1)} %bitcast.275, bf16[1024,512]{1,0:T(8,128)(2,1)S(1)} %bitcast.268, bf16[3072,1024]{1,0:T(8,128)(2,1)} %bitcast.287, bf16[2048,1024]{1,0:T(8,128)(2,1)} %pad_maximum_fusion.left_ref.g_ref.right_ref), custom_call_target="tpu_custom_call" | custom-call | bytes 1048576 | tf_op jit(solution)/shard_map/attention_weight_grads/pallas_call | solution.py:994
  241.4 16.8 %feed_forward.1 = (bf16[2048,1024]{1,0:T(8,128)(2,1)}, bf16[2048,1024]{1,0:T(8,128)(2,1)}, f32[8,1024]{1,0:T(8,128)S(1)}) custom-call(bf16[2048,1024]{1,0:T(8,128)(2,1)} %copy-done.2, bf16[2048,1024]{1,0:T(8,128)(2,1)} %pad_maximum_fusion.left_ref.g_ref.right_ref, bf16[1024,1024]{1,0:T(8,128)(2,1)S(1)} %get-tuple-element.26.wi_ref.right_ref, ...), custom_call_target="tpu_custom_call" | custom-call | bytes 1048576 | tf_op jit(solution)/shard_map/feed_forward/pallas_call | solution.py:567
  258.2 14.3 %collective-permute-done.17.refs_0_ = bf16[512,1024]{1,0:T(8,128)(2,1)S(1)} collective-permute-done((bf16[512,1024]{1,0:T(8,128)(2,1)}, bf16[512,1024]{1,0:T(8,128)(2,1)S(1)}, u32[]{:S(2)}, u32[]{:S(2)}) %collective-permute-start.17) | collective-permute-done | bytes 1048608 | tf_op jit(solution)/shard_map/ppermute | solution.py:1187
  272.9 8.0 %matmul_tn.2 = bf16[1024,1024]{1,0:T(8,128)(2,1)S(1)} custom-call(bf16[2048,1024]{1,0:T(8,128)(2,1)} %copy-done.2, bf16[2048,1024]{1,0:T(8,128)(2,1)} %get-tuple-element.36.right_ref.left_ref, bf16[512,1024]{1,0:T(8,128)(2,1)S(1)} %fusion.23.rest_0_), custom_call_target="tpu_custom_call" | custom-call | bytes 1048576 | tf_op jit(solution)/shard_map/matmul_tn/pallas_call | solution.py:504
  282.3 8.2 %matmul_nt.5 = bf16[2048,1024]{1,0:T(8,128)(2,1)} custom-call(bf16[2048,1024]{1,0:T(8,128)(2,1)} %get-tuple-element.36.right_ref.left_ref, bf16[1024,1024]{1,0:T(8,128)(2,1)S(1)} %get-tuple-element.26.wi_ref.right_ref, bf16[512,1024]{1,0:T(8,128)(2,1)S(1)} %dynamic-slice_bitcast_fusion.1.rest_0_), custom_call_target="tpu_custom_call" | custom-call | bytes 1048576 | tf_op jit(solution)/shard_map/matmul_nt/pallas_call | solution.py:504
  295.9 7.7 %matmul_tn.3 = bf16[1024,1024]{1,0:T(8,128)(2,1)S(1)} custom-call(bf16[2048,1024]{1,0:T(8,128)(2,1)} %get-tuple-element.35.left_ref, bf16[2048,1024]{1,0:T(8,128)(2,1)} %pad_maximum_fusion.left_ref.g_ref.right_ref, bf16[2,512,1024]{2,1,0:T(8,128)(2,1)} %pad_maximum_fusion.1.rest_0_), custom_call_target="tpu_custom_call" | custom-call | bytes 1048576 | tf_op jit(solution)/shard_map/matmul_tn/pallas_call | solution.py:504
  309.0 8.4 %matmul_nn.4 = bf16[2048,1024]{1,0:T(8,128)(2,1)} custom-call(bf16[2048,1024]{1,0:T(8,128)(2,1)} %get-tuple-element.35.left_ref, bf16[1024,1024]{1,0:T(8,128)(2,1)S(1)} %copy-done.13, bf16[512,1024]{1,0:T(8,128)(2,1)} %dynamic-slice_bitcast_fusion.rest_0_, bf16[512,1024]{1,0:T(8,128)(2,1)S(1)} %fusion.21.rest_1_.rest_0_), custom_call_target="tpu_custom_call" | custom-call | bytes 1048576 | tf_op jit(solution)/shard_map/matmul_nn/pallas_call | solution.py:504
  336.4 12.8 %collective-permute-done.22.refs_0_ = bf16[512,1024]{1,0:T(8,128)(2,1)S(1)} collective-permute-done((bf16[512,1024]{1,0:T(8,128)(2,1)}, bf16[512,1024]{1,0:T(8,128)(2,1)S(1)}, u32[]{:S(2)}, u32[]{:S(2)}) %collective-permute-start.22) | collective-permute-done | bytes 1048608 | tf_op jit(solution)/shard_map/ppermute | solution.py:473
  352.7 9.9 %collective-permute-start.24 = (bf16[4,2,32,1024]{3,2,1,0:T(8,128)(2,1)}, bf16[4,2,32,1024]{3,2,1,0:T(8,128)(2,1)}, u32[]{:S(2)}, u32[]{:S(2)}) collective-permute-start(bf16[4,2,32,1024]{3,2,1,0:T(8,128)(2,1)} %dynamic-slice_bitcast_fusion.3), channel_id=1, source_target_pairs={{0,1},{1,0},{2,3},{3,2},{4,5},{5,4},{6,7},{7,6},{8,9},{9,8},{10,11... | collective-permute-start | bytes 1572872 | tf_op jit(solution)/shard_map/ppermute | solution.py:1022
  362.6 16.6 %collective-permute-done.23 = bf16[512,1024]{1,0:T(8,128)(2,1)} collective-permute-done((bf16[512,1024]{1,0:T(8,128)(2,1)}, bf16[512,1024]{1,0:T(8,128)(2,1)}, u32[]{:S(2)}, u32[]{:S(2)}) %collective-permute-start.23) | collective-permute-done | bytes 1048608 | tf_op jit(solution)/shard_map/ppermute | solution.py:1189
  388.3 4.5 collective-permute-start.35
  395.2 5.5 %collective-permute-start.27 = (bf16[4,1,32,1024]{3,2,1,0:T(8,128)(2,1)S(1)}, bf16[4,1,32,1024]{3,2,1,0:T(8,128)(2,1)S(1)}, u32[]{:S(2)}, u32[]{:S(2)}) collective-permute-start(bf16[4,1,32,1024]{3,2,1,0:T(8,128)(2,1)S(1)} %constant_dynamic-slice_fusion.2), channel_id=1, source_target_pairs={{0,2},{1,3},{2,0},{3,1},{4,6},{5,7},{6,4},{7,5},{8,10},{9,11},{10,... | collective-permute-start | bytes 786440 | tf_op jit(solution)/shard_map/ppermute | solution.py:1022
  401.6 8.2 %collective-permute-done.35 = bf16[2,128,1024]{2,1,0:T(8,128)(2,1)} collective-permute-done((bf16[2,128,1024]{2,1,0:T(8,128)(2,1)}, bf16[2,128,1024]{2,1,0:T(8,128)(2,1)}, u32[]{:S(2)}, u32[]{:S(2)}) %collective-permute-start.35) | collective-permute-done | bytes 524320 | tf_op jit(solution)/shard_map/ppermute | solution.py:1022
  411.7 4.6 %collective-permute-start.26 = (f32[10240]{0:T(1024)S(1)}, f32[10240]{0:T(1024)S(1)}, u32[]{:S(2)}, u32[]{:S(2)}) collective-permute-start(f32[10240]{0:T(1024)S(1)} %add.318), channel_id=1, source_target_pairs={{0,8},{8,0},{1,9},{9,1},{2,10},{10,2},{3,11},{11,3},{4,12},{12,4},... | collective-permute-start | bytes 122888 | tf_op jit(solution)/shard_map/ppermute | solution.py:469
  425.5 6.6 %collective-permute-done.30 = f32[10240]{0:T(1024)S(1)} collective-permute-done((f32[10240]{0:T(1024)S(1)}, f32[10240]{0:T(1024)S(1)}, u32[]{:S(2)}, u32[]{:S(2)}) %collective-permute-start.30) | collective-permute-done | bytes 40992 | tf_op jit(solution)/shard_map/ppermute | solution.py:1259
  (333 shorter events, 159.9 us)
Async XLA Ops:
  7.2 111.3 %all-gather.5.cloned.1.call-start = ((), (), s32[]{:S(2)}) async-start(), calls=%async_computation.3 | async-start | bytes 4456448 | tf_op jit(solution)/shard_map/all_gather | solution.py:1081
  9.1 229.7 %all-gather.7.cloned.1.call-start = ((), (), s32[]{:S(2)}) async-start(), calls=%async_computation.4 | async-start | bytes 4718592 | tf_op jit(solution)/shard_map/all_gather | solution.py:1134
  12.5 75.6 %collective-permute-start.1 = (bf16[2,512,1024]{2,1,0:T(8,128)(2,1)}, bf16[2,512,1024]{2,1,0:T(8,128)(2,1)S(1)}, u32[]{:S(2)}, u32[]{:S(2)}) collective-permute-start(bf16[2,512,1024]{2,1,0:T(8,128)(2,1)} %constant_dynamic-update-slice_fusion.refs_0_), channel_id=1, source_target_pairs={{0,8},{8,0},{1,9},{9,1},{2,10},{10,2},{3,11},{11,3},{4,12},{12,4},... | collective-permute-start | bytes 6291464 | tf_op jit(solution)/shard_map/ppermute | solution.py:469
  15.5 110.2 %collective-permute-start = (bf16[2,512,1024]{2,1,0:T(8,128)(2,1)}, bf16[2,512,1024]{2,1,0:T(8,128)(2,1)}, u32[]{:S(2)}, u32[]{:S(2)}) collective-permute-start(bf16[2,512,1024]{2,1,0:T(8,128)(2,1)} %constant_dynamic-update-slice_fusion.refs_0_), channel_id=1, source_target_pairs={{0,4},{4,0},{1,5},{5,1},{2,6},{6,2},{3,7},{7,3},{8,12},{12,8},{9,1... | collective-permute-start | bytes 6291464 | tf_op jit(solution)/shard_map/ppermute | solution.py:465
  18.7 69.7 %collective-permute-start.8 = (bf16[32,2048]{1,0:T(8,128)(2,1)}, bf16[32,2048]{1,0:T(8,128)(2,1)}, u32[]{:S(2)}, u32[]{:S(2)}) collective-permute-start(bf16[32,2048]{1,0:T(8,128)(2,1)} %bitcast.136), channel_id=1, source_target_pairs={{0,4},{4,0},{1,5},{5,1},{2,6},{6,2},{3,7},{7,3},{8,12},{12,8},{9,1... | collective-permute-start | bytes 393224 | tf_op jit(solution)/shard_map/ppermute | solution.py:465
  23.7 59.8 %collective-permute-start.12 = (bf16[512,1024]{1,0:T(8,128)(2,1)}, bf16[512,1024]{1,0:T(8,128)(2,1)S(1)}, u32[]{:S(2)}, u32[]{:S(2)}) collective-permute-start(bf16[512,1024]{1,0:T(8,128)(2,1)} %bitcast.285), channel_id=1, source_target_pairs={{0,1},{1,2},{2,3},{4,5},{5,6},{6,7},{8,9},{9,10},{10,11},{12,13},{... | collective-permute-start | bytes 3145736 | tf_op jit(solution)/shard_map/ppermute | solution.py:1099
  27.4 43.3 %collective-permute-start.4 = (bf16[2,352]{1,0:T(2,128)(2,1)S(1)}, bf16[2,352]{1,0:T(2,128)(2,1)S(1)}, u32[]{:S(2)}, u32[]{:S(2)}) collective-permute-start(bf16[2,352]{1,0:T(2,128)(2,1)S(1)} %maximum_bitcast_fusion.1), channel_id=1, source_target_pairs={{0,8},{8,0},{1,9},{9,1},{2,10},{10,2},{3,11},{11,3},{4,12},{12,4},... | collective-permute-start | bytes 4232 | tf_op jit(solution)/shard_map/ppermute | solution.py:469
  83.5 33.9 %collective-permute-start.13 = (bf16[512,1024]{1,0:T(8,128)(2,1)S(1)}, bf16[512,1024]{1,0:T(8,128)(2,1)}, u32[]{:S(2)}, u32[]{:S(2)}) collective-permute-start(bf16[512,1024]{1,0:T(8,128)(2,1)S(1)} %collective-permute-done.12), channel_id=1, source_target_pairs={{0,1},{1,2},{2,3},{4,5},{5,6},{6,7},{8,9},{9,10},{10,11},{12,13},{... | collective-permute-start | bytes 3145736 | tf_op jit(solution)/shard_map/ppermute | solution.py:1099
  88.1 38.9 %collective-permute-start.2 = (bf16[2,512,1024]{2,1,0:T(8,128)(2,1)S(1)}, bf16[2,512,1024]{2,1,0:T(8,128)(2,1)}, u32[]{:S(2)}, u32[]{:S(2)}) collective-permute-start(bf16[2,512,1024]{2,1,0:T(8,128)(2,1)S(1)} %collective-permute-done.1.refs_2_), channel_id=1, source_target_pairs={{0,4},{4,0},{1,5},{5,1},{2,6},{6,2},{3,7},{7,3},{8,12},{12,8},{9,1... | collective-permute-start | bytes 6291464 | tf_op jit(solution)/shard_map/ppermute | solution.py:465
  94.2 28.5 %collective-permute-start.9 = (bf16[64,1024]{1,0:T(8,128)(2,1)}, bf16[64,1024]{1,0:T(8,128)(2,1)S(1)}, u32[]{:S(2)}, u32[]{:S(2)}) collective-permute-start(bf16[64,1024]{1,0:T(8,128)(2,1)} %bitcast.140), channel_id=1, source_target_pairs={{0,8},{8,0},{1,9},{9,1},{2,10},{10,2},{3,11},{11,3},{4,12},{12,4},... | collective-permute-start | bytes 393224 | tf_op jit(solution)/shard_map/ppermute | solution.py:469
  96.3 36.9 %collective-permute-start.15 = (bf16[512,1024]{1,0:T(8,128)(2,1)S(1)}, bf16[512,1024]{1,0:T(8,128)(2,1)}, u32[]{:S(2)}, u32[]{:S(2)}) collective-permute-start(bf16[512,1024]{1,0:T(8,128)(2,1)S(1)} %collective-permute-done.12), channel_id=1, source_target_pairs={{0,4},{4,0},{1,5},{5,1},{2,6},{6,2},{3,7},{7,3},{8,12},{12,8},{9,1... | collective-permute-start | bytes 3145736 | tf_op jit(solution)/shard_map/ppermute | solution.py:465
  122.7 24.5 %collective-permute-start.11 = (bf16[16,32,1536]{2,1,0:T(8,128)(2,1)}, bf16[16,32,1536]{2,1,0:T(8,128)(2,1)}, u32[]{:S(2)}, u32[]{:S(2)}) collective-permute-start(bf16[16,32,1536]{2,1,0:T(8,128)(2,1)} %away_columns.1), channel_id=1, source_target_pairs={{0,4},{4,0},{1,5},{5,1},{2,6},{6,2},{3,7},{7,3},{8,12},{12,8},{9,1... | collective-permute-start | bytes 4718600 | tf_op jit(solution)/shard_map/ppermute | solution.py:465
  125.2 208.2 %reduce-scatter.7.cloned.1.call-start = ((), (), s32[]{:S(2)}) async-start(), calls=%async_computation.5 | async-start | bytes 5242880
  222.6 170.2 %reduce-scatter.5.cloned.1.call-start = ((), (), s32[]{:S(2)}) async-start(), calls=%async_computation.2 | async-start | bytes 1310720 | tf_op jit(solution)/shard_map/reduce_scatter | solution.py:1179
  230.8 41.7 %collective-permute-start.17 = (bf16[512,1024]{1,0:T(8,128)(2,1)}, bf16[512,1024]{1,0:T(8,128)(2,1)S(1)}, u32[]{:S(2)}, u32[]{:S(2)}) collective-permute-start(bf16[512,1024]{1,0:T(8,128)(2,1)} %slice_bitcast_fusion.15), channel_id=1, source_target_pairs={{1,0},{2,1},{3,2},{5,4},{6,5},{7,6},{9,8},{10,9},{11,10},{13,12},{... | collective-permute-start | bytes 3145736 | tf_op jit(solution)/shard_map/ppermute | solution.py:1187
  323.0 26.2 %collective-permute-start.22 = (bf16[512,1024]{1,0:T(8,128)(2,1)}, bf16[512,1024]{1,0:T(8,128)(2,1)S(1)}, u32[]{:S(2)}, u32[]{:S(2)}) collective-permute-start(bf16[512,1024]{1,0:T(8,128)(2,1)} %copy-done.21), channel_id=1, source_target_pairs={{0,16},{16,0},{1,17},{17,1},{2,18},{18,2},{3,19},{19,3},{4,20},{20... | collective-permute-start | bytes 3145736 | tf_op jit(solution)/shard_map/ppermute | solution.py:473
  328.8 50.4 %collective-permute-start.23 = (bf16[512,1024]{1,0:T(8,128)(2,1)}, bf16[512,1024]{1,0:T(8,128)(2,1)}, u32[]{:S(2)}, u32[]{:S(2)}) collective-permute-start(bf16[512,1024]{1,0:T(8,128)(2,1)} %copy-done.18), channel_id=1, source_target_pairs={{1,0},{2,1},{3,2},{5,4},{6,5},{7,6},{9,8},{10,9},{11,10},{13,12},{... | collective-permute-start | bytes 3145736 | tf_op jit(solution)/shard_map/ppermute | solution.py:1189
  330.1 32.6 %collective-permute-start.21 = (bf16[512,1024]{1,0:T(8,128)(2,1)S(1)}, bf16[512,1024]{1,0:T(8,128)(2,1)S(1)}, u32[]{:S(2)}, u32[]{:S(2)}) collective-permute-start(bf16[512,1024]{1,0:T(8,128)(2,1)S(1)} %fusion.21.rest_1_.rest_0_), channel_id=1, source_target_pairs={{0,8},{8,0},{1,9},{9,1},{2,10},{10,2},{3,11},{11,3},{4,12},{12,4},... | collective-permute-start | bytes 3145736 | tf_op jit(solution)/shard_map/ppermute | solution.py:469
  333.3 50.1 %collective-permute-start.34 = (bf16[512,1024]{1,0:T(8,128)(2,1)}, bf16[512,1024]{1,0:T(8,128)(2,1)}, u32[]{:S(2)}, u32[]{:S(2)}) collective-permute-start(bf16[512,1024]{1,0:T(8,128)(2,1)} %dynamic-slice_bitcast_fusion.rest_0_), channel_id=1, source_target_pairs={{0,16},{16,0},{1,17},{17,1},{2,18},{18,2},{3,19},{19,3},{4,20},{20... | collective-permute-start | bytes 3145736 | tf_op jit(solution)/shard_map/ppermute | solution.py:473
  336.4 104.5 %collective-permute-start.20 = (bf16[512,1024]{1,0:T(8,128)(2,1)}, bf16[512,1024]{1,0:T(8,128)(2,1)}, u32[]{:S(2)}, u32[]{:S(2)}) collective-permute-start(bf16[512,1024]{1,0:T(8,128)(2,1)} %fusion.18.refs_1_), channel_id=1, source_target_pairs={{0,8},{8,0},{1,9},{9,1},{2,10},{10,2},{3,11},{11,3},{4,12},{12,4},... | collective-permute-start | bytes 3145736 | tf_op jit(solution)/shard_map/ppermute | solution.py:469
  352.7 41.1 %collective-permute-start.24 = (bf16[4,2,32,1024]{3,2,1,0:T(8,128)(2,1)}, bf16[4,2,32,1024]{3,2,1,0:T(8,128)(2,1)}, u32[]{:S(2)}, u32[]{:S(2)}) collective-permute-start(bf16[4,2,32,1024]{3,2,1,0:T(8,128)(2,1)} %dynamic-slice_bitcast_fusion.3), channel_id=1, source_target_pairs={{0,1},{1,0},{2,3},{3,2},{4,5},{5,4},{6,7},{7,6},{8,9},{9,8},{10,11... | collective-permute-start | bytes 1572872 | tf_op jit(solution)/shard_map/ppermute | solution.py:1022
  388.3 21.5 %collective-permute-start.35 = (bf16[2,128,1024]{2,1,0:T(8,128)(2,1)}, bf16[2,128,1024]{2,1,0:T(8,128)(2,1)}, u32[]{:S(2)}, u32[]{:S(2)}) collective-permute-start(bf16[2,128,1024]{2,1,0:T(8,128)(2,1)} %dynamic-slice_bitcast_fusion.2), channel_id=1, source_target_pairs={{0,1},{1,0},{2,3},{3,2},{4,5},{5,4},{6,7},{7,6},{8,9},{9,8},{10,11... | collective-permute-start | bytes 1572872 | tf_op jit(solution)/shard_map/ppermute | solution.py:1022
  395.1 16.6 %collective-permute-start.25 = (f32[10240]{0:T(1024)S(1)}, f32[10240]{0:T(1024)S(1)}, u32[]{:S(2)}, u32[]{:S(2)}) collective-permute-start(f32[10240]{0:T(1024)S(1)} %held.18), channel_id=1, source_target_pairs={{0,4},{4,0},{1,5},{5,1},{2,6},{6,2},{3,7},{7,3},{8,12},{12,8},{9,1... | collective-permute-start | bytes 122888 | tf_op jit(solution)/shard_map/ppermute | solution.py:465
  395.2 23.3 %collective-permute-start.27 = (bf16[4,1,32,1024]{3,2,1,0:T(8,128)(2,1)S(1)}, bf16[4,1,32,1024]{3,2,1,0:T(8,128)(2,1)S(1)}, u32[]{:S(2)}, u32[]{:S(2)}) collective-permute-start(bf16[4,1,32,1024]{3,2,1,0:T(8,128)(2,1)S(1)} %constant_dynamic-slice_fusion.2), channel_id=1, source_target_pairs={{0,2},{1,3},{2,0},{3,1},{4,6},{5,7},{6,4},{7,5},{8,10},{9,11},{10,... | collective-permute-start | bytes 786440 | tf_op jit(solution)/shard_map/ppermute | solution.py:1022
  (67 other events, 541.2 us)
Sparse Core Ops, SparseCore 0:
  11.3 93.7 all-gather.4
  125.3 75.5 all-gather.6
  222.7 77.8 reduce-scatter.6
  333.6 57.6 reduce-scatter.4
